TPU v7x, 128 devices: a whole 4x4x4 slice. The times are simulated.
128 devices in a mesh: wide: 16 (over x_hi, y, core), narrow: 8 (over z, x_lo).
Axes of the slice: x: 4 (x_hi: 2, x_lo: 2; x = x_hi * 2 + x_lo), y: 4, z: 4, core: 2. Of those that a mesh axis runs over, the one named last changes fastest.
Arguments:
- tokens: bfloat16 [8192, 5120], P('wide', 'narrow'), may hold values from -400 to 400
- ln_gain: float32 [5120], replicated, may hold values from 0.1 to 1.9
- w_qkv: bfloat16 [5120, 10240], P('narrow', 'wide'), may hold values from -0.078125 to 0.078125
- q_gain: float32 [128], replicated, may hold values from 0.1 to 1.9
- k_gain: float32 [128], replicated, may hold values from 1 to 2
- stored_keys: bfloat16 [512, 256, 1024], P(('wide', 'narrow')), may hold values from -700 to 700
- stored_values: bfloat16 [512, 256, 1024], P(('wide', 'narrow')), may hold values from -6 to 6
- span_lengths: int32 [512], P(('wide', 'narrow')), may hold values from 1 to 16, 6144 in all
- fill_positions: int32 [512], P(('wide', 'narrow')), may hold values from 1 to 256, as said below
- w_out: bfloat16 [8192, 5120], P('wide', 'narrow'), may hold values from -0.25 to 0.25
Outputs:
- block_out: bfloat16 [8192, 5120], P('wide', 'narrow')
Inputs may be any that keep to these rules, and one draw needn't show every extreme that they name: Slots 0 to span_lengths[s] - 1 of stream s are live, the rest of its 16 slots are padding. Frames 0 to fill_positions[s] - 1 of stream s hold its past.
All inputs are finite; a program needn't handle non-finite values. No bound on the sum of `span_lengths` on one device may be relied on, other than what follows from the above.
Results may differ from a plain program's by a relative error of at most 0.006.
The roundings to bfloat16 on the way count: a program that leaves them out, or rounds other values in their place, can miss the bound.
Values may be sent and summed in bfloat16 or wider, within the bound.
No kernel may reach another device: no remote copies, remote signals or barrier semaphores. Data moves between devices by JAX's collectives and lax.ppermute only.
A program may use at most 128 MiB of HBM per device.

v0:
```python
import functools
import math

import jax
import jax.numpy as jnp
from jax import lax
from jax.experimental import pallas as pl
from jax.experimental.pallas import tpu as pltpu
from jax.sharding import PartitionSpec as P

D = 5120
QUERY_HEADS = 64
KEY_VALUE_HEADS = 8
HEAD_SIZE = 128


EPSILON = 1e-06
ROPE_BASE = 1000000.0


def turn_tables(fill_positions, slots):
    half = HEAD_SIZE // 2
    slot_index = jnp.arange(slots, dtype=jnp.int32)
    position = (fill_positions[:, None] + slot_index[None, :]).reshape(-1).astype(jnp.float32)
    frequency = jnp.exp(
        jnp.arange(half, dtype=jnp.float32) * (-2.0 * math.log(ROPE_BASE) / HEAD_SIZE)
    )
    angles = position[:, None] * frequency[None, :]
    cosine, sine = jnp.cos(angles), jnp.sin(angles)
    return (
        jnp.concatenate([cosine, cosine], axis=1),
        jnp.concatenate([-sine, sine], axis=1),
    )


def attend_kernel(
    fills,
    spans,
    packed,
    inverse,
    cosine,
    sine,
    q_gain,
    k_gain,
    keys,
    values,
    attended,
):
    stream = pl.program_id(0)
    fill, span = fills[stream], spans[stream]
    slots = packed.shape[1]
    frames = keys.shape[1]
    group = QUERY_HEADS // KEY_VALUE_HEADS
    rows = group * slots
    cos_one, sin_one = cosine[...], sine[...]

    def turned(vectors, gains, cos_rows, sin_rows):
        mean_square = jnp.mean(vectors * vectors, axis=-1, keepdims=True)
        normed = vectors * lax.rsqrt(mean_square + EPSILON) * gains
        swapped = pltpu.roll(normed, HEAD_SIZE // 2, 1)
        return (normed * cos_rows + swapped * sin_rows).astype(jnp.bfloat16)

    cos_all = jnp.concatenate([cos_one] * group, axis=0)
    sin_all = jnp.concatenate([sin_one] * group, axis=0)
    low = lax.broadcasted_iota(jnp.int32, (slots, HEAD_SIZE), 1) < HEAD_SIZE // 2
    frame_live = lax.broadcasted_iota(jnp.int32, (rows, frames), 1) < fill
    slot_row = lax.broadcasted_iota(jnp.int32, (group, slots, HEAD_SIZE), 1)
    slot_row = slot_row.reshape(rows, HEAD_SIZE)
    slot_column = lax.broadcasted_iota(jnp.int32, (rows, HEAD_SIZE), 1)
    slot_live = (slot_column <= slot_row) & (slot_column < span)
    row_live = slot_row < span
    empty = jnp.zeros((HEAD_SIZE - slots, HEAD_SIZE), jnp.bfloat16)
    query_columns = group // 2 * HEAD_SIZE
    contract_last = (((1,), (1,)), ((), ()))
    score_scale = 1.0 / math.sqrt(HEAD_SIZE)
    for head in range(KEY_VALUE_HEADS):
        queries = jnp.concatenate(
            [
                packed[2 * head + g // 4, :, g % 4 * HEAD_SIZE : (g % 4 + 1) * HEAD_SIZE]
                for g in range(group)
            ],
            axis=0,
        ).astype(jnp.float32)
        queries = turned(queries, q_gain[...], cos_all, sin_all)
        first = packed[2 * head, :, query_columns:].astype(jnp.float32)
        second = packed[2 * head + 1, :, query_columns:].astype(jnp.float32)
        fresh_key = jnp.where(low, first, pltpu.roll(second, HEAD_SIZE // 2, 1))
        fresh_value = jnp.where(low, pltpu.roll(first, HEAD_SIZE // 2, 1), second)
        fresh_key = jnp.concatenate([turned(fresh_key, k_gain[...], cos_one, sin_one), empty])
        fresh_value = jnp.concatenate([(fresh_value * inverse[...]).astype(jnp.bfloat16), empty])
        columns = slice(head * HEAD_SIZE, (head + 1) * HEAD_SIZE)
        old = lax.dot_general(
            queries, keys[0, :, columns], contract_last, preferred_element_type=jnp.float32
        )
        new = lax.dot_general(
            queries, fresh_key, contract_last, preferred_element_type=jnp.float32
        )
        old = jnp.where(frame_live, old * score_scale, -1e30)
        new = jnp.where(slot_live, new * score_scale, -1e30)
        scores = jnp.concatenate([old, new], axis=1)
        weights = jnp.exp(scores - jnp.max(scores, axis=-1, keepdims=True))
        total = jnp.sum(weights, axis=-1, keepdims=True)
        weights = weights.astype(jnp.bfloat16)
        mixed = jnp.dot(
            weights[:, :frames], values[0, :, columns], preferred_element_type=jnp.float32
        ) + jnp.dot(weights[:, frames:], fresh_value, preferred_element_type=jnp.float32)
        mixed = jnp.where(row_live, mixed / total, 0.0).astype(jnp.bfloat16)
        for g in range(group):
            start = (head * group + g) * HEAD_SIZE
            attended[:, start : start + HEAD_SIZE] = mixed[g * slots : (g + 1) * slots]


def attend(packed, inverse, cosine, sine, q_gain, k_gain, keys, values, spans, fills):
    groups, rows, columns = packed.shape
    streams, frames, width = keys.shape
    slots = rows // streams
    heads = QUERY_HEADS * HEAD_SIZE
    tables = pl.BlockSpec((slots, HEAD_SIZE), lambda s, *_: (s, 0))
    gains = pl.BlockSpec((1, HEAD_SIZE), lambda s, *_: (0, 0))
    cache = pl.BlockSpec((1, frames, width), lambda s, *_: (s, 0, 0))
    return pl.pallas_call(
        attend_kernel,
        grid_spec=pltpu.PrefetchScalarGridSpec(
            num_scalar_prefetch=2,
            grid=(streams,),
            in_specs=[
                pl.BlockSpec((groups, slots, columns), lambda s, *_: (0, s, 0)),
                tables,
                tables,
                tables,
                gains,
                gains,
                cache,
                cache,
            ],
            out_specs=pl.BlockSpec((slots, heads), lambda s, *_: (s, 0)),
        ),
        out_shape=jax.ShapeDtypeStruct((rows, heads), jnp.bfloat16),
        compiler_params=pltpu.CompilerParams(vmem_limit_bytes=24 << 20),
        cost_estimate=pl.CostEstimate(
            flops=4 * rows * heads * (frames + slots),
            bytes_accessed=4 * streams * frames * width + 4 * rows * 9216,
            transcendentals=rows * QUERY_HEADS * (frames + slots),
        ),
        name="attend",
    )(
        fills,
        spans,
        packed,
        inverse,
        cosine,
        sine,
        q_gain[None],
        k_gain[None],
        keys,
        values,
    )


class Ring:
    def __init__(self, axis):
        self.axis = axis
        if axis == "narrow":
            self.split = lambda i: (i // 2, i % 2, 0)
        else:
            self.split = lambda i: (i // 2 % 4, i // 8, i % 2)
        self.places = [self.split(i) for i in range(lax.axis_size(axis))]
        index_of = {place: i for i, place in enumerate(self.places)}

        def pairs(steps, flip, core):
            return [
                (i, index_of[((r + steps) % 4, p ^ flip, c ^ core)])
                for i, (r, p, c) in enumerate(self.places)
            ]

        self.pairs = pairs
        self.at_ring, self.at_pair, self.at_core = self.split(lax.axis_index(axis))

    def up(self, block):
        return lax.ppermute(block, self.axis, self.pairs(1, 0, 0))

    def down(self, block):
        return lax.ppermute(block, self.axis, self.pairs(-1, 0, 0))

    def swap(self, block):
        return lax.ppermute(block, self.axis, self.pairs(0, 1, 0))

    def cores(self, block):
        return lax.ppermute(block, self.axis, self.pairs(0, 0, 1))

    def ring(self, steps):
        return (self.at_ring + steps) % 4


def place(buffer, block, *index):
    start = tuple(index) + (0,) * (buffer.ndim - len(index))
    shape = (1,) * (buffer.ndim - block.ndim) + block.shape
    return lax.dynamic_update_slice(buffer, block.reshape(shape), start)


def halves(block):
    return block.reshape((2, -1) + block.shape[1:])


def gathered_wide(wide, own_core, other_core):
    block = own_core[0]
    rows, half = block.shape[0], block.shape[0] // 2
    every = jnp.zeros((2, 4, 2, 2, half) + block.shape[1:], block.dtype)
    one, other = wide.at_pair, 1 - wide.at_pair
    for core, pieces in ((wide.at_core, own_core), (1 - wide.at_core, other_core)):
        own, up, down, swap, two_up, two_down, far_up, far_down = pieces
        every = place(every, halves(own), one, wide.ring(0), core)
        every = place(every, halves(up), one, wide.ring(3), core)
        every = place(every, halves(down), one, wide.ring(1), core)
        every = place(every, halves(swap), other, wide.ring(0), core)
        every = place(every, halves(two_up[:rows]), other, wide.ring(3), core)
        every = place(every, halves(two_down[:rows]), other, wide.ring(1), core)
        every = place(every, two_up[rows:], one, wide.ring(2), core, 0)
        every = place(every, two_down[rows:], one, wide.ring(2), core, 1)
        every = place(every, far_up, other, wide.ring(2), core, 0)
        every = place(every, far_down, other, wide.ring(2), core, 1)
    return every.reshape((-1,) + block.shape[1:])


def put_kernel(sources, aliased, places, *refs):
    pieces, result = refs[aliased:-1], refs[-1]
    rows = result.shape[1]
    step = pl.program_id(0)
    for i, (piece, block) in enumerate(sources):

        @pl.when(step == i)
        def _():
            result[0] = pieces[piece][block * rows : (block + 1) * rows]


def put(buffer, pieces, sources, places, blocks, rows, vmem_limit=24 << 20):
    columns = pieces[0].shape[1]
    aliased = 0 if buffer is None else 1
    held = () if buffer is None else (buffer,)
    return pl.pallas_call(
        functools.partial(put_kernel, sources, aliased),
        grid_spec=pltpu.PrefetchScalarGridSpec(
            num_scalar_prefetch=1,
            grid=(len(sources),),
            in_specs=[pl.BlockSpec(memory_space=pl.ANY)] * aliased
            + [pl.BlockSpec(piece.shape, lambda i, *_: (0, 0)) for piece in pieces],
            out_specs=pl.BlockSpec((1, rows, columns), lambda i, places: (places[i], 0, 0)),
        ),
        out_shape=jax.ShapeDtypeStruct((blocks, rows, columns), pieces[0].dtype),
        input_output_aliases={1: 0} if aliased else {},
        compiler_params=pltpu.CompilerParams(vmem_limit_bytes=vmem_limit),
        cost_estimate=pl.CostEstimate(
            flops=0, bytes_accessed=4 * len(sources) * rows * columns, transcendentals=0
        ),
        name="put",
    )(places, *held, *pieces)


def pack_kernel(payloads, pieces, *refs):
    for payload, out in zip(payloads, refs[pieces:]):
        start = 0
        for piece, source, count in payload:
            out[start : start + count] = refs[piece][source : source + count]
            start += count


def pack(pieces, payloads, steps, vmem_limit=8 << 20):
    columns = pieces[0].shape[1]
    rows = [sum(count for _, _, count in payload) for payload in payloads]
    block = lambda count: pl.BlockSpec((count, columns // steps), lambda i: (0, i))
    return pl.pallas_call(
        functools.partial(pack_kernel, tuple(payloads), len(pieces)),
        grid=(steps,),
        in_specs=[block(piece.shape[0]) for piece in pieces],
        out_specs=[block(count) for count in rows],
        out_shape=[jax.ShapeDtypeStruct((count, columns), pieces[0].dtype) for count in rows],
        compiler_params=pltpu.CompilerParams(vmem_limit_bytes=vmem_limit),
        cost_estimate=pl.CostEstimate(
            flops=0, bytes_accessed=4 * sum(rows) * columns, transcendentals=0
        ),
        name="pack",
    )(*pieces)


def shards(
    tokens,
    ln_gain,
    w_qkv,
    q_gain,
    k_gain,
    stored_keys,
    stored_values,
    span_lengths,
    fill_positions,
    w_out,
):
    barrier = lax.optimization_barrier
    wide, narrow = Ring("wide"), Ring("narrow")
    wide_count = lax.axis_size("wide")
    streams = span_lengths.shape[0]
    rows = tokens.shape[0] // lax.axis_size("narrow")
    slots = rows // streams
    depth = w_qkv.shape[0]
    half_rows, half_depth = rows // 2, depth // 2

    own_rows = lax.all_to_all(tokens, "narrow", split_axis=0, concat_axis=1, tiled=True)
    w_up, w_down, w_swap = narrow.up(w_qkv), narrow.down(w_qkv), narrow.swap(w_qkv)
    o_up, o_down = wide.up(w_out), wide.down(w_out)
    token_values = own_rows.astype(jnp.float32)
    own_squares = jnp.sum(token_values * token_values, axis=1)
    normed = (token_values * ln_gain[None, :]).astype(jnp.bfloat16)
    w_up, w_down, w_swap, o_up, o_down, normed = barrier(
        (w_up, w_down, w_swap, o_up, o_down, normed)
    )

    w_swap_up, w_swap_down = narrow.up(w_swap), narrow.down(w_swap)
    t_up, t_down, t_swap = wide.up(normed), wide.down(normed), wide.swap(normed)
    inverse = jnp.broadcast_to(lax.rsqrt(own_squares / D + EPSILON)[:, None], (rows, HEAD_SIZE))
    cosine, sine = turn_tables(fill_positions, slots)
    w_swap_up, w_swap_down, t_up, t_down, t_swap, inverse, cosine, sine = barrier(
        (w_swap_up, w_swap_down, t_up, t_down, t_swap, inverse, cosine, sine)
    )

    w_far_up = narrow.up(jnp.concatenate([w_up[:half_depth], w_swap_up[:half_depth]]))
    w_far_down = narrow.down(jnp.concatenate([w_down[half_depth:], w_swap_down[half_depth:]]))
    t_two_up = wide.up(jnp.concatenate([t_swap, t_up[:half_rows]]))
    t_two_down = wide.down(jnp.concatenate([t_swap, t_down[half_rows:]]))
    near = wide.cores(jnp.stack([normed, t_up, t_down, t_swap]))
    t_two_up, t_two_down, w_far_up, w_far_down, near = barrier(
        (t_two_up, t_two_down, w_far_up, w_far_down, near)
    )

    t_far_up = wide.up(t_two_up[:half_rows])
    t_far_down = wide.down(t_two_down[half_rows:rows])
    o_swap = wide.swap(w_out)
    two = wide.cores(jnp.stack([t_two_up, t_two_down]))
    far = wide.cores(jnp.stack([t_far_up, t_far_down]))

    columns = jnp.zeros((4, 2, 2, half_depth) + w_qkv.shape[1:], w_qkv.dtype)
    one, other = narrow.at_pair, 1 - narrow.at_pair
    columns = place(columns, halves(w_qkv), narrow.ring(0), one)
    columns = place(columns, halves(w_up), narrow.ring(3), one)
    columns = place(columns, halves(w_down), narrow.ring(1), one)
    columns = place(columns, halves(w_swap), narrow.ring(0), other)
    columns = place(columns, halves(w_swap_up), narrow.ring(3), other)
    columns = place(columns, halves(w_swap_down), narrow.ring(1), other)
    w_far_up, w_far_down = halves(w_far_up), halves(w_far_down)
    columns = place(columns, w_far_up[0], narrow.ring(2), one, 0)
    columns = place(columns, w_far_down[0], narrow.ring(2), one, 1)
    columns = place(columns, w_far_up[1], narrow.ring(2), other, 0)
    columns = place(columns, w_far_down[1], narrow.ring(2), other, 1)
    columns = columns.reshape(-1, w_qkv.shape[1])

    every = gathered_wide(
        wide,
        (normed, t_up, t_down, t_swap, t_two_up, t_two_down, t_far_up, t_far_down),
        (*near, *two, *far),
    )

    every, columns, o_swap = barrier((every, columns, o_swap))
    projected = jnp.dot(every, columns, preferred_element_type=jnp.float32).astype(jnp.bfloat16)
    packed = lax.all_to_all(
        projected.reshape(wide_count, rows, -1), "wide", split_axis=0, concat_axis=0, tiled=True
    )
    packed, o_swap, o_up, o_down = barrier((packed, o_swap, o_up, o_down))

    out_rows = w_out.shape[0]
    half_out = out_rows // 2
    o_two_up = wide.up(jnp.concatenate([o_swap, o_up[:half_out]]))
    o_two_down = wide.down(jnp.concatenate([o_swap, o_down[half_out:]]))
    attended = attend(
        packed,
        inverse,
        cosine,
        sine,
        q_gain,
        k_gain,
        stored_keys,
        stored_values,
        span_lengths,
        fill_positions,
    )

    quarter = rows // 4
    attended, w_out, o_up, o_down, o_swap = barrier((attended, w_out, o_up, o_down, o_swap))
    a_up, a_down, a_swap = narrow.up(attended), narrow.down(attended), narrow.swap(attended)
    o_far_up = wide.up(o_two_up[:half_out])
    o_far_down = wide.down(o_two_down[half_out:out_rows])
    o_near, o_rest = pack(
        (w_out, o_up, o_down, o_swap, o_two_up, o_two_down, o_far_up, o_far_down),
        (
            tuple((i, 0, out_rows) for i in range(4)),
            ((4, 0, 3 * half_out), (5, 0, 3 * half_out), (6, 0, half_out), (7, 0, half_out)),
        ),
        5,
        12 << 20,
    )
    a_up, a_down, a_swap, o_far_up, o_far_down, o_near, o_rest = barrier(
        (a_up, a_down, a_swap, o_far_up, o_far_down, o_near, o_rest)
    )

    b_up, b_down, b_swap = pack(
        (a_up, a_down, a_swap),
        (
            ((2, half_rows, half_rows), (0, 0, half_rows)),
            ((2, half_rows, half_rows), (1, half_rows, half_rows)),
            ((0, 0, half_rows), (1, 0, half_rows)),
        ),
        4,
    )
    b_up, b_down, b_swap = narrow.up(b_up), narrow.down(b_down), narrow.swap(b_swap)
    o_near = wide.cores(o_near)
    o_rest = wide.cores(o_rest)
    chips = tuple(
        (pair * 4 + wide.ring(ring)) * 2
        for ring, pair in (
            (0, wide.at_pair),
            (3, wide.at_pair),
            (1, wide.at_pair),
            (0, 1 - wide.at_pair),
            (3, 1 - wide.at_pair),
            (1, 1 - wide.at_pair),
            (2, wide.at_pair),
            (2, 1 - wide.at_pair),
        )
    )
    every_w_out = put(
        None,
        (w_out, o_up, o_down, o_swap, o_two_up, o_two_down, o_far_up, o_far_down),
        tuple((i, half) for i in range(6) for half in range(2))
        + ((4, 2), (5, 2), (6, 0), (7, 0)),
        jnp.stack([(chip + wide.at_core) * 2 + half for chip in chips for half in range(2)]),
        wide_count * 2,
        half_out,
    )
    every_w_out = put(
        every_w_out,
        (o_near, o_rest),
        tuple((0, i) for i in range(8)) + tuple((1, i) for i in (0, 1, 3, 4, 2, 5, 6, 7)),
        jnp.stack([(chip + 1 - wide.at_core) * 2 + half for chip in chips for half in range(2)]),
        wide_count * 2,
        half_out,
    ).reshape(-1, w_out.shape[1])

    def project_out(part):
        product = jnp.dot(part, every_w_out, preferred_element_type=jnp.float32)
        return product.astype(jnp.bfloat16)

    near_rows = project_out(jnp.concatenate([attended, a_swap, a_up, a_down]))
    b_up, b_down, b_swap, near_rows = barrier((b_up, b_down, b_swap, near_rows))
    c_up = narrow.up(b_up[:quarter])
    c_down = narrow.down(b_down[quarter:half_rows])
    c_swap = narrow.swap(b_up[half_rows:])
    one, other = narrow.at_pair, 1 - narrow.at_pair
    place_of = lambda ring, pair, half: (narrow.ring(ring) * 2 + pair) * 2 + half
    result = put(
        None,
        (near_rows, project_out(jnp.concatenate([b_swap, b_up, b_down]))),
        tuple((0, i) for i in range(8)) + tuple((1, i) for i in range(6)),
        jnp.stack(
            [
                place_of(ring, pair, half)
                for ring, pair in ((0, one), (0, other), (3, one), (1, one))
                for half in range(2)
            ]
            + [
                place_of(*place)
                for place in (
                    (3, other, 0),
                    (1, other, 0),
                    (3, other, 1),
                    (2, one, 0),
                    (1, other, 1),
                    (2, one, 1),
                )
            ]
        ),
        16,
        half_rows,
    )
    result, c_up, c_down, c_swap = barrier((result, c_up, c_down, c_swap))
    result = put(
        result,
        (project_out(jnp.concatenate([c_swap, c_up, c_down])),),
        ((0, 0), (0, 1)),
        jnp.stack([place_of(2, other, 0), place_of(2, other, 1)]),
        16,
        half_rows,
    )
    return result.reshape(-1, result.shape[-1])


def solution(mesh):
    placed = (
        P("wide", "narrow"),
        P(),
        P("narrow", "wide"),
        P(),
        P(),
        P(("wide", "narrow"), None, None),
        P(("wide", "narrow"), None, None),
        P(("wide", "narrow")),
        P(("wide", "narrow")),
        P("wide", "narrow"),
    )
    return jax.shard_map(
        shards, mesh=mesh, in_specs=placed, out_specs=P("wide", "narrow"), check_vma=False
    )
```

profile of v0, /device:TPU:0, one launch (start us, length us, event | category | flops | bytes accessed | tf_op | source)
XLA Modules:
  0.0 231.1 jit_solution(11604220902236546737)
XLA Ops:
  0.0 2.0 collective-permute-start
  2.0 2.1 collective-permute-start.1
  4.1 1.5 collective-permute-start.2
  5.6 1.6 collective-permute-start.3
  7.2 1.7 collective-permute-start.4
  8.9 3.5 %all-to-all-start = ((bf16[8,64,640]{2,1,0:T(8,128)(2,1)}), bf16[8,64,640]{2,1,0:T(8,128)(2,1)S(1)}, u32[]{:S(2)}, u32[]{:S(2)}) async-start(bf16[8,64,640]{2,1,0:T(8,128)(2,1)} %bitcast.150), calls=%async_computation | async-start | bytes 1310720 | tf_op jit(solution)/shard_map/all_to_all | solution.py:306
  13.8 3.5 %broadcast_in_dim.12 = bf16[4,2,2,320,640]{4,3,2,1,0:T(8,128)(2,1)} broadcast(bf16[]{:T(256)} %constant.198.clone.1), dimensions={} | broadcast | bytes 6553602 | tf_op jit(solution)/shard_map/broadcast_in_dim | solution.py:339
  17.2 1.0 constant_dynamic-update-slice_fusion.5
  18.3 14.0 %all-to-all-done = bf16[8,64,640]{2,1,0:T(8,128)(2,1)S(1)} async-done(((bf16[8,64,640]{2,1,0:T(8,128)(2,1)}), bf16[8,64,640]{2,1,0:T(8,128)(2,1)S(1)}, u32[]{:S(2)}, u32[]{:S(2)}) %all-to-all-start) | async-done | bytes 655392 | tf_op jit(solution)/shard_map/all_to_all | solution.py:306
  33.2 3.0 %collective-permute-start.6 = (bf16[640,640]{1,0:T(8,128)(2,1)}, bf16[640,640]{1,0:T(8,128)(2,1)}, u32[]{:S(2)}, u32[]{:S(2)}) collective-permute-start(bf16[640,640]{1,0:T(8,128)(2,1)} %collective-permute-done.2), channel_id=1, source_target_pairs={{0,6},{1,7},{2,0},{3,1},{4,2},{5,3},{6,4},{7,5},{8,14},{9,15},{10,... | collective-permute-start | bytes 2457608 | tf_op jit(solution)/shard_map/ppermute | solution.py:183
  36.2 1.6 collective-permute-start.7
  37.7 1.7 collective-permute-start.8
  39.4 3.0 %collective-permute-start.9 = (bf16[64,5120]{1,0:T(8,128)(2,1)S(1)}, bf16[64,5120]{1,0:T(8,128)(2,1)S(1)}, u32[]{:S(2)}, u32[]{:S(2)}) collective-permute-start(bf16[64,5120]{1,0:T(8,128)(2,1)S(1)} %multiply_convert_fusion), channel_id=1, source_target_pairs={{0,64},{8,72},{16,80},{24,88},{32,96},{40,104},{48,112},{56,120},{... | collective-permute-start | bytes 1966088 | tf_op jit(solution)/shard_map/ppermute | solution.py:186
  42.4 1.8 slice.95
  44.2 1.0 slice.97
  45.3 2.1 constant_dynamic-update-slice_fusion.4
  47.4 2.1 constant_dynamic-update-slice_fusion.3
  49.5 2.1 constant_dynamic-update-slice_fusion.2
  51.6 1.3 broadcast_in_dim.10
  53.0 1.6 collective-permute-done.9
  54.8 1.0 slice.94
  55.8 1.4 pad_maximum_fusion
  57.9 2.9 %collective-permute-start.11 = (bf16[96,5120]{1,0:T(8,128)(2,1)S(1)}, bf16[96,5120]{1,0:T(8,128)(2,1)S(1)}, u32[]{:S(2)}, u32[]{:S(2)}) collective-permute-start(bf16[96,5120]{1,0:T(8,128)(2,1)S(1)} %get-tuple-element.115), channel_id=1, source_target_pairs={{0,48},{8,56},{16,0},{24,8},{32,16},{40,24},{48,32},{56,40},{64,11... | collective-permute-start | bytes 2949128 | tf_op jit(solution)/shard_map/ppermute | solution.py:183
  60.8 1.0 slice.96
  62.0 1.0 slice.98
  63.2 3.3 %collective-permute-start.13 = (bf16[640,640]{1,0:T(8,128)(2,1)S(1)}, bf16[640,640]{1,0:T(8,128)(2,1)S(1)}, u32[]{:S(2)}, u32[]{:S(2)}) collective-permute-start(bf16[640,640]{1,0:T(8,128)(2,1)S(1)} %pad_maximum_fusion.7), channel_id=1, source_target_pairs={{0,6},{1,7},{2,0},{3,1},{4,2},{5,3},{6,4},{7,5},{8,14},{9,15},{10,... | collective-permute-start | bytes 2457608 | tf_op jit(solution)/shard_map/ppermute | solution.py:183
  66.5 1.1 constant_dynamic-update-slice_fusion.15
  67.7 2.1 constant_dynamic-update-slice_fusion.1
  69.8 2.1 constant_dynamic-update-slice_fusion
  71.9 11.4 %collective-permute-done.12 = bf16[640,640]{1,0:T(8,128)(2,1)S(1)} collective-permute-done((bf16[640,640]{1,0:T(8,128)(2,1)S(1)}, bf16[640,640]{1,0:T(8,128)(2,1)S(1)}, u32[]{:S(2)}, u32[]{:S(2)}) %collective-permute-start.12) | collective-permute-done | bytes 819232 | tf_op jit(solution)/shard_map/ppermute | solution.py:180
  83.3 3.0 %collective-permute-start.19 = (bf16[512,640]{1,0:T(8,128)(2,1)S(1)}, bf16[512,640]{1,0:T(8,128)(2,1)S(1)}, u32[]{:S(2)}, u32[]{:S(2)}) collective-permute-start(bf16[512,640]{1,0:T(8,128)(2,1)S(1)} %copy-done.3), channel_id=1, source_target_pairs={{0,64},{8,72},{16,80},{24,88},{32,96},{40,104},{48,112},{56,120},{... | collective-permute-start | bytes 1966088 | tf_op jit(solution)/shard_map/ppermute | solution.py:186
  86.8 3.2 %collective-permute-start.16 = (bf16[32,5120]{1,0:T(8,128)(2,1)S(1)}, bf16[32,5120]{1,0:T(8,128)(2,1)S(1)}, u32[]{:S(2)}, u32[]{:S(2)}) collective-permute-start(bf16[32,5120]{1,0:T(8,128)(2,1)S(1)} %slice.104), channel_id=1, source_target_pairs={{0,48},{8,56},{16,0},{24,8},{32,16},{40,24},{48,32},{56,40},{64,11... | collective-permute-start | bytes 983048 | tf_op jit(solution)/shard_map/ppermute | solution.py:183
  93.7 2.7 %collective-permute-done.15 = bf16[32,5120]{1,0:T(8,128)(2,1)S(1)} collective-permute-done((bf16[32,5120]{1,0:T(8,128)(2,1)S(1)}, bf16[32,5120]{1,0:T(8,128)(2,1)S(1)}, u32[]{:S(2)}, u32[]{:S(2)}) %collective-permute-start.15) | collective-permute-done | bytes 327712 | tf_op jit(solution)/shard_map/ppermute | solution.py:180
  97.4 1.4 collective-permute-done.18
  98.9 1.6 collective-permute-done.19.refs_3_
  100.5 10.4 %convolution_convert_fusion = bf16[1024,640]{1,0:T(8,128)(2,1)S(1)} fusion(bf16[1024,5120]{1,0:T(8,128)(2,1)S(1)} %bitcast.128, bf16[5120,640]{1,0:T(8,128)(2,1)} %bitcast.57), kind=kOutput, calls=%fused_computation.18 | convolution fusion | flops 6711541760 | bytes 18350080 | tf_op jit(solution)/shard_map/dot_general | solution.py:361
  111.0 25.4 %all_to_all.18.packed = bf16[16,64,640]{2,1,0:T(8,128)(2,1)S(1)} all-to-all(bf16[16,64,640]{2,1,0:T(8,128)(2,1)S(1)} %bitcast.146), channel_id=1, replica_groups=mesh['wide'=16,'narrow'=8] {'wide'}, dimensions={0} | all-to-all | bytes 2621440 | tf_op jit(solution)/shard_map/all_to_all | solution.py:362
  136.8 3.2 %collective-permute-start.25 = (bf16[768,640]{1,0:T(8,128)(2,1)S(1)}, bf16[768,640]{1,0:T(8,128)(2,1)S(1)}, u32[]{:S(2)}, u32[]{:S(2)}) collective-permute-start(bf16[768,640]{1,0:T(8,128)(2,1)S(1)} %get-tuple-element.113), channel_id=1, source_target_pairs={{0,48},{8,56},{16,0},{24,8},{32,16},{40,24},{48,32},{56,40},{64,11... | collective-permute-start | bytes 2949128 | tf_op jit(solution)/shard_map/ppermute | solution.py:183
  140.0 11.3 %attend.1 = bf16[64,8192]{1,0:T(8,128)(2,1)S(1)} custom-call(s32[4]{0:T(128)S(1)} %copy-done.22, s32[4]{0:T(128)S(1)} %copy-done.23, bf16[16,64,640]{2,1,0:T(8,128)(2,1)S(1)} %all_to_all.18.packed, f32[64,128]{1,0:T(8,128)S(1)} %broadcast_in_dim.11.inverse, f32[64,128]{1,0:T(8,128)S(1)} %get-tuple-element.77.cosine, f32[64,128]{1,0:T(8,128)S(1)} %get-tuple-element.78.sine, ...), custom_call_target="tpu_custom_call" | custom-call | flops 570425344 | bytes 6553600 | tf_op jit(solution)/shard_map/attend/pallas_call | solution.py:121
  151.4 3.2 %collective-permute-start.21 = (bf16[64,8192]{1,0:T(8,128)(2,1)S(1)}, bf16[64,8192]{1,0:T(8,128)(2,1)S(1)}, u32[]{:S(2)}, u32[]{:S(2)}) collective-permute-start(bf16[64,8192]{1,0:T(8,128)(2,1)S(1)} %attend.1), channel_id=1, source_target_pairs={{0,6},{1,7},{2,0},{3,1},{4,2},{5,3},{6,4},{7,5},{8,14},{9,15},{10,... | collective-permute-start | bytes 3145736 | tf_op jit(solution)/shard_map/ppermute | solution.py:183
  154.6 6.5 %collective-permute-done.23.refs_4_ = bf16[768,640]{1,0:T(8,128)(2,1)S(1)} collective-permute-done((bf16[768,640]{1,0:T(8,128)(2,1)S(1)}, bf16[768,640]{1,0:T(8,128)(2,1)S(1)}, u32[]{:S(2)}, u32[]{:S(2)}) %collective-permute-start.23) | collective-permute-done | bytes 983072 | tf_op jit(solution)/shard_map/ppermute | solution.py:180
  161.3 3.3 %collective-permute-start.26 = (bf16[256,640]{1,0:T(8,128)(2,1)S(1)}, bf16[256,640]{1,0:T(8,128)(2,1)S(1)}, u32[]{:S(2)}, u32[]{:S(2)}) collective-permute-start(bf16[256,640]{1,0:T(8,128)(2,1)S(1)} %slice.125), channel_id=1, source_target_pairs={{0,48},{8,56},{16,0},{24,8},{32,16},{40,24},{48,32},{56,40},{64,11... | collective-permute-start | bytes 983048 | tf_op jit(solution)/shard_map/ppermute | solution.py:183
  164.6 6.1 %collective-permute-done.24.refs_6_ = bf16[256,640]{1,0:T(8,128)(2,1)S(1)} collective-permute-done((bf16[256,640]{1,0:T(8,128)(2,1)S(1)}, bf16[256,640]{1,0:T(8,128)(2,1)S(1)}, u32[]{:S(2)}, u32[]{:S(2)}) %collective-permute-start.24) | collective-permute-done | bytes 327712 | tf_op jit(solution)/shard_map/ppermute | solution.py:180
  170.7 4.0 %pack.2 = (bf16[2048,640]{1,0:T(8,128)(2,1)}, bf16[2048,640]{1,0:T(8,128)(2,1)}) custom-call(bf16[512,640]{1,0:T(8,128)(2,1)S(1)} %copy-done.3, bf16[512,640]{1,0:T(8,128)(2,1)S(1)} %collective-permute-done.3.refs_1_, bf16[512,640]{1,0:T(8,128)(2,1)S(1)} %copy-done.1, bf16[512,640]{1,0:T(8,128)(2,1)S(1)} %collective-permute-done.19.refs_3_, ...), custom_call_target="tpu_custom_call" | custom-call | bytes 10485760 | tf_op jit(solution)/shard_map/pack/pallas_call | solution.py:271
  174.8 1.9 collective-permute-done.20.refs_0_
  177.6 1.0 copy-done.14
  178.7 1.0 copy-done.17
  180.5 1.2 copy-done.12
  181.8 1.2 copy-done.15
  183.0 1.2 copy-done.18
  185.0 3.2 %collective-permute-start.28 = (bf16[64,8192]{1,0:T(8,128)(2,1)S(1)}, bf16[64,8192]{1,0:T(8,128)(2,1)S(1)}, u32[]{:S(2)}, u32[]{:S(2)}) collective-permute-start(bf16[64,8192]{1,0:T(8,128)(2,1)S(1)} %get-tuple-element.93), channel_id=1, source_target_pairs={{0,6},{1,7},{2,0},{3,1},{4,2},{5,3},{6,4},{7,5},{8,14},{9,15},{10,... | collective-permute-start | bytes 3145736 | tf_op jit(solution)/shard_map/ppermute | solution.py:183
  188.3 1.1 copy-done.2
  189.3 1.1 copy-done.4
  192.4 2.3 put.4.refs_0_
  194.7 5.2 %put.5 = bf16[32,256,640]{2,1,0:T(8,128)(2,1)S(1)} custom-call(s32[16]{0:T(128)S(1)} %stack.234.places, bf16[32,256,640]{2,1,0:T(8,128)(2,1)S(1)} %put.4.refs_0_, bf16[2048,640]{1,0:T(8,128)(2,1)} %collective-permute-done.30.refs_1_, bf16[2048,640]{1,0:T(8,128)(2,1)} %collective-permute-done.31.refs_2_), custom_call_target="tpu_custom_call", output_to_operand_aliasing={{}: (1, {})} | custom-call | bytes 10485760 | tf_op jit(solution)/shard_map/put/pallas_call | solution.py:240
  200.0 3.4 %fusion.15.refs_0_ = bf16[256,640]{1,0:T(8,128)(2,1)S(1)} fusion(bf16[8192,640]{1,0:T(8,128)(2,1)S(1)} %bitcast.123, bf16[64,8192]{1,0:T(8,128)(2,1)S(1)} %copy-done.16, bf16[64,8192]{1,0:T(8,128)(2,1)S(1)} %copy-done.13, bf16[64,8192]{1,0:T(8,128)(2,1)S(1)} %copy-done.19, bf16[64,8192]{1,0:T(8,128)(2,1)S(1)} %copy-done.21), kind=kOutput, calls=%fused_computation.21 | convolution fusion | flops 2701295616 | bytes 15007744 | tf_op jit(solution)/shard_map/dot_general | solution.py:446
  203.4 7.9 %collective-permute-done.27 = bf16[64,8192]{1,0:T(8,128)(2,1)S(1)} collective-permute-done((bf16[64,8192]{1,0:T(8,128)(2,1)S(1)}, bf16[64,8192]{1,0:T(8,128)(2,1)S(1)}, u32[]{:S(2)}, u32[]{:S(2)}) %collective-permute-start.27) | collective-permute-done | bytes 1048608 | tf_op jit(solution)/shard_map/ppermute | solution.py:180
  211.3 1.5 collective-permute-done.29
  212.9 3.3 %collective-permute-start.33 = (bf16[16,8192]{1,0:T(8,128)(2,1)S(1)}, bf16[16,8192]{1,0:T(8,128)(2,1)S(1)}, u32[]{:S(2)}, u32[]{:S(2)}) collective-permute-start(bf16[16,8192]{1,0:T(8,128)(2,1)S(1)} %slice.118), channel_id=1, source_target_pairs={{0,6},{1,7},{2,0},{3,1},{4,2},{5,3},{6,4},{7,5},{8,14},{9,15},{10,... | collective-permute-start | bytes 786440 | tf_op jit(solution)/shard_map/ppermute | solution.py:183
  216.5 2.8 %fusion.18.refs_1_ = bf16[192,640]{1,0:T(8,128)(2,1)S(1)} fusion(bf16[8192,640]{1,0:T(8,128)(2,1)S(1)} %bitcast.124, bf16[64,8192]{1,0:T(8,128)(2,1)S(1)} %collective-permute-done.28, bf16[64,8192]{1,0:T(8,128)(2,1)S(1)} %collective-permute-done.27, bf16[64,8192]{1,0:T(8,128)(2,1)S(1)} %collective-permute-done.29), kind=kOutput, calls=%fused_computation.22 | convolution fusion | flops 2022825984 | bytes 13877248 | tf_op jit(solution)/shard_map/dot_general | solution.py:446
  219.3 5.1 %put.6.refs_0_ = bf16[16,32,640]{2,1,0:T(8,128)(2,1)} custom-call(s32[14]{0:T(128)S(1)} %stack.206.places, bf16[256,640]{1,0:T(8,128)(2,1)S(1)} %fusion.15.refs_0_, bf16[192,640]{1,0:T(8,128)(2,1)S(1)} %fusion.18.refs_1_), custom_call_target="tpu_custom_call" | custom-call | bytes 1146880 | tf_op jit(solution)/shard_map/put/pallas_call | solution.py:240
  224.3 3.7 %collective-permute-done.34 = bf16[32,8192]{1,0:T(8,128)(2,1)S(1)} collective-permute-done((bf16[32,8192]{1,0:T(8,128)(2,1)S(1)}, bf16[32,8192]{1,0:T(8,128)(2,1)S(1)}, u32[]{:S(2)}, u32[]{:S(2)}) %collective-permute-start.34) | collective-permute-done | bytes 524320 | tf_op jit(solution)/shard_map/ppermute | solution.py:186
  228.0 1.9 convolution_convert_fusion.1.refs_1_
  229.9 1.2 put.7
  (151 shorter events, 13.8 us)
Async XLA Ops:
  0.0 32.8 %collective-permute-start = (bf16[640,640]{1,0:T(8,128)(2,1)}, bf16[640,640]{1,0:T(8,128)(2,1)}, u32[]{:S(2)}, u32[]{:S(2)}) collective-permute-start(bf16[640,640]{1,0:T(8,128)(2,1)} %param.12), channel_id=1, source_target_pairs={{0,2},{1,3},{2,4},{3,5},{4,6},{5,7},{6,0},{7,1},{8,10},{9,11},{10,... | collective-permute-start | bytes 2457608 | tf_op jit(solution)/shard_map/ppermute | solution.py:180
  2.0 30.8 %collective-permute-start.1 = (bf16[640,640]{1,0:T(8,128)(2,1)}, bf16[640,640]{1,0:T(8,128)(2,1)}, u32[]{:S(2)}, u32[]{:S(2)}) collective-permute-start(bf16[640,640]{1,0:T(8,128)(2,1)} %param.12), channel_id=1, source_target_pairs={{0,6},{1,7},{2,0},{3,1},{4,2},{5,3},{6,4},{7,5},{8,14},{9,15},{10,... | collective-permute-start | bytes 2457608 | tf_op jit(solution)/shard_map/ppermute | solution.py:183
  4.1 28.7 %collective-permute-start.2 = (bf16[640,640]{1,0:T(8,128)(2,1)}, bf16[640,640]{1,0:T(8,128)(2,1)}, u32[]{:S(2)}, u32[]{:S(2)}) collective-permute-start(bf16[640,640]{1,0:T(8,128)(2,1)} %param.12), channel_id=1, source_target_pairs={{0,1},{1,0},{2,3},{3,2},{4,5},{5,4},{6,7},{7,6},{8,9},{9,8},{10,11... | collective-permute-start | bytes 2457608 | tf_op jit(solution)/shard_map/ppermute | solution.py:186
  5.6 27.2 %collective-permute-start.3 = (bf16[512,640]{1,0:T(8,128)(2,1)}, bf16[512,640]{1,0:T(8,128)(2,1)S(1)}, u32[]{:S(2)}, u32[]{:S(2)}) collective-permute-start(bf16[512,640]{1,0:T(8,128)(2,1)} %refs_0_.1), channel_id=1, source_target_pairs={{0,16},{8,24},{16,32},{24,40},{32,48},{40,56},{48,0},{56,8},{64,80... | collective-permute-start | bytes 1966088 | tf_op jit(solution)/shard_map/ppermute | solution.py:180
  7.2 25.6 %collective-permute-start.4 = (bf16[512,640]{1,0:T(8,128)(2,1)}, bf16[512,640]{1,0:T(8,128)(2,1)S(1)}, u32[]{:S(2)}, u32[]{:S(2)}) collective-permute-start(bf16[512,640]{1,0:T(8,128)(2,1)} %refs_0_.1), channel_id=1, source_target_pairs={{0,48},{8,56},{16,0},{24,8},{32,16},{40,24},{48,32},{56,40},{64,11... | collective-permute-start | bytes 1966088 | tf_op jit(solution)/shard_map/ppermute | solution.py:183
  8.9 23.4 %all-to-all-start = ((bf16[8,64,640]{2,1,0:T(8,128)(2,1)}), bf16[8,64,640]{2,1,0:T(8,128)(2,1)S(1)}, u32[]{:S(2)}, u32[]{:S(2)}) async-start(bf16[8,64,640]{2,1,0:T(8,128)(2,1)} %bitcast.150), calls=%async_computation | async-start | bytes 1310720 | tf_op jit(solution)/shard_map/all_to_all | solution.py:306
  12.6 19.8 %copy-start.28 = (f32[5120]{0:T(1024)S(1)}, f32[5120]{0:T(1024)}, u32[]{:S(2)}) copy-start(f32[5120]{0:T(1024)} %param.11) | copy-start | bytes 61444
  13.4 3.8 %copy-start.27 = (bf16[640,640]{1,0:T(8,128)(2,1)S(1)}, bf16[640,640]{1,0:T(8,128)(2,1)}, u32[]{:S(2)}) copy-start(bf16[640,640]{1,0:T(8,128)(2,1)} %param.12) | copy-start | bytes 2457604
  32.8 103.6 %copy-start = (bf16[512,640]{1,0:T(8,128)(2,1)}, bf16[512,640]{1,0:T(8,128)(2,1)S(1)}, u32[]{:S(2)}) copy-start(bf16[512,640]{1,0:T(8,128)(2,1)S(1)} %collective-permute-done.4.refs_2_) | copy-start | bytes 1966084
  32.8 21.8 %collective-permute-start.5 = (bf16[640,640]{1,0:T(8,128)(2,1)}, bf16[640,640]{1,0:T(8,128)(2,1)}, u32[]{:S(2)}, u32[]{:S(2)}) collective-permute-start(bf16[640,640]{1,0:T(8,128)(2,1)} %collective-permute-done.2), channel_id=1, source_target_pairs={{0,2},{1,3},{2,4},{3,5},{4,6},{5,7},{6,0},{7,1},{8,10},{9,11},{10,... | collective-permute-start | bytes 2457608 | tf_op jit(solution)/shard_map/ppermute | solution.py:180
  33.2 21.5 %collective-permute-start.6 = (bf16[640,640]{1,0:T(8,128)(2,1)}, bf16[640,640]{1,0:T(8,128)(2,1)}, u32[]{:S(2)}, u32[]{:S(2)}) collective-permute-start(bf16[640,640]{1,0:T(8,128)(2,1)} %collective-permute-done.2), channel_id=1, source_target_pairs={{0,6},{1,7},{2,0},{3,1},{4,2},{5,3},{6,4},{7,5},{8,14},{9,15},{10,... | collective-permute-start | bytes 2457608 | tf_op jit(solution)/shard_map/ppermute | solution.py:183
  36.2 16.9 %collective-permute-start.7 = (bf16[64,5120]{1,0:T(8,128)(2,1)S(1)}, bf16[64,5120]{1,0:T(8,128)(2,1)S(1)}, u32[]{:S(2)}, u32[]{:S(2)}) collective-permute-start(bf16[64,5120]{1,0:T(8,128)(2,1)S(1)} %multiply_convert_fusion), channel_id=1, source_target_pairs={{0,16},{8,24},{16,32},{24,40},{32,48},{40,56},{48,0},{56,8},{64,80... | collective-permute-start | bytes 1966088 | tf_op jit(solution)/shard_map/ppermute | solution.py:180
  37.7 15.3 %collective-permute-start.8 = (bf16[64,5120]{1,0:T(8,128)(2,1)S(1)}, bf16[64,5120]{1,0:T(8,128)(2,1)}, u32[]{:S(2)}, u32[]{:S(2)}) collective-permute-start(bf16[64,5120]{1,0:T(8,128)(2,1)S(1)} %multiply_convert_fusion), channel_id=1, source_target_pairs={{0,48},{8,56},{16,0},{24,8},{32,16},{40,24},{48,32},{56,40},{64,11... | collective-permute-start | bytes 1966088 | tf_op jit(solution)/shard_map/ppermute | solution.py:183
  39.4 15.3 %collective-permute-start.9 = (bf16[64,5120]{1,0:T(8,128)(2,1)S(1)}, bf16[64,5120]{1,0:T(8,128)(2,1)S(1)}, u32[]{:S(2)}, u32[]{:S(2)}) collective-permute-start(bf16[64,5120]{1,0:T(8,128)(2,1)S(1)} %multiply_convert_fusion), channel_id=1, source_target_pairs={{0,64},{8,72},{16,80},{24,88},{32,96},{40,104},{48,112},{56,120},{... | collective-permute-start | bytes 1966088 | tf_op jit(solution)/shard_map/ppermute | solution.py:186
  52.9 8.9 %copy-start.26 = (bf16[320,640]{1,0:T(8,128)(2,1)S(1)}, bf16[320,640]{1,0:T(8,128)(2,1)}, u32[]{:S(2)}) copy-start(bf16[320,640]{1,0:T(8,128)(2,1)} %slice.95) | copy-start | bytes 1228804
  57.2 29.2 %collective-permute-start.14 = (bf16[4,64,5120]{2,1,0:T(8,128)(2,1)S(1)}, bf16[4,64,5120]{2,1,0:T(8,128)(2,1)S(1)}, u32[]{:S(2)}, u32[]{:S(2)}) collective-permute-start(bf16[4,64,5120]{2,1,0:T(8,128)(2,1)S(1)} %pad_maximum_fusion), channel_id=1, source_target_pairs={{0,8},{8,0},{16,24},{24,16},{32,40},{40,32},{48,56},{56,48},{64,72... | collective-permute-start | bytes 7864328 | tf_op jit(solution)/shard_map/ppermute | solution.py:189
  57.5 25.8 %copy-start.3 = (bf16[512,640]{1,0:T(8,128)(2,1)S(1)}, bf16[512,640]{1,0:T(8,128)(2,1)}, u32[]{:S(2)}) copy-start(bf16[512,640]{1,0:T(8,128)(2,1)} %refs_0_.1) | copy-start | bytes 1966084
  57.5 28.8 %collective-permute-start.10 = (bf16[96,5120]{1,0:T(8,128)(2,1)S(1)}, bf16[96,5120]{1,0:T(8,128)(2,1)S(1)}, u32[]{:S(2)}, u32[]{:S(2)}) collective-permute-start(bf16[96,5120]{1,0:T(8,128)(2,1)S(1)} %get-tuple-element.116), channel_id=1, source_target_pairs={{0,16},{8,24},{16,32},{24,40},{32,48},{40,56},{48,0},{56,8},{64,80... | collective-permute-start | bytes 2949128 | tf_op jit(solution)/shard_map/ppermute | solution.py:180
  57.9 28.5 %collective-permute-start.11 = (bf16[96,5120]{1,0:T(8,128)(2,1)S(1)}, bf16[96,5120]{1,0:T(8,128)(2,1)S(1)}, u32[]{:S(2)}, u32[]{:S(2)}) collective-permute-start(bf16[96,5120]{1,0:T(8,128)(2,1)S(1)} %get-tuple-element.115), channel_id=1, source_target_pairs={{0,48},{8,56},{16,0},{24,8},{32,16},{40,24},{48,32},{56,40},{64,11... | collective-permute-start | bytes 2949128 | tf_op jit(solution)/shard_map/ppermute | solution.py:183
  62.0 21.4 %collective-permute-start.12 = (bf16[640,640]{1,0:T(8,128)(2,1)S(1)}, bf16[640,640]{1,0:T(8,128)(2,1)S(1)}, u32[]{:S(2)}, u32[]{:S(2)}) collective-permute-start(bf16[640,640]{1,0:T(8,128)(2,1)S(1)} %pad_maximum_fusion.6), channel_id=1, source_target_pairs={{0,2},{1,3},{2,4},{3,5},{4,6},{5,7},{6,0},{7,1},{8,10},{9,11},{10,... | collective-permute-start | bytes 2457608 | tf_op jit(solution)/shard_map/ppermute | solution.py:180
  63.2 23.2 %collective-permute-start.13 = (bf16[640,640]{1,0:T(8,128)(2,1)S(1)}, bf16[640,640]{1,0:T(8,128)(2,1)S(1)}, u32[]{:S(2)}, u32[]{:S(2)}) collective-permute-start(bf16[640,640]{1,0:T(8,128)(2,1)S(1)} %pad_maximum_fusion.7), channel_id=1, source_target_pairs={{0,6},{1,7},{2,0},{3,1},{4,2},{5,3},{6,4},{7,5},{8,14},{9,15},{10,... | collective-permute-start | bytes 2457608 | tf_op jit(solution)/shard_map/ppermute | solution.py:183
  83.3 17.2 %collective-permute-start.19 = (bf16[512,640]{1,0:T(8,128)(2,1)S(1)}, bf16[512,640]{1,0:T(8,128)(2,1)S(1)}, u32[]{:S(2)}, u32[]{:S(2)}) collective-permute-start(bf16[512,640]{1,0:T(8,128)(2,1)S(1)} %copy-done.3), channel_id=1, source_target_pairs={{0,64},{8,72},{16,80},{24,88},{32,96},{40,104},{48,112},{56,120},{... | collective-permute-start | bytes 1966088 | tf_op jit(solution)/shard_map/ppermute | solution.py:186
  86.7 9.7 %collective-permute-start.15 = (bf16[32,5120]{1,0:T(8,128)(2,1)S(1)}, bf16[32,5120]{1,0:T(8,128)(2,1)S(1)}, u32[]{:S(2)}, u32[]{:S(2)}) collective-permute-start(bf16[32,5120]{1,0:T(8,128)(2,1)S(1)} %slice.103), channel_id=1, source_target_pairs={{0,16},{8,24},{16,32},{24,40},{32,48},{40,56},{48,0},{56,8},{64,80... | collective-permute-start | bytes 983048 | tf_op jit(solution)/shard_map/ppermute | solution.py:180
  86.8 9.6 %collective-permute-start.16 = (bf16[32,5120]{1,0:T(8,128)(2,1)S(1)}, bf16[32,5120]{1,0:T(8,128)(2,1)S(1)}, u32[]{:S(2)}, u32[]{:S(2)}) collective-permute-start(bf16[32,5120]{1,0:T(8,128)(2,1)S(1)} %slice.104), channel_id=1, source_target_pairs={{0,48},{8,56},{16,0},{24,8},{32,16},{40,24},{48,32},{56,40},{64,11... | collective-permute-start | bytes 983048 | tf_op jit(solution)/shard_map/ppermute | solution.py:183
  90.4 6.7 %collective-permute-start.17 = (bf16[2,96,5120]{2,1,0:T(8,128)(2,1)S(1)}, bf16[2,96,5120]{2,1,0:T(8,128)(2,1)S(1)}, u32[]{:S(2)}, u32[]{:S(2)}) collective-permute-start(bf16[2,96,5120]{2,1,0:T(8,128)(2,1)S(1)} %pad_maximum_fusion.1), channel_id=1, source_target_pairs={{0,8},{8,0},{16,24},{24,16},{32,40},{40,32},{48,56},{56,48},{64,72... | collective-permute-start | bytes 5898248 | tf_op jit(solution)/shard_map/ppermute | solution.py:189
  96.5 2.4 %collective-permute-start.18 = (bf16[2,32,5120]{2,1,0:T(8,128)(2,1)S(1)}, bf16[2,32,5120]{2,1,0:T(8,128)(2,1)S(1)}, u32[]{:S(2)}, u32[]{:S(2)}) collective-permute-start(bf16[2,32,5120]{2,1,0:T(8,128)(2,1)S(1)} %pad_maximum_fusion.8), channel_id=1, source_target_pairs={{0,8},{8,0},{16,24},{24,16},{32,40},{40,32},{48,56},{56,48},{64,72... | collective-permute-start | bytes 1966088 | tf_op jit(solution)/shard_map/ppermute | solution.py:189
  110.9 29.0 %copy-start.5 = (bf16[4,256,1024]{2,1,0:T(8,128)(2,1)S(1)}, bf16[4,256,1024]{2,1,0:T(8,128)(2,1)}, u32[]{:S(2)}) copy-start(bf16[4,256,1024]{2,1,0:T(8,128)(2,1)} %keys.1) | copy-start | bytes 6291460
  111.0 29.0 %copy-start.6 = (bf16[4,256,1024]{2,1,0:T(8,128)(2,1)S(1)}, bf16[4,256,1024]{2,1,0:T(8,128)(2,1)}, u32[]{:S(2)}) copy-start(bf16[4,256,1024]{2,1,0:T(8,128)(2,1)} %values.1) | copy-start | bytes 6291460
  111.0 29.0 %copy-start.22 = (s32[4]{0:T(128)S(1)}, s32[4]{0:T(128)}, u32[]{:S(2)}) copy-start(s32[4]{0:T(128)} %fills.1) | copy-start | bytes 52
  111.0 29.0 %copy-start.23 = (s32[4]{0:T(128)S(1)}, s32[4]{0:T(128)}, u32[]{:S(2)}) copy-start(s32[4]{0:T(128)} %spans.1) | copy-start | bytes 52
  111.0 29.0 %copy-start.24 = (f32[128]{0:T(128)S(1)}, f32[128]{0:T(128)}, u32[]{:S(2)}) copy-start(f32[128]{0:T(128)} %param.13) | copy-start | bytes 1540
  111.0 29.0 %copy-start.25 = (f32[128]{0:T(128)S(1)}, f32[128]{0:T(128)}, u32[]{:S(2)}) copy-start(f32[128]{0:T(128)} %param.14) | copy-start | bytes 1540
  136.5 34.2 %copy-start.1 = (bf16[512,640]{1,0:T(8,128)(2,1)S(1)}, bf16[512,640]{1,0:T(8,128)(2,1)}, u32[]{:S(2)}) copy-start(bf16[512,640]{1,0:T(8,128)(2,1)} %copy-done) | copy-start | bytes 1966084
  136.7 24.5 %collective-permute-start.23 = (bf16[768,640]{1,0:T(8,128)(2,1)S(1)}, bf16[768,640]{1,0:T(8,128)(2,1)S(1)}, u32[]{:S(2)}, u32[]{:S(2)}) collective-permute-start(bf16[768,640]{1,0:T(8,128)(2,1)S(1)} %get-tuple-element.114), channel_id=1, source_target_pairs={{0,16},{8,24},{16,32},{24,40},{32,48},{40,56},{48,0},{56,8},{64,80... | collective-permute-start | bytes 2949128 | tf_op jit(solution)/shard_map/ppermute | solution.py:180
  136.8 24.5 %collective-permute-start.25 = (bf16[768,640]{1,0:T(8,128)(2,1)S(1)}, bf16[768,640]{1,0:T(8,128)(2,1)S(1)}, u32[]{:S(2)}, u32[]{:S(2)}) collective-permute-start(bf16[768,640]{1,0:T(8,128)(2,1)S(1)} %get-tuple-element.113), channel_id=1, source_target_pairs={{0,48},{8,56},{16,0},{24,8},{32,16},{40,24},{48,32},{56,40},{64,11... | collective-permute-start | bytes 2949128 | tf_op jit(solution)/shard_map/ppermute | solution.py:183
  151.3 27.4 %copy-start.20 = (bf16[64,8192]{1,0:T(8,128)(2,1)}, bf16[64,8192]{1,0:T(8,128)(2,1)S(1)}, u32[]{:S(2)}) copy-start(bf16[64,8192]{1,0:T(8,128)(2,1)S(1)} %attend.1) | copy-start | bytes 3145732
  151.3 25.3 %collective-permute-start.20 = (bf16[64,8192]{1,0:T(8,128)(2,1)S(1)}, bf16[64,8192]{1,0:T(8,128)(2,1)S(1)}, u32[]{:S(2)}, u32[]{:S(2)}) collective-permute-start(bf16[64,8192]{1,0:T(8,128)(2,1)S(1)} %attend.1), channel_id=1, source_target_pairs={{0,2},{1,3},{2,4},{3,5},{4,6},{5,7},{6,0},{7,1},{8,10},{9,11},{10,... | collective-permute-start | bytes 3145736 | tf_op jit(solution)/shard_map/ppermute | solution.py:180
  151.4 26.2 %collective-permute-start.21 = (bf16[64,8192]{1,0:T(8,128)(2,1)S(1)}, bf16[64,8192]{1,0:T(8,128)(2,1)S(1)}, u32[]{:S(2)}, u32[]{:S(2)}) collective-permute-start(bf16[64,8192]{1,0:T(8,128)(2,1)S(1)} %attend.1), channel_id=1, source_target_pairs={{0,6},{1,7},{2,0},{3,1},{4,2},{5,3},{6,4},{7,5},{8,14},{9,15},{10,... | collective-permute-start | bytes 3145736 | tf_op jit(solution)/shard_map/ppermute | solution.py:183
  154.6 24.1 %collective-permute-start.22 = (bf16[64,8192]{1,0:T(8,128)(2,1)S(1)}, bf16[64,8192]{1,0:T(8,128)(2,1)S(1)}, u32[]{:S(2)}, u32[]{:S(2)}) collective-permute-start(bf16[64,8192]{1,0:T(8,128)(2,1)S(1)} %attend.1), channel_id=1, source_target_pairs={{0,1},{1,0},{2,3},{3,2},{4,5},{5,4},{6,7},{7,6},{8,9},{9,8},{10,11... | collective-permute-start | bytes 3145736 | tf_op jit(solution)/shard_map/ppermute | solution.py:186
  161.2 9.5 %collective-permute-start.24 = (bf16[256,640]{1,0:T(8,128)(2,1)S(1)}, bf16[256,640]{1,0:T(8,128)(2,1)S(1)}, u32[]{:S(2)}, u32[]{:S(2)}) collective-permute-start(bf16[256,640]{1,0:T(8,128)(2,1)S(1)} %slice.124), channel_id=1, source_target_pairs={{0,16},{8,24},{16,32},{24,40},{32,48},{40,56},{48,0},{56,8},{64,80... | collective-permute-start | bytes 983048 | tf_op jit(solution)/shard_map/ppermute | solution.py:180
  161.3 9.4 %collective-permute-start.26 = (bf16[256,640]{1,0:T(8,128)(2,1)S(1)}, bf16[256,640]{1,0:T(8,128)(2,1)S(1)}, u32[]{:S(2)}, u32[]{:S(2)}) collective-permute-start(bf16[256,640]{1,0:T(8,128)(2,1)S(1)} %slice.125), channel_id=1, source_target_pairs={{0,48},{8,56},{16,0},{24,8},{32,16},{40,24},{48,32},{56,40},{64,11... | collective-permute-start | bytes 983048 | tf_op jit(solution)/shard_map/ppermute | solution.py:183
  170.7 4.1 %copy-start.7 = (bf16[256,640]{1,0:T(8,128)(2,1)}, bf16[256,640]{1,0:T(8,128)(2,1)S(1)}, u32[]{:S(2)}) copy-start(bf16[256,640]{1,0:T(8,128)(2,1)S(1)} %collective-permute-done.24.refs_6_) | copy-start | bytes 983044
  170.7 5.9 %copy-start.9 = (bf16[256,640]{1,0:T(8,128)(2,1)}, bf16[256,640]{1,0:T(8,128)(2,1)S(1)}, u32[]{:S(2)}) copy-start(bf16[256,640]{1,0:T(8,128)(2,1)S(1)} %collective-permute-done.26.refs_7_) | copy-start | bytes 983044
  176.6 1.0 copy-start.11
  177.6 1.0 copy-start.14
  178.7 1.0 copy-start.17
  179.7 15.1 %collective-permute-start.30 = (bf16[2048,640]{1,0:T(8,128)(2,1)}, bf16[2048,640]{1,0:T(8,128)(2,1)}, u32[]{:S(2)}, u32[]{:S(2)}) collective-permute-start(bf16[2048,640]{1,0:T(8,128)(2,1)} %get-tuple-element.97), channel_id=1, source_target_pairs={{0,8},{8,0},{16,24},{24,16},{32,40},{40,32},{48,56},{56,48},{64,72... | collective-permute-start | bytes 7864328 | tf_op jit(solution)/shard_map/ppermute | solution.py:189
  179.7 15.1 %collective-permute-start.31 = (bf16[2048,640]{1,0:T(8,128)(2,1)}, bf16[2048,640]{1,0:T(8,128)(2,1)}, u32[]{:S(2)}, u32[]{:S(2)}) collective-permute-start(bf16[2048,640]{1,0:T(8,128)(2,1)} %get-tuple-element.98), channel_id=1, source_target_pairs={{0,8},{8,0},{16,24},{24,16},{32,40},{40,32},{48,56},{56,48},{64,72... | collective-permute-start | bytes 7864328 | tf_op jit(solution)/shard_map/ppermute | solution.py:189
  180.5 1.2 copy-start.12
  181.8 1.2 copy-start.15
  183.0 1.2 copy-start.18
  184.9 26.3 %collective-permute-start.27 = (bf16[64,8192]{1,0:T(8,128)(2,1)S(1)}, bf16[64,8192]{1,0:T(8,128)(2,1)S(1)}, u32[]{:S(2)}, u32[]{:S(2)}) collective-permute-start(bf16[64,8192]{1,0:T(8,128)(2,1)S(1)} %get-tuple-element.92), channel_id=1, source_target_pairs={{0,2},{1,3},{2,4},{3,5},{4,6},{5,7},{6,0},{7,1},{8,10},{9,11},{10,... | collective-permute-start | bytes 3145736 | tf_op jit(solution)/shard_map/ppermute | solution.py:180
  185.0 26.3 %collective-permute-start.28 = (bf16[64,8192]{1,0:T(8,128)(2,1)S(1)}, bf16[64,8192]{1,0:T(8,128)(2,1)S(1)}, u32[]{:S(2)}, u32[]{:S(2)}) collective-permute-start(bf16[64,8192]{1,0:T(8,128)(2,1)S(1)} %get-tuple-element.93), channel_id=1, source_target_pairs={{0,6},{1,7},{2,0},{3,1},{4,2},{5,3},{6,4},{7,5},{8,14},{9,15},{10,... | collective-permute-start | bytes 3145736 | tf_op jit(solution)/shard_map/ppermute | solution.py:183
  188.3 24.5 %collective-permute-start.29 = (bf16[64,8192]{1,0:T(8,128)(2,1)S(1)}, bf16[64,8192]{1,0:T(8,128)(2,1)S(1)}, u32[]{:S(2)}, u32[]{:S(2)}) collective-permute-start(bf16[64,8192]{1,0:T(8,128)(2,1)S(1)} %get-tuple-element.94), channel_id=1, source_target_pairs={{0,1},{1,0},{2,3},{3,2},{4,5},{5,4},{6,7},{7,6},{8,9},{9,8},{10,11... | collective-permute-start | bytes 3145736 | tf_op jit(solution)/shard_map/ppermute | solution.py:186
  188.3 1.1 copy-start.2
  189.3 1.1 copy-start.4
  190.4 1.0 copy-start.8
  194.7 5.3 %copy-start.13 = (bf16[64,8192]{1,0:T(8,128)(2,1)S(1)}, bf16[64,8192]{1,0:T(8,128)(2,1)}, u32[]{:S(2)}) copy-start(bf16[64,8192]{1,0:T(8,128)(2,1)} %copy-done.11) | copy-start | bytes 3145732
  194.7 5.3 %copy-start.16 = (bf16[64,8192]{1,0:T(8,128)(2,1)S(1)}, bf16[64,8192]{1,0:T(8,128)(2,1)}, u32[]{:S(2)}) copy-start(bf16[64,8192]{1,0:T(8,128)(2,1)} %copy-done.14) | copy-start | bytes 3145732
  194.7 5.3 %copy-start.19 = (bf16[64,8192]{1,0:T(8,128)(2,1)S(1)}, bf16[64,8192]{1,0:T(8,128)(2,1)}, u32[]{:S(2)}) copy-start(bf16[64,8192]{1,0:T(8,128)(2,1)} %copy-done.17) | copy-start | bytes 3145732
  194.7 5.3 %copy-start.21 = (bf16[64,8192]{1,0:T(8,128)(2,1)S(1)}, bf16[64,8192]{1,0:T(8,128)(2,1)}, u32[]{:S(2)}) copy-start(bf16[64,8192]{1,0:T(8,128)(2,1)} %copy-done.20) | copy-start | bytes 3145732
  212.8 11.5 %collective-permute-start.32 = (bf16[16,8192]{1,0:T(8,128)(2,1)S(1)}, bf16[16,8192]{1,0:T(8,128)(2,1)S(1)}, u32[]{:S(2)}, u32[]{:S(2)}) collective-permute-start(bf16[16,8192]{1,0:T(8,128)(2,1)S(1)} %slice.117), channel_id=1, source_target_pairs={{0,2},{1,3},{2,4},{3,5},{4,6},{5,7},{6,0},{7,1},{8,10},{9,11},{10,... | collective-permute-start | bytes 786440 | tf_op jit(solution)/shard_map/ppermute | solution.py:180
  212.9 11.4 %collective-permute-start.33 = (bf16[16,8192]{1,0:T(8,128)(2,1)S(1)}, bf16[16,8192]{1,0:T(8,128)(2,1)S(1)}, u32[]{:S(2)}, u32[]{:S(2)}) collective-permute-start(bf16[16,8192]{1,0:T(8,128)(2,1)S(1)} %slice.118), channel_id=1, source_target_pairs={{0,6},{1,7},{2,0},{3,1},{4,2},{5,3},{6,4},{7,5},{8,14},{9,15},{10,... | collective-permute-start | bytes 786440 | tf_op jit(solution)/shard_map/ppermute | solution.py:183
  216.2 11.8 %collective-permute-start.34 = (bf16[32,8192]{1,0:T(8,128)(2,1)S(1)}, bf16[32,8192]{1,0:T(8,128)(2,1)S(1)}, u32[]{:S(2)}, u32[]{:S(2)}) collective-permute-start(bf16[32,8192]{1,0:T(8,128)(2,1)S(1)} %slice.119), channel_id=1, source_target_pairs={{0,1},{1,0},{2,3},{3,2},{4,5},{5,4},{6,7},{7,6},{8,9},{9,8},{10,11... | collective-permute-start | bytes 1572872 | tf_op jit(solution)/shard_map/ppermute | solution.py:186
  (1 other events, 1.0 us)
where the time goes:
time: 232 us; the launch traced here: 231 us
  waiting for transfers between devices  60.3 us (26%)
  starting transfers between devices  52.8 us (23%)
  local copies, waits for them, and re-layouts  39.6 us (17%)
  Pallas kernels  29.8 us (13%)
  blocking collectives  25.4 us (11%)
  matrix products  18.5 us (8%)
  other arithmetic  3.69 us (2%)
    ppermute x12, waiting for transfers between devices, up(): return lax.ppermute(block, self.axis, self.pairs(1, 0, 0))  36.5 us
    ppermute x12, starting transfers between devices, down(): return lax.ppermute(block, self.axis, self.pairs(-1, 0, 0))  34.1 us
    all_to_all x1, blocking collectives, shards(): lax.all_to_all(projected.reshape(wide_count, rows, -1), 'wide', split_axi...  25.4 us
    dynamic_update_slice x30, local copies, waits for them, and re-layouts, place(): return lax.dynamic_update_slice(buffer, block.reshape(shape), start)  16.8 us
    all_to_all x1, waiting for transfers between devices, shards(): lax.all_to_all(tokens, 'narrow', split_axis=0, concat_axis=1, tiled=True)  14 us
    pallas_call x4, Pallas kernels, put(): pl.pallas_call(functools.partial(put_kernel, sources, aliased), grid_spec...  13.8 us
    pallas_call x1, Pallas kernels, attend(): pl.pallas_call(attend_kernel, grid_spec=pltpu.PrefetchScalarGridSpec(num_...  11.3 us
    unnamed x58, local copies, waits for them, and re-layouts  10.9 us
  transfers between devices with their start and end apart: 36, of which 12 were waited for; matrix products, arithmetic and copies ran while one was open for 15% of the time, Pallas kernels for 12%

commit v1 on v0

--- a/solution.py
+++ b/solution.py
@@ -202,26 +202,6 @@
     return block.reshape((2, -1) + block.shape[1:])
 
 
-def gathered_wide(wide, own_core, other_core):
-    block = own_core[0]
-    rows, half = block.shape[0], block.shape[0] // 2
-    every = jnp.zeros((2, 4, 2, 2, half) + block.shape[1:], block.dtype)
-    one, other = wide.at_pair, 1 - wide.at_pair
-    for core, pieces in ((wide.at_core, own_core), (1 - wide.at_core, other_core)):
-        own, up, down, swap, two_up, two_down, far_up, far_down = pieces
-        every = place(every, halves(own), one, wide.ring(0), core)
-        every = place(every, halves(up), one, wide.ring(3), core)
-        every = place(every, halves(down), one, wide.ring(1), core)
-        every = place(every, halves(swap), other, wide.ring(0), core)
-        every = place(every, halves(two_up[:rows]), other, wide.ring(3), core)
-        every = place(every, halves(two_down[:rows]), other, wide.ring(1), core)
-        every = place(every, two_up[rows:], one, wide.ring(2), core, 0)
-        every = place(every, two_down[rows:], one, wide.ring(2), core, 1)
-        every = place(every, far_up, other, wide.ring(2), core, 0)
-        every = place(every, far_down, other, wide.ring(2), core, 1)
-    return every.reshape((-1,) + block.shape[1:])
-
-
 def put_kernel(sources, aliased, places, *refs):
     pieces, result = refs[aliased:-1], refs[-1]
     rows = result.shape[1]
@@ -249,9 +229,7 @@
         out_shape=jax.ShapeDtypeStruct((blocks, rows, columns), pieces[0].dtype),
         input_output_aliases={1: 0} if aliased else {},
         compiler_params=pltpu.CompilerParams(vmem_limit_bytes=vmem_limit),
-        cost_estimate=pl.CostEstimate(
-            flops=0, bytes_accessed=4 * len(sources) * rows * columns, transcendentals=0
-        ),
+        cost_estimate=pl.CostEstimate(flops=0, bytes_accessed=rows, transcendentals=0),
         name="put",
     )(places, *held, *pieces)
 
@@ -275,9 +253,7 @@
         out_specs=[block(count) for count in rows],
         out_shape=[jax.ShapeDtypeStruct((count, columns), pieces[0].dtype) for count in rows],
         compiler_params=pltpu.CompilerParams(vmem_limit_bytes=vmem_limit),
-        cost_estimate=pl.CostEstimate(
-            flops=0, bytes_accessed=4 * sum(rows) * columns, transcendentals=0
-        ),
+        cost_estimate=pl.CostEstimate(flops=0, bytes_accessed=sum(rows), transcendentals=0),
         name="pack",
     )(*pieces)
 
@@ -309,55 +285,74 @@
     token_values = own_rows.astype(jnp.float32)
     own_squares = jnp.sum(token_values * token_values, axis=1)
     normed = (token_values * ln_gain[None, :]).astype(jnp.bfloat16)
-    w_up, w_down, w_swap, o_up, o_down, normed = barrier(
-        (w_up, w_down, w_swap, o_up, o_down, normed)
+    o_up, o_down, w_swap, w_up, w_down, normed = barrier(
+        (o_up, o_down, w_swap, w_up, w_down, normed)
     )
 
     w_swap_up, w_swap_down = narrow.up(w_swap), narrow.down(w_swap)
     t_up, t_down, t_swap = wide.up(normed), wide.down(normed), wide.swap(normed)
     inverse = jnp.broadcast_to(lax.rsqrt(own_squares / D + EPSILON)[:, None], (rows, HEAD_SIZE))
     cosine, sine = turn_tables(fill_positions, slots)
-    w_swap_up, w_swap_down, t_up, t_down, t_swap, inverse, cosine, sine = barrier(
-        (w_swap_up, w_swap_down, t_up, t_down, t_swap, inverse, cosine, sine)
+    one, other = wide.at_pair, 1 - wide.at_pair
+    every = jnp.zeros((2, 4, 2, 2, half_rows) + normed.shape[1:], normed.dtype)
+    every = place(every, halves(normed), one, wide.ring(0), wide.at_core)
+    w_swap_up, w_swap_down, t_up, t_down, t_swap, inverse, cosine, sine, every = barrier(
+        (w_swap_up, w_swap_down, t_up, t_down, t_swap, inverse, cosine, sine, every)
     )
 
     w_far_up = narrow.up(jnp.concatenate([w_up[:half_depth], w_swap_up[:half_depth]]))
     w_far_down = narrow.down(jnp.concatenate([w_down[half_depth:], w_swap_down[half_depth:]]))
     t_two_up = wide.up(jnp.concatenate([t_swap, t_up[:half_rows]]))
     t_two_down = wide.down(jnp.concatenate([t_swap, t_down[half_rows:]]))
-    near = wide.cores(jnp.stack([normed, t_up, t_down, t_swap]))
-    t_two_up, t_two_down, w_far_up, w_far_down, near = barrier(
-        (t_two_up, t_two_down, w_far_up, w_far_down, near)
+    o_swap = wide.swap(w_out)
+    near = jnp.stack([normed, t_up, t_down, t_swap])
+    at_narrow = tuple(
+        narrow.ring(ring) * 2 + pair
+        for pair in (narrow.at_pair, 1 - narrow.at_pair)
+        for ring in (0, 3, 1, 2)
+    )
+    columns = put(
+        None,
+        (w_qkv, w_up, w_down, w_swap, w_swap_up, w_swap_down),
+        tuple((i, half) for i in range(6) for half in range(2)),
+        jnp.stack([at_narrow[i] * 2 + half for i in (0, 1, 2, 4, 5, 6) for half in range(2)]),
+        16,
+        half_depth,
+    )
+    every = place(every, halves(t_up), one, wide.ring(3), wide.at_core)
+    every = place(every, halves(t_down), one, wide.ring(1), wide.at_core)
+    every = place(every, halves(t_swap), other, wide.ring(0), wide.at_core)
+    w_far_up, w_far_down, t_two_up, t_two_down, o_swap, near, columns, every = barrier(
+        (w_far_up, w_far_down, t_two_up, t_two_down, o_swap, near, columns, every)
     )
 
     t_far_up = wide.up(t_two_up[:half_rows])
     t_far_down = wide.down(t_two_down[half_rows:rows])
-    o_swap = wide.swap(w_out)
+    near = wide.cores(near)
     two = wide.cores(jnp.stack([t_two_up, t_two_down]))
     far = wide.cores(jnp.stack([t_far_up, t_far_down]))
-
-    columns = jnp.zeros((4, 2, 2, half_depth) + w_qkv.shape[1:], w_qkv.dtype)
-    one, other = narrow.at_pair, 1 - narrow.at_pair
-    columns = place(columns, halves(w_qkv), narrow.ring(0), one)
-    columns = place(columns, halves(w_up), narrow.ring(3), one)
-    columns = place(columns, halves(w_down), narrow.ring(1), one)
-    columns = place(columns, halves(w_swap), narrow.ring(0), other)
-    columns = place(columns, halves(w_swap_up), narrow.ring(3), other)
-    columns = place(columns, halves(w_swap_down), narrow.ring(1), other)
-    w_far_up, w_far_down = halves(w_far_up), halves(w_far_down)
-    columns = place(columns, w_far_up[0], narrow.ring(2), one, 0)
-    columns = place(columns, w_far_down[0], narrow.ring(2), one, 1)
-    columns = place(columns, w_far_up[1], narrow.ring(2), other, 0)
-    columns = place(columns, w_far_down[1], narrow.ring(2), other, 1)
-    columns = columns.reshape(-1, w_qkv.shape[1])
-
-    every = gathered_wide(
-        wide,
-        (normed, t_up, t_down, t_swap, t_two_up, t_two_down, t_far_up, t_far_down),
-        (*near, *two, *far),
-    )
-
-    every, columns, o_swap = barrier((every, columns, o_swap))
+    columns = put(
+        columns,
+        (w_far_up, w_far_down),
+        ((0, 0), (1, 0), (0, 1), (1, 1)),
+        jnp.stack([at_narrow[i] * 2 + half for i in (3, 7) for half in range(2)]),
+        16,
+        half_depth,
+    ).reshape(-1, w_qkv.shape[1])
+    for core, (two_up, two_down), (far_up, far_down) in (
+        (wide.at_core, (t_two_up, t_two_down), (t_far_up, t_far_down)),
+        (1 - wide.at_core, two, far),
+    ):
+        every = place(every, halves(two_up[:rows]), other, wide.ring(3), core)
+        every = place(every, halves(two_down[:rows]), other, wide.ring(1), core)
+        every = place(every, two_up[rows:], one, wide.ring(2), core, 0)
+        every = place(every, two_down[rows:], one, wide.ring(2), core, 1)
+        every = place(every, far_up, other, wide.ring(2), core, 0)
+        every = place(every, far_down, other, wide.ring(2), core, 1)
+    for block, pair, ring in zip(near, (one, one, one, other), (0, 3, 1, 0)):
+        every = place(every, halves(block), pair, wide.ring(ring), 1 - wide.at_core)
+    every = every.reshape(-1, normed.shape[1])
+    every, columns = barrier((every, columns))
     projected = jnp.dot(every, columns, preferred_element_type=jnp.float32).astype(jnp.bfloat16)
     packed = lax.all_to_all(
         projected.reshape(wide_count, rows, -1), "wide", split_axis=0, concat_axis=0, tiled=True
@@ -386,31 +381,25 @@
     a_up, a_down, a_swap = narrow.up(attended), narrow.down(attended), narrow.swap(attended)
     o_far_up = wide.up(o_two_up[:half_out])
     o_far_down = wide.down(o_two_down[half_out:out_rows])
-    o_near, o_rest = pack(
-        (w_out, o_up, o_down, o_swap, o_two_up, o_two_down, o_far_up, o_far_down),
+    (o_near,) = pack(
+        (w_out, o_up, o_down, o_swap, o_two_up, o_two_down),
         (
-            tuple((i, 0, out_rows) for i in range(4)),
-            ((4, 0, 3 * half_out), (5, 0, 3 * half_out), (6, 0, half_out), (7, 0, half_out)),
+            tuple((i, 0, out_rows) for i in range(4))
+            + tuple((i, 0, 3 * half_out) for i in (4, 5)),
         ),
         5,
         12 << 20,
     )
-    a_up, a_down, a_swap, o_far_up, o_far_down, o_near, o_rest = barrier(
-        (a_up, a_down, a_swap, o_far_up, o_far_down, o_near, o_rest)
-    )
-
-    b_up, b_down, b_swap = pack(
-        (a_up, a_down, a_swap),
-        (
-            ((2, half_rows, half_rows), (0, 0, half_rows)),
-            ((2, half_rows, half_rows), (1, half_rows, half_rows)),
-            ((0, 0, half_rows), (1, 0, half_rows)),
-        ),
-        4,
-    )
-    b_up, b_down, b_swap = narrow.up(b_up), narrow.down(b_down), narrow.swap(b_swap)
+    other_far = jnp.stack([o_far_up, o_far_down])
+    a_up, a_down, a_swap, o_far_up, o_far_down, o_near, other_far = barrier(
+        (a_up, a_down, a_swap, o_far_up, o_far_down, o_near, other_far)
+    )
+
+    b_up = narrow.up(jnp.concatenate([a_swap[half_rows:], a_up[:half_rows]]))
+    b_down = narrow.down(jnp.concatenate([a_swap[half_rows:], a_down[half_rows:]]))
+    b_swap = narrow.swap(jnp.concatenate([a_up[:half_rows], a_down[:half_rows]]))
     o_near = wide.cores(o_near)
-    o_rest = wide.cores(o_rest)
+    other_far = wide.cores(other_far).reshape(out_rows, -1)
     chips = tuple(
         (pair * 4 + wide.ring(ring)) * 2
         for ring, pair in (
@@ -435,8 +424,8 @@
     )
     every_w_out = put(
         every_w_out,
-        (o_near, o_rest),
-        tuple((0, i) for i in range(8)) + tuple((1, i) for i in (0, 1, 3, 4, 2, 5, 6, 7)),
+        (o_near, other_far),
+        tuple((0, i) for i in (0, 1, 2, 3, 4, 5, 6, 7, 8, 9, 11, 12, 10, 13)) + ((1, 0), (1, 1)),
         jnp.stack([(chip + 1 - wide.at_core) * 2 + half for chip in chips for half in range(2)]),
         wide_count * 2,
         half_out,

time: 232 us -> 222 us (0.957)
  local copies, waits for them, and re-layouts: 39.6 us -> 17.6 us
  waiting for transfers between devices: 60.3 us -> 75 us
  starting transfers between devices: 52.8 us -> 49 us
  Pallas kernels: 29.8 us -> 32.8 us
    ppermute x12, waiting for transfers between devices: 0.03 us -> 20.8 us  [down(): return lax.ppermute(block, self.axis, self.pairs(-1, 0, 0))]
    ppermute x12, waiting for transfers between devices: 36.5 us -> 17.8 us  [up(): return lax.ppermute(block, self.axis, self.pairs(1, 0, 0))]
    dynamic_update_slice x30 -> x20, local copies, waits for them, and re-layouts: 16.8 us -> 4.3 us  [place(): return lax.dynamic_update_slice(buffer, block.reshape(shape), start)]
    unnamed x58 -> x52, local copies, waits for them, and re-layouts: 10.9 us -> 1.89 us
    all_to_all x1, waiting for transfers between devices: 14 us -> 20.1 us  [shards(): lax.all_to_all(tokens, 'narrow', split_axis=0, concat_axis=1, tiled=True)]
    ppermute x6, waiting for transfers between devices: 8.39 us -> 14.4 us  [swap(): return lax.ppermute(block, self.axis, self.pairs(0, 1, 0))]
    ppermute x12, starting transfers between devices: 34.1 us -> 28.3 us  [down(): return lax.ppermute(block, self.axis, self.pairs(-1, 0, 0))]
    pallas_call x4 -> x6, Pallas kernels: 13.8 us -> 17.7 us  [put(): pl.pallas_call(functools.partial(put_kernel, sources, aliased), grid_spec...]
  transfers between devices with their start and end apart: 36 -> 36, of which waited for: 12 -> 17; matrix products, arithmetic and copies ran while one was open for 15% -> 12% of each run, Pallas kernels for 12% -> 14%
where the time goes in v1:
time: 222 us
  waiting for transfers between devices  75 us (34%)
  starting transfers between devices  49 us (22%)
  Pallas kernels  32.8 us (15%)
  blocking collectives  25.2 us (11%)
  local copies, waits for them, and re-layouts  17.6 us (8%)
  matrix products  17.5 us (8%)
  other arithmetic  3.99 us (2%)
    ppermute x12, starting transfers between devices, down(): return lax.ppermute(block, self.axis, self.pairs(-1, 0, 0))  28.3 us
    all_to_all x1, blocking collectives, shards(): lax.all_to_all(projected.reshape(wide_count, rows, -1), 'wide', split_axi...  25.2 us
    ppermute x12, waiting for transfers between devices, down(): return lax.ppermute(block, self.axis, self.pairs(-1, 0, 0))  20.8 us
    all_to_all x1, waiting for transfers between devices, shards(): lax.all_to_all(tokens, 'narrow', split_axis=0, concat_axis=1, tiled=True)  20.1 us
    ppermute x12, waiting for transfers between devices, up(): return lax.ppermute(block, self.axis, self.pairs(1, 0, 0))  17.8 us
    pallas_call x6, Pallas kernels, put(): pl.pallas_call(functools.partial(put_kernel, sources, aliased), grid_spec...  17.7 us
    ppermute x6, waiting for transfers between devices, swap(): return lax.ppermute(block, self.axis, self.pairs(0, 1, 0))  14.4 us
    pallas_call x1, Pallas kernels, attend(): pl.pallas_call(attend_kernel, grid_spec=pltpu.PrefetchScalarGridSpec(num_...  11.3 us
  transfers between devices with their start and end apart: 36, of which 17 were waited for; matrix products, arithmetic and copies ran while one was open for 12% of the time, Pallas kernels for 14%

profile of v1, /device:TPU:0, one launch (start us, length us, event | category | flops | bytes accessed | tf_op | source)
XLA Modules:
  0.0 222.0 jit_solution(933930406899870415)
XLA Ops:
  0.0 3.1 %collective-permute-start.1 = (bf16[512,640]{1,0:T(8,128)(2,1)}, bf16[512,640]{1,0:T(8,128)(2,1)S(1)}, u32[]{:S(2)}, u32[]{:S(2)}) collective-permute-start(bf16[512,640]{1,0:T(8,128)(2,1)} %refs_0_.3), channel_id=1, source_target_pairs={{0,48},{8,56},{16,0},{24,8},{32,16},{40,24},{48,32},{56,40},{64,11... | collective-permute-start | bytes 1966088 | tf_op jit(solution)/shard_map/ppermute | solution.py:183
  3.1 1.9 collective-permute-start.3
  5.0 1.5 collective-permute-start.2
  6.5 2.1 collective-permute-start.4
  8.6 3.5 %all-to-all-start = ((bf16[8,64,640]{2,1,0:T(8,128)(2,1)}), bf16[8,64,640]{2,1,0:T(8,128)(2,1)S(1)}, u32[]{:S(2)}, u32[]{:S(2)}) async-start(bf16[8,64,640]{2,1,0:T(8,128)(2,1)} %bitcast.146), calls=%async_computation | async-start | bytes 1310720 | tf_op jit(solution)/shard_map/all_to_all | solution.py:282
  12.2 0.7 add_convert_fusion
  13.5 20.1 %all-to-all-done = bf16[8,64,640]{2,1,0:T(8,128)(2,1)S(1)} async-done(((bf16[8,64,640]{2,1,0:T(8,128)(2,1)}), bf16[8,64,640]{2,1,0:T(8,128)(2,1)S(1)}, u32[]{:S(2)}, u32[]{:S(2)}) %all-to-all-start) | async-done | bytes 655392 | tf_op jit(solution)/shard_map/all_to_all | solution.py:282
  34.0 2.9 %collective-permute-start.6 = (bf16[640,640]{1,0:T(8,128)(2,1)}, bf16[640,640]{1,0:T(8,128)(2,1)S(1)}, u32[]{:S(2)}, u32[]{:S(2)}) collective-permute-start(bf16[640,640]{1,0:T(8,128)(2,1)} %collective-permute-done.2.refs_3_), channel_id=1, source_target_pairs={{0,6},{1,7},{2,0},{3,1},{4,2},{5,3},{6,4},{7,5},{8,14},{9,15},{10,... | collective-permute-start | bytes 2457608 | tf_op jit(solution)/shard_map/ppermute | solution.py:183
  37.2 2.8 %collective-permute-start.9 = (bf16[64,5120]{1,0:T(8,128)(2,1)S(1)}, bf16[64,5120]{1,0:T(8,128)(2,1)S(1)}, u32[]{:S(2)}, u32[]{:S(2)}) collective-permute-start(bf16[64,5120]{1,0:T(8,128)(2,1)S(1)} %multiply_convert_fusion), channel_id=1, source_target_pairs={{0,64},{8,72},{16,80},{24,88},{32,96},{40,104},{48,112},{56,120},{... | collective-permute-start | bytes 1966088 | tf_op jit(solution)/shard_map/ppermute | solution.py:186
  40.0 3.0 %collective-permute-start.8 = (bf16[64,5120]{1,0:T(8,128)(2,1)S(1)}, bf16[64,5120]{1,0:T(8,128)(2,1)S(1)}, u32[]{:S(2)}, u32[]{:S(2)}) collective-permute-start(bf16[64,5120]{1,0:T(8,128)(2,1)S(1)} %multiply_convert_fusion), channel_id=1, source_target_pairs={{0,48},{8,56},{16,0},{24,8},{32,16},{40,24},{48,32},{56,40},{64,11... | collective-permute-start | bytes 1966088 | tf_op jit(solution)/shard_map/ppermute | solution.py:183
  43.0 1.1 slice.93
  44.1 5.3 %broadcast_in_dim.9 = bf16[2,4,2,2,32,5120]{5,4,3,2,1,0:T(8,128)(2,1)} broadcast(bf16[]{:T(256)} %constant.196.clone.1), dimensions={} | broadcast | bytes 10485762 | tf_op jit(solution)/shard_map/broadcast_in_dim | solution.py:297
  49.4 0.9 constant_dynamic-update-slice_fusion.11
  50.4 2.2 collective-permute-done.9
  52.6 3.0 %collective-permute-start.14 = (bf16[512,640]{1,0:T(8,128)(2,1)S(1)}, bf16[512,640]{1,0:T(8,128)(2,1)S(1)}, u32[]{:S(2)}, u32[]{:S(2)}) collective-permute-start(bf16[512,640]{1,0:T(8,128)(2,1)S(1)} %copy-done.3), channel_id=1, source_target_pairs={{0,64},{8,72},{16,80},{24,88},{32,96},{40,104},{48,112},{56,120},{... | collective-permute-start | bytes 1966088 | tf_op jit(solution)/shard_map/ppermute | solution.py:186
  55.6 1.8 collective-permute-done.7
  57.7 2.8 %collective-permute-start.11 = (bf16[640,640]{1,0:T(8,128)(2,1)S(1)}, bf16[640,640]{1,0:T(8,128)(2,1)S(1)}, u32[]{:S(2)}, u32[]{:S(2)}) collective-permute-start(bf16[640,640]{1,0:T(8,128)(2,1)S(1)} %pad_maximum_fusion.10), channel_id=1, source_target_pairs={{0,6},{1,7},{2,0},{3,1},{4,2},{5,3},{6,4},{7,5},{8,14},{9,15},{10,... | collective-permute-start | bytes 2457608 | tf_op jit(solution)/shard_map/ppermute | solution.py:183
  60.9 1.0 collective-permute-start.13
  61.9 1.1 collective-permute-start.12
  63.0 0.9 constant_dynamic-update-slice_fusion.10
  63.9 0.9 constant_dynamic-update-slice_fusion.9
  64.8 0.9 constant_dynamic-update-slice_fusion.8
  65.7 3.4 %put.6.refs_0_ = bf16[16,320,640]{2,1,0:T(8,128)(2,1)S(1)} custom-call(s32[12]{0:T(128)S(1)} %stack.243.places, bf16[640,640]{1,0:T(8,128)(2,1)S(1)} %copy-done.13, bf16[640,640]{1,0:T(8,128)(2,1)S(1)} %collective-permute-done.3.refs_1_, bf16[640,640]{1,0:T(8,128)(2,1)} %collective-permute-done.4.refs_2_, bf16[640,640]{1,0:T(8,128)(2,1)} %collective-permute-done.2.refs_3_, ...), custom_call_target="tpu_custom_call" | custom-call | bytes 320 | tf_op jit(solution)/shard_map/put/pallas_call | solution.py:220
  69.5 4.1 %collective-permute-done.11.refs_2_ = bf16[640,640]{1,0:T(8,128)(2,1)S(1)} collective-permute-done((bf16[640,640]{1,0:T(8,128)(2,1)S(1)}, bf16[640,640]{1,0:T(8,128)(2,1)S(1)}, u32[]{:S(2)}, u32[]{:S(2)}) %collective-permute-start.11) | collective-permute-done | bytes 819232 | tf_op jit(solution)/shard_map/ppermute | solution.py:183
  73.5 3.4 %collective-permute-done.10.refs_1_ = bf16[640,640]{1,0:T(8,128)(2,1)S(1)} collective-permute-done((bf16[640,640]{1,0:T(8,128)(2,1)S(1)}, bf16[640,640]{1,0:T(8,128)(2,1)S(1)}, u32[]{:S(2)}, u32[]{:S(2)}) %collective-permute-start.10) | collective-permute-done | bytes 819232 | tf_op jit(solution)/shard_map/ppermute | solution.py:180
  76.9 3.7 %collective-permute-done.13 = bf16[96,5120]{1,0:T(8,128)(2,1)S(1)} collective-permute-done((bf16[96,5120]{1,0:T(8,128)(2,1)S(1)}, bf16[96,5120]{1,0:T(8,128)(2,1)S(1)}, u32[]{:S(2)}, u32[]{:S(2)}) %collective-permute-start.13) | collective-permute-done | bytes 983072 | tf_op jit(solution)/shard_map/ppermute | solution.py:183
  80.7 2.7 %collective-permute-done.12 = bf16[96,5120]{1,0:T(8,128)(2,1)S(1)} collective-permute-done((bf16[96,5120]{1,0:T(8,128)(2,1)S(1)}, bf16[96,5120]{1,0:T(8,128)(2,1)S(1)}, u32[]{:S(2)}, u32[]{:S(2)}) %collective-permute-start.12) | collective-permute-done | bytes 983072 | tf_op jit(solution)/shard_map/ppermute | solution.py:180
  83.8 1.7 collective-permute-start.15
  86.6 0.8 put.7
  87.4 3.2 %collective-permute-done.16 = bf16[32,5120]{1,0:T(8,128)(2,1)S(1)} collective-permute-done((bf16[32,5120]{1,0:T(8,128)(2,1)S(1)}, bf16[32,5120]{1,0:T(8,128)(2,1)S(1)}, u32[]{:S(2)}, u32[]{:S(2)}) %collective-permute-start.16) | collective-permute-done | bytes 327712 | tf_op jit(solution)/shard_map/ppermute | solution.py:183
  90.6 1.5 collective-permute-done.15
  92.9 1.9 collective-permute-done.18
  95.3 8.3 %convolution_convert_fusion = bf16[1024,640]{1,0:T(8,128)(2,1)S(1)} fusion(bf16[1024,5120]{1,0:T(8,128)(2,1)S(1)} %bitcast.123, bf16[5120,640]{1,0:T(8,128)(2,1)S(1)} %bitcast.115), kind=kOutput, calls=%fused_computation.18 | convolution fusion | flops 6711541760 | bytes 18350080 | tf_op jit(solution)/shard_map/dot_general | solution.py:356
  103.6 25.2 %all_to_all.18.packed = bf16[16,64,640]{2,1,0:T(8,128)(2,1)S(1)} all-to-all(bf16[16,64,640]{2,1,0:T(8,128)(2,1)S(1)} %bitcast.143), channel_id=1, replica_groups=mesh['wide'=16,'narrow'=8] {'wide'}, dimensions={0} | all-to-all | bytes 2621440 | tf_op jit(solution)/shard_map/all_to_all | solution.py:357
  129.1 1.1 collective-permute-start.25
  130.2 1.0 collective-permute-start.23
  131.2 11.3 %attend.1 = bf16[64,8192]{1,0:T(8,128)(2,1)S(1)} custom-call(s32[4]{0:T(128)S(1)} %copy-done.14, s32[4]{0:T(128)S(1)} %copy-done.15, bf16[16,64,640]{2,1,0:T(8,128)(2,1)S(1)} %all_to_all.18.packed, f32[64,128]{1,0:T(8,128)S(1)} %broadcast_in_dim.8.inverse, f32[64,128]{1,0:T(8,128)S(1)} %get-tuple-element.78.cosine, f32[64,128]{1,0:T(8,128)S(1)} %get-tuple-element.79.sine, ...), custom_call_target="tpu_custom_call" | custom-call | flops 570425344 | bytes 6553600 | tf_op jit(solution)/shard_map/attend/pallas_call | solution.py:121
  142.6 2.5 %collective-permute-start.21 = (bf16[64,8192]{1,0:T(8,128)(2,1)S(1)}, bf16[64,8192]{1,0:T(8,128)(2,1)}, u32[]{:S(2)}, u32[]{:S(2)}) collective-permute-start(bf16[64,8192]{1,0:T(8,128)(2,1)S(1)} %attend.1), channel_id=1, source_target_pairs={{0,6},{1,7},{2,0},{3,1},{4,2},{5,3},{6,4},{7,5},{8,14},{9,15},{10,... | collective-permute-start | bytes 3145736 | tf_op jit(solution)/shard_map/ppermute | solution.py:183
  145.1 7.3 %collective-permute-done.25.refs_5_ = bf16[768,640]{1,0:T(8,128)(2,1)S(1)} collective-permute-done((bf16[768,640]{1,0:T(8,128)(2,1)S(1)}, bf16[768,640]{1,0:T(8,128)(2,1)S(1)}, u32[]{:S(2)}, u32[]{:S(2)}) %collective-permute-start.25) | collective-permute-done | bytes 983072 | tf_op jit(solution)/shard_map/ppermute | solution.py:183
  152.4 3.0 %collective-permute-start.26 = (bf16[256,640]{1,0:T(8,128)(2,1)S(1)}, bf16[256,640]{1,0:T(8,128)(2,1)S(1)}, u32[]{:S(2)}, u32[]{:S(2)}) collective-permute-start(bf16[256,640]{1,0:T(8,128)(2,1)S(1)} %slice.123), channel_id=1, source_target_pairs={{0,48},{8,56},{16,0},{24,8},{32,16},{40,24},{48,32},{56,40},{64,11... | collective-permute-start | bytes 983048 | tf_op jit(solution)/shard_map/ppermute | solution.py:183
  155.8 3.8 %pack.1 = bf16[3584,640]{1,0:T(8,128)(2,1)} custom-call(bf16[512,640]{1,0:T(8,128)(2,1)S(1)} %copy-done.3, bf16[512,640]{1,0:T(8,128)(2,1)S(1)} %copy-done.1, bf16[512,640]{1,0:T(8,128)(2,1)S(1)} %collective-permute-done.1.refs_2_, bf16[512,640]{1,0:T(8,128)(2,1)S(1)} %collective-permute-done.14.refs_3_, ...), custom_call_target="tpu_custom_call" | custom-call | bytes 3584 | tf_op jit(solution)/shard_map/pack/pallas_call | solution.py:249
  159.6 2.5 %collective-permute-done.26.refs_7_ = bf16[256,640]{1,0:T(8,128)(2,1)S(1)} collective-permute-done((bf16[256,640]{1,0:T(8,128)(2,1)S(1)}, bf16[256,640]{1,0:T(8,128)(2,1)S(1)}, u32[]{:S(2)}, u32[]{:S(2)}) %collective-permute-start.26) | collective-permute-done | bytes 327712 | tf_op jit(solution)/shard_map/ppermute | solution.py:183
  162.1 3.7 %collective-permute-done.24.refs_6_ = bf16[256,640]{1,0:T(8,128)(2,1)S(1)} collective-permute-done((bf16[256,640]{1,0:T(8,128)(2,1)S(1)}, bf16[256,640]{1,0:T(8,128)(2,1)S(1)}, u32[]{:S(2)}, u32[]{:S(2)}) %collective-permute-start.24) | collective-permute-done | bytes 327712 | tf_op jit(solution)/shard_map/ppermute | solution.py:180
  165.8 1.0 pad_maximum_fusion.12
  166.8 0.7 copy-done.7
  167.5 2.3 %collective-permute-done.20 = bf16[64,8192]{1,0:T(8,128)(2,1)S(1)} collective-permute-done((bf16[64,8192]{1,0:T(8,128)(2,1)S(1)}, bf16[64,8192]{1,0:T(8,128)(2,1)S(1)}, u32[]{:S(2)}, u32[]{:S(2)}) %collective-permute-start.20) | collective-permute-done | bytes 1048608 | tf_op jit(solution)/shard_map/ppermute | solution.py:180
  169.8 1.0 copy-done.20
  171.4 1.2 slice.111
  172.5 1.1 slice.112
  174.2 1.3 fusion.36
  175.8 1.5 collective-permute-start.29
  177.3 3.2 %collective-permute-start.28 = (bf16[64,8192]{1,0:T(8,128)(2,1)S(1)}, bf16[64,8192]{1,0:T(8,128)(2,1)S(1)}, u32[]{:S(2)}, u32[]{:S(2)}) collective-permute-start(bf16[64,8192]{1,0:T(8,128)(2,1)S(1)} %get-tuple-element.117), channel_id=1, source_target_pairs={{0,6},{1,7},{2,0},{3,1},{4,2},{5,3},{6,4},{7,5},{8,14},{9,15},{10,... | collective-permute-start | bytes 3145736 | tf_op jit(solution)/shard_map/ppermute | solution.py:183
  180.6 2.3 %put.8.refs_0_ = bf16[32,256,640]{2,1,0:T(8,128)(2,1)S(1)} custom-call(s32[16]{0:T(128)S(1)} %stack.287.places, bf16[512,640]{1,0:T(8,128)(2,1)S(1)} %copy-done.4, bf16[512,640]{1,0:T(8,128)(2,1)S(1)} %copy-done.2, bf16[512,640]{1,0:T(8,128)(2,1)S(1)} %collective-permute-done.1.refs_2_, bf16[512,640]{1,0:T(8,128)(2,1)S(1)} %collective-permute-done.14.refs_3_, ...), custom_call_target="tpu_custom_call" | custom-call | bytes 256 | tf_op jit(solution)/shard_map/put/pallas_call | solution.py:220
  182.9 4.9 %put.9 = bf16[32,256,640]{2,1,0:T(8,128)(2,1)S(1)} custom-call(s32[16]{0:T(128)S(1)} %stack.270.places, bf16[32,256,640]{2,1,0:T(8,128)(2,1)S(1)} %put.8.refs_0_, bf16[3584,640]{1,0:T(8,128)(2,1)} %collective-permute-done.30.refs_1_, bf16[512,640]{1,0:T(8,128)(2,1)S(1)} %bitcast.118), custom_call_target="tpu_custom_call", output_to_operand_aliasing={{}: (1, {})} | custom-call | bytes 256 | tf_op jit(solution)/shard_map/put/pallas_call | solution.py:220
  187.9 4.7 %fusion.15.refs_0_ = bf16[256,640]{1,0:T(8,128)(2,1)S(1)} fusion(bf16[8192,640]{1,0:T(8,128)(2,1)S(1)} %bitcast.112, bf16[64,8192]{1,0:T(8,128)(2,1)} %collective-permute-done.21, bf16[64,8192]{1,0:T(8,128)(2,1)S(1)} %copy-done.21, bf16[64,8192]{1,0:T(8,128)(2,1)S(1)} %copy-done.19, bf16[64,8192]{1,0:T(8,128)(2,1)S(1)} %copy-done.12), kind=kOutput, calls=%fused_computation.21 | convolution fusion | flops 2701295616 | bytes 15007744 | tf_op jit(solution)/shard_map/dot_general | solution.py:435
  192.6 8.4 %collective-permute-done.29 = bf16[64,8192]{1,0:T(8,128)(2,1)S(1)} collective-permute-done((bf16[64,8192]{1,0:T(8,128)(2,1)S(1)}, bf16[64,8192]{1,0:T(8,128)(2,1)S(1)}, u32[]{:S(2)}, u32[]{:S(2)}) %collective-permute-start.29) | collective-permute-done | bytes 1048608 | tf_op jit(solution)/shard_map/ppermute | solution.py:186
  201.0 2.4 %collective-permute-done.27 = bf16[64,8192]{1,0:T(8,128)(2,1)S(1)} collective-permute-done((bf16[64,8192]{1,0:T(8,128)(2,1)S(1)}, bf16[64,8192]{1,0:T(8,128)(2,1)S(1)}, u32[]{:S(2)}, u32[]{:S(2)}) %collective-permute-start.27) | collective-permute-done | bytes 1048608 | tf_op jit(solution)/shard_map/ppermute | solution.py:180
  203.5 3.2 %collective-permute-start.33 = (bf16[16,8192]{1,0:T(8,128)(2,1)S(1)}, bf16[16,8192]{1,0:T(8,128)(2,1)S(1)}, u32[]{:S(2)}, u32[]{:S(2)}) collective-permute-start(bf16[16,8192]{1,0:T(8,128)(2,1)S(1)} %slice.116), channel_id=1, source_target_pairs={{0,6},{1,7},{2,0},{3,1},{4,2},{5,3},{6,4},{7,5},{8,14},{9,15},{10,... | collective-permute-start | bytes 786440 | tf_op jit(solution)/shard_map/ppermute | solution.py:183
  206.8 0.6 collective-permute-start.34
  207.4 2.6 %fusion.18.refs_1_ = bf16[192,640]{1,0:T(8,128)(2,1)S(1)} fusion(bf16[8192,640]{1,0:T(8,128)(2,1)S(1)} %bitcast.113, bf16[64,8192]{1,0:T(8,128)(2,1)S(1)} %collective-permute-done.28, bf16[64,8192]{1,0:T(8,128)(2,1)S(1)} %collective-permute-done.27, bf16[64,8192]{1,0:T(8,128)(2,1)S(1)} %collective-permute-done.29), kind=kOutput, calls=%fused_computation.22 | convolution fusion | flops 2022825984 | bytes 13877248 | tf_op jit(solution)/shard_map/dot_general | solution.py:435
  210.0 5.1 %put.10.refs_0_ = bf16[16,32,640]{2,1,0:T(8,128)(2,1)} custom-call(s32[14]{0:T(128)S(1)} %stack.237.places, bf16[256,640]{1,0:T(8,128)(2,1)S(1)} %fusion.15.refs_0_, bf16[192,640]{1,0:T(8,128)(2,1)S(1)} %fusion.18.refs_1_), custom_call_target="tpu_custom_call" | custom-call | bytes 32 | tf_op jit(solution)/shard_map/put/pallas_call | solution.py:220
  215.1 3.8 %collective-permute-done.34 = bf16[32,8192]{1,0:T(8,128)(2,1)S(1)} collective-permute-done((bf16[32,8192]{1,0:T(8,128)(2,1)S(1)}, bf16[32,8192]{1,0:T(8,128)(2,1)S(1)}, u32[]{:S(2)}, u32[]{:S(2)}) %collective-permute-start.34) | collective-permute-done | bytes 524320 | tf_op jit(solution)/shard_map/ppermute | solution.py:186
  218.9 1.9 convolution_convert_fusion.1.refs_1_
  220.8 1.2 put.11
  (143 shorter events, 6.9 us)
Async XLA Ops:
  0.0 33.9 %copy-start.22 = (f32[5120]{0:T(1024)S(1)}, f32[5120]{0:T(1024)}, u32[]{:S(2)}) copy-start(f32[5120]{0:T(1024)} %param.11) | copy-start | bytes 61444
  0.0 34.0 %collective-permute-start.1 = (bf16[512,640]{1,0:T(8,128)(2,1)}, bf16[512,640]{1,0:T(8,128)(2,1)S(1)}, u32[]{:S(2)}, u32[]{:S(2)}) collective-permute-start(bf16[512,640]{1,0:T(8,128)(2,1)} %refs_0_.3), channel_id=1, source_target_pairs={{0,48},{8,56},{16,0},{24,8},{32,16},{40,24},{48,32},{56,40},{64,11... | collective-permute-start | bytes 1966088 | tf_op jit(solution)/shard_map/ppermute | solution.py:183
  3.1 30.9 %collective-permute-start = (bf16[512,640]{1,0:T(8,128)(2,1)}, bf16[512,640]{1,0:T(8,128)(2,1)S(1)}, u32[]{:S(2)}, u32[]{:S(2)}) collective-permute-start(bf16[512,640]{1,0:T(8,128)(2,1)} %refs_0_.3), channel_id=1, source_target_pairs={{0,16},{8,24},{16,32},{24,40},{32,48},{40,56},{48,0},{56,8},{64,80... | collective-permute-start | bytes 1966088 | tf_op jit(solution)/shard_map/ppermute | solution.py:180
  3.1 30.9 %collective-permute-start.3 = (bf16[640,640]{1,0:T(8,128)(2,1)}, bf16[640,640]{1,0:T(8,128)(2,1)S(1)}, u32[]{:S(2)}, u32[]{:S(2)}) collective-permute-start(bf16[640,640]{1,0:T(8,128)(2,1)} %refs_0_.1), channel_id=1, source_target_pairs={{0,2},{1,3},{2,4},{3,5},{4,6},{5,7},{6,0},{7,1},{8,10},{9,11},{10,... | collective-permute-start | bytes 2457608 | tf_op jit(solution)/shard_map/ppermute | solution.py:180
  5.0 29.0 %collective-permute-start.2 = (bf16[640,640]{1,0:T(8,128)(2,1)}, bf16[640,640]{1,0:T(8,128)(2,1)}, u32[]{:S(2)}, u32[]{:S(2)}) collective-permute-start(bf16[640,640]{1,0:T(8,128)(2,1)} %refs_0_.1), channel_id=1, source_target_pairs={{0,1},{1,0},{2,3},{3,2},{4,5},{5,4},{6,7},{7,6},{8,9},{9,8},{10,11... | collective-permute-start | bytes 2457608 | tf_op jit(solution)/shard_map/ppermute | solution.py:186
  6.5 27.5 %collective-permute-start.4 = (bf16[640,640]{1,0:T(8,128)(2,1)}, bf16[640,640]{1,0:T(8,128)(2,1)}, u32[]{:S(2)}, u32[]{:S(2)}) collective-permute-start(bf16[640,640]{1,0:T(8,128)(2,1)} %refs_0_.1), channel_id=1, source_target_pairs={{0,6},{1,7},{2,0},{3,1},{4,2},{5,3},{6,4},{7,5},{8,14},{9,15},{10,... | collective-permute-start | bytes 2457608 | tf_op jit(solution)/shard_map/ppermute | solution.py:183
  8.6 25.0 %all-to-all-start = ((bf16[8,64,640]{2,1,0:T(8,128)(2,1)}), bf16[8,64,640]{2,1,0:T(8,128)(2,1)S(1)}, u32[]{:S(2)}, u32[]{:S(2)}) async-start(bf16[8,64,640]{2,1,0:T(8,128)(2,1)} %bitcast.146), calls=%async_computation | async-start | bytes 1310720 | tf_op jit(solution)/shard_map/all_to_all | solution.py:282
  34.0 94.9 %copy-start = (bf16[512,640]{1,0:T(8,128)(2,1)}, bf16[512,640]{1,0:T(8,128)(2,1)S(1)}, u32[]{:S(2)}) copy-start(bf16[512,640]{1,0:T(8,128)(2,1)S(1)} %collective-permute-done.refs_1_) | copy-start | bytes 1966084
  34.0 23.3 %collective-permute-start.6 = (bf16[640,640]{1,0:T(8,128)(2,1)}, bf16[640,640]{1,0:T(8,128)(2,1)S(1)}, u32[]{:S(2)}, u32[]{:S(2)}) collective-permute-start(bf16[640,640]{1,0:T(8,128)(2,1)} %collective-permute-done.2.refs_3_), channel_id=1, source_target_pairs={{0,6},{1,7},{2,0},{3,1},{4,2},{5,3},{6,4},{7,5},{8,14},{9,15},{10,... | collective-permute-start | bytes 2457608 | tf_op jit(solution)/shard_map/ppermute | solution.py:183
  36.9 20.4 %collective-permute-start.5 = (bf16[640,640]{1,0:T(8,128)(2,1)}, bf16[640,640]{1,0:T(8,128)(2,1)S(1)}, u32[]{:S(2)}, u32[]{:S(2)}) collective-permute-start(bf16[640,640]{1,0:T(8,128)(2,1)} %collective-permute-done.2.refs_3_), channel_id=1, source_target_pairs={{0,2},{1,3},{2,4},{3,5},{4,6},{5,7},{6,0},{7,1},{8,10},{9,11},{10,... | collective-permute-start | bytes 2457608 | tf_op jit(solution)/shard_map/ppermute | solution.py:180
  37.2 15.4 %collective-permute-start.9 = (bf16[64,5120]{1,0:T(8,128)(2,1)S(1)}, bf16[64,5120]{1,0:T(8,128)(2,1)S(1)}, u32[]{:S(2)}, u32[]{:S(2)}) collective-permute-start(bf16[64,5120]{1,0:T(8,128)(2,1)S(1)} %multiply_convert_fusion), channel_id=1, source_target_pairs={{0,64},{8,72},{16,80},{24,88},{32,96},{40,104},{48,112},{56,120},{... | collective-permute-start | bytes 1966088 | tf_op jit(solution)/shard_map/ppermute | solution.py:186
  40.0 15.6 %collective-permute-start.8 = (bf16[64,5120]{1,0:T(8,128)(2,1)S(1)}, bf16[64,5120]{1,0:T(8,128)(2,1)S(1)}, u32[]{:S(2)}, u32[]{:S(2)}) collective-permute-start(bf16[64,5120]{1,0:T(8,128)(2,1)S(1)} %multiply_convert_fusion), channel_id=1, source_target_pairs={{0,48},{8,56},{16,0},{24,8},{32,16},{40,24},{48,32},{56,40},{64,11... | collective-permute-start | bytes 1966088 | tf_op jit(solution)/shard_map/ppermute | solution.py:183
  42.9 14.4 %collective-permute-start.7 = (bf16[64,5120]{1,0:T(8,128)(2,1)S(1)}, bf16[64,5120]{1,0:T(8,128)(2,1)S(1)}, u32[]{:S(2)}, u32[]{:S(2)}) collective-permute-start(bf16[64,5120]{1,0:T(8,128)(2,1)S(1)} %multiply_convert_fusion), channel_id=1, source_target_pairs={{0,16},{8,24},{16,32},{24,40},{32,48},{40,56},{48,0},{56,8},{64,80... | collective-permute-start | bytes 1966088 | tf_op jit(solution)/shard_map/ppermute | solution.py:180
  42.9 9.6 %copy-start.3 = (bf16[512,640]{1,0:T(8,128)(2,1)S(1)}, bf16[512,640]{1,0:T(8,128)(2,1)}, u32[]{:S(2)}) copy-start(bf16[512,640]{1,0:T(8,128)(2,1)} %refs_0_.3) | copy-start | bytes 1966084
  52.6 16.9 %collective-permute-start.14 = (bf16[512,640]{1,0:T(8,128)(2,1)S(1)}, bf16[512,640]{1,0:T(8,128)(2,1)S(1)}, u32[]{:S(2)}, u32[]{:S(2)}) collective-permute-start(bf16[512,640]{1,0:T(8,128)(2,1)S(1)} %copy-done.3), channel_id=1, source_target_pairs={{0,64},{8,72},{16,80},{24,88},{32,96},{40,104},{48,112},{56,120},{... | collective-permute-start | bytes 1966088 | tf_op jit(solution)/shard_map/ppermute | solution.py:186
  57.5 8.2 %copy-start.13 = (bf16[640,640]{1,0:T(8,128)(2,1)S(1)}, bf16[640,640]{1,0:T(8,128)(2,1)}, u32[]{:S(2)}) copy-start(bf16[640,640]{1,0:T(8,128)(2,1)} %refs_0_.1) | copy-start | bytes 2457604
  57.7 15.9 %collective-permute-start.11 = (bf16[640,640]{1,0:T(8,128)(2,1)S(1)}, bf16[640,640]{1,0:T(8,128)(2,1)S(1)}, u32[]{:S(2)}, u32[]{:S(2)}) collective-permute-start(bf16[640,640]{1,0:T(8,128)(2,1)S(1)} %pad_maximum_fusion.10), channel_id=1, source_target_pairs={{0,6},{1,7},{2,0},{3,1},{4,2},{5,3},{6,4},{7,5},{8,14},{9,15},{10,... | collective-permute-start | bytes 2457608 | tf_op jit(solution)/shard_map/ppermute | solution.py:183
  60.6 16.3 %collective-permute-start.10 = (bf16[640,640]{1,0:T(8,128)(2,1)S(1)}, bf16[640,640]{1,0:T(8,128)(2,1)S(1)}, u32[]{:S(2)}, u32[]{:S(2)}) collective-permute-start(bf16[640,640]{1,0:T(8,128)(2,1)S(1)} %pad_maximum_fusion.9), channel_id=1, source_target_pairs={{0,2},{1,3},{2,4},{3,5},{4,6},{5,7},{6,0},{7,1},{8,10},{9,11},{10,... | collective-permute-start | bytes 2457608 | tf_op jit(solution)/shard_map/ppermute | solution.py:180
  60.9 19.8 %collective-permute-start.13 = (bf16[96,5120]{1,0:T(8,128)(2,1)S(1)}, bf16[96,5120]{1,0:T(8,128)(2,1)S(1)}, u32[]{:S(2)}, u32[]{:S(2)}) collective-permute-start(bf16[96,5120]{1,0:T(8,128)(2,1)S(1)} %get-tuple-element.113), channel_id=1, source_target_pairs={{0,48},{8,56},{16,0},{24,8},{32,16},{40,24},{48,32},{56,40},{64,11... | collective-permute-start | bytes 2949128 | tf_op jit(solution)/shard_map/ppermute | solution.py:183
  61.9 21.4 %collective-permute-start.12 = (bf16[96,5120]{1,0:T(8,128)(2,1)S(1)}, bf16[96,5120]{1,0:T(8,128)(2,1)S(1)}, u32[]{:S(2)}, u32[]{:S(2)}) collective-permute-start(bf16[96,5120]{1,0:T(8,128)(2,1)S(1)} %get-tuple-element.114), channel_id=1, source_target_pairs={{0,16},{8,24},{16,32},{24,40},{32,48},{40,56},{48,0},{56,8},{64,80... | collective-permute-start | bytes 2949128 | tf_op jit(solution)/shard_map/ppermute | solution.py:180
  65.7 19.9 %slice-start = ((s8[10485760]{0:T(1024)(128)(4,1)}), s8[4194304]{0:T(1024)(128)(4,1)S(1)}, s32[]{:S(2)}) async-start(s8[10485760]{0:T(1024)(128)(4,1)} %bitcast.121), calls=%async_computation.2 | async-start | bytes 8388608
  65.7 19.9 %slice-start.1 = ((s8[10485760]{0:T(1024)(128)(4,1)}), s8[4194304]{0:T(1024)(128)(4,1)S(1)}, s32[]{:S(2)}) async-start(s8[10485760]{0:T(1024)(128)(4,1)} %bitcast.121), calls=%async_computation.3 | async-start | bytes 8388608
  69.1 16.5 %slice-start.2 = ((s8[10485760]{0:T(1024)(128)(4,1)}), s8[2097152]{0:T(1024)(128)(4,1)S(1)}, s32[]{:S(2)}) async-start(s8[10485760]{0:T(1024)(128)(4,1)} %bitcast.121), calls=%async_computation.4 | async-start | bytes 4194304
  83.5 7.1 %collective-permute-start.16 = (bf16[32,5120]{1,0:T(8,128)(2,1)S(1)}, bf16[32,5120]{1,0:T(8,128)(2,1)S(1)}, u32[]{:S(2)}, u32[]{:S(2)}) collective-permute-start(bf16[32,5120]{1,0:T(8,128)(2,1)S(1)} %slice.102), channel_id=1, source_target_pairs={{0,48},{8,56},{16,0},{24,8},{32,16},{40,24},{48,32},{56,40},{64,11... | collective-permute-start | bytes 983048 | tf_op jit(solution)/shard_map/ppermute | solution.py:183
  83.8 8.3 %collective-permute-start.15 = (bf16[32,5120]{1,0:T(8,128)(2,1)S(1)}, bf16[32,5120]{1,0:T(8,128)(2,1)S(1)}, u32[]{:S(2)}, u32[]{:S(2)}) collective-permute-start(bf16[32,5120]{1,0:T(8,128)(2,1)S(1)} %slice.101), channel_id=1, source_target_pairs={{0,16},{8,24},{16,32},{24,40},{32,48},{40,56},{48,0},{56,8},{64,80... | collective-permute-start | bytes 983048 | tf_op jit(solution)/shard_map/ppermute | solution.py:180
  86.0 6.6 %collective-permute-start.17 = (bf16[2,96,5120]{2,1,0:T(8,128)(2,1)S(1)}, bf16[2,96,5120]{2,1,0:T(8,128)(2,1)S(1)}, u32[]{:S(2)}, u32[]{:S(2)}) collective-permute-start(bf16[2,96,5120]{2,1,0:T(8,128)(2,1)S(1)} %pad_maximum_fusion.1), channel_id=1, source_target_pairs={{0,8},{8,0},{16,24},{24,16},{32,40},{40,32},{48,56},{56,48},{64,72... | collective-permute-start | bytes 5898248 | tf_op jit(solution)/shard_map/ppermute | solution.py:189
  86.1 8.7 %collective-permute-start.19 = (bf16[4,64,5120]{2,1,0:T(8,128)(2,1)S(1)}, bf16[4,64,5120]{2,1,0:T(8,128)(2,1)S(1)}, u32[]{:S(2)}, u32[]{:S(2)}) collective-permute-start(bf16[4,64,5120]{2,1,0:T(8,128)(2,1)S(1)} %pad_maximum_fusion), channel_id=1, source_target_pairs={{0,8},{8,0},{16,24},{24,16},{32,40},{40,32},{48,56},{56,48},{64,72... | collective-permute-start | bytes 7864328 | tf_op jit(solution)/shard_map/ppermute | solution.py:189
  92.2 2.5 %collective-permute-start.18 = (bf16[2,32,5120]{2,1,0:T(8,128)(2,1)S(1)}, bf16[2,32,5120]{2,1,0:T(8,128)(2,1)S(1)}, u32[]{:S(2)}, u32[]{:S(2)}) collective-permute-start(bf16[2,32,5120]{2,1,0:T(8,128)(2,1)S(1)} %pad_maximum_fusion.11), channel_id=1, source_target_pairs={{0,8},{8,0},{16,24},{24,16},{32,40},{40,32},{48,56},{56,48},{64,72... | collective-permute-start | bytes 1966088 | tf_op jit(solution)/shard_map/ppermute | solution.py:189
  103.6 27.6 %copy-start.5 = (bf16[4,256,1024]{2,1,0:T(8,128)(2,1)S(1)}, bf16[4,256,1024]{2,1,0:T(8,128)(2,1)}, u32[]{:S(2)}) copy-start(bf16[4,256,1024]{2,1,0:T(8,128)(2,1)} %keys.1) | copy-start | bytes 6291460
  103.6 27.6 %copy-start.6 = (bf16[4,256,1024]{2,1,0:T(8,128)(2,1)S(1)}, bf16[4,256,1024]{2,1,0:T(8,128)(2,1)}, u32[]{:S(2)}) copy-start(bf16[4,256,1024]{2,1,0:T(8,128)(2,1)} %values.1) | copy-start | bytes 6291460
  103.6 27.6 %copy-start.14 = (s32[4]{0:T(128)S(1)}, s32[4]{0:T(128)}, u32[]{:S(2)}) copy-start(s32[4]{0:T(128)} %fills.1) | copy-start | bytes 52
  103.6 27.6 %copy-start.15 = (s32[4]{0:T(128)S(1)}, s32[4]{0:T(128)}, u32[]{:S(2)}) copy-start(s32[4]{0:T(128)} %spans.1) | copy-start | bytes 52
  103.6 27.6 %copy-start.16 = (f32[128]{0:T(128)S(1)}, f32[128]{0:T(128)}, u32[]{:S(2)}) copy-start(f32[128]{0:T(128)} %param.13) | copy-start | bytes 1540
  103.6 27.6 %copy-start.17 = (f32[128]{0:T(128)S(1)}, f32[128]{0:T(128)}, u32[]{:S(2)}) copy-start(f32[128]{0:T(128)} %param.14) | copy-start | bytes 1540
  128.9 26.9 %copy-start.1 = (bf16[512,640]{1,0:T(8,128)(2,1)S(1)}, bf16[512,640]{1,0:T(8,128)(2,1)}, u32[]{:S(2)}) copy-start(bf16[512,640]{1,0:T(8,128)(2,1)} %copy-done) | copy-start | bytes 1966084
  129.1 23.3 %collective-permute-start.25 = (bf16[768,640]{1,0:T(8,128)(2,1)S(1)}, bf16[768,640]{1,0:T(8,128)(2,1)S(1)}, u32[]{:S(2)}, u32[]{:S(2)}) collective-permute-start(bf16[768,640]{1,0:T(8,128)(2,1)S(1)} %get-tuple-element.111), channel_id=1, source_target_pairs={{0,48},{8,56},{16,0},{24,8},{32,16},{40,24},{48,32},{56,40},{64,11... | collective-permute-start | bytes 2949128 | tf_op jit(solution)/shard_map/ppermute | solution.py:183
  130.2 25.3 %collective-permute-start.23 = (bf16[768,640]{1,0:T(8,128)(2,1)S(1)}, bf16[768,640]{1,0:T(8,128)(2,1)S(1)}, u32[]{:S(2)}, u32[]{:S(2)}) collective-permute-start(bf16[768,640]{1,0:T(8,128)(2,1)S(1)} %get-tuple-element.112), channel_id=1, source_target_pairs={{0,16},{8,24},{16,32},{24,40},{32,48},{40,56},{48,0},{56,8},{64,80... | collective-permute-start | bytes 2949128 | tf_op jit(solution)/shard_map/ppermute | solution.py:180
  142.5 25.0 %copy-start.11 = (bf16[64,8192]{1,0:T(8,128)(2,1)}, bf16[64,8192]{1,0:T(8,128)(2,1)S(1)}, u32[]{:S(2)}) copy-start(bf16[64,8192]{1,0:T(8,128)(2,1)S(1)} %attend.1) | copy-start | bytes 3145732
  142.5 25.0 %collective-permute-start.22 = (bf16[64,8192]{1,0:T(8,128)(2,1)S(1)}, bf16[64,8192]{1,0:T(8,128)(2,1)S(1)}, u32[]{:S(2)}, u32[]{:S(2)}) collective-permute-start(bf16[64,8192]{1,0:T(8,128)(2,1)S(1)} %attend.1), channel_id=1, source_target_pairs={{0,1},{1,0},{2,3},{3,2},{4,5},{5,4},{6,7},{7,6},{8,9},{9,8},{10,11... | collective-permute-start | bytes 3145736 | tf_op jit(solution)/shard_map/ppermute | solution.py:186
  142.6 24.9 %collective-permute-start.21 = (bf16[64,8192]{1,0:T(8,128)(2,1)S(1)}, bf16[64,8192]{1,0:T(8,128)(2,1)}, u32[]{:S(2)}, u32[]{:S(2)}) collective-permute-start(bf16[64,8192]{1,0:T(8,128)(2,1)S(1)} %attend.1), channel_id=1, source_target_pairs={{0,6},{1,7},{2,0},{3,1},{4,2},{5,3},{6,4},{7,5},{8,14},{9,15},{10,... | collective-permute-start | bytes 3145736 | tf_op jit(solution)/shard_map/ppermute | solution.py:183
  145.1 24.7 %collective-permute-start.20 = (bf16[64,8192]{1,0:T(8,128)(2,1)S(1)}, bf16[64,8192]{1,0:T(8,128)(2,1)S(1)}, u32[]{:S(2)}, u32[]{:S(2)}) collective-permute-start(bf16[64,8192]{1,0:T(8,128)(2,1)S(1)} %attend.1), channel_id=1, source_target_pairs={{0,2},{1,3},{2,4},{3,5},{4,6},{5,7},{6,0},{7,1},{8,10},{9,11},{10,... | collective-permute-start | bytes 3145736 | tf_op jit(solution)/shard_map/ppermute | solution.py:180
  152.4 9.7 %collective-permute-start.26 = (bf16[256,640]{1,0:T(8,128)(2,1)S(1)}, bf16[256,640]{1,0:T(8,128)(2,1)S(1)}, u32[]{:S(2)}, u32[]{:S(2)}) collective-permute-start(bf16[256,640]{1,0:T(8,128)(2,1)S(1)} %slice.123), channel_id=1, source_target_pairs={{0,48},{8,56},{16,0},{24,8},{32,16},{40,24},{48,32},{56,40},{64,11... | collective-permute-start | bytes 983048 | tf_op jit(solution)/shard_map/ppermute | solution.py:183
  155.5 10.3 %collective-permute-start.24 = (bf16[256,640]{1,0:T(8,128)(2,1)S(1)}, bf16[256,640]{1,0:T(8,128)(2,1)S(1)}, u32[]{:S(2)}, u32[]{:S(2)}) collective-permute-start(bf16[256,640]{1,0:T(8,128)(2,1)S(1)} %slice.122), channel_id=1, source_target_pairs={{0,16},{8,24},{16,32},{24,40},{32,48},{40,56},{48,0},{56,8},{64,80... | collective-permute-start | bytes 983048 | tf_op jit(solution)/shard_map/ppermute | solution.py:180
  165.8 1.0 copy-start.9
  166.8 0.7 copy-start.7
  167.5 2.3 %copy-start.18 = (bf16[64,8192]{1,0:T(8,128)(2,1)}, bf16[64,8192]{1,0:T(8,128)(2,1)S(1)}, u32[]{:S(2)}) copy-start(bf16[64,8192]{1,0:T(8,128)(2,1)S(1)} %collective-permute-done.22) | copy-start | bytes 3145732
  169.8 1.0 copy-start.20
  170.9 12.0 %collective-permute-start.30 = (bf16[3584,640]{1,0:T(8,128)(2,1)}, bf16[3584,640]{1,0:T(8,128)(2,1)}, u32[]{:S(2)}, u32[]{:S(2)}) collective-permute-start(bf16[3584,640]{1,0:T(8,128)(2,1)} %pack.1), channel_id=1, source_target_pairs={{0,8},{8,0},{16,24},{24,16},{32,40},{40,32},{48,56},{56,48},{64,72... | collective-permute-start | bytes 13762568 | tf_op jit(solution)/shard_map/ppermute | solution.py:189
  171.2 9.4 %copy-start.2 = (bf16[512,640]{1,0:T(8,128)(2,1)S(1)}, bf16[512,640]{1,0:T(8,128)(2,1)}, u32[]{:S(2)}) copy-start(bf16[512,640]{1,0:T(8,128)(2,1)} %copy-done) | copy-start | bytes 1966084
  171.2 9.3 %copy-start.4 = (bf16[512,640]{1,0:T(8,128)(2,1)S(1)}, bf16[512,640]{1,0:T(8,128)(2,1)}, u32[]{:S(2)}) copy-start(bf16[512,640]{1,0:T(8,128)(2,1)} %refs_0_.3) | copy-start | bytes 1966084
  171.3 9.3 %copy-start.8 = (bf16[256,640]{1,0:T(8,128)(2,1)S(1)}, bf16[256,640]{1,0:T(8,128)(2,1)}, u32[]{:S(2)}) copy-start(bf16[256,640]{1,0:T(8,128)(2,1)} %copy-done.7) | copy-start | bytes 983044
  171.3 9.3 %copy-start.10 = (bf16[256,640]{1,0:T(8,128)(2,1)S(1)}, bf16[256,640]{1,0:T(8,128)(2,1)}, u32[]{:S(2)}) copy-start(bf16[256,640]{1,0:T(8,128)(2,1)} %copy-done.9) | copy-start | bytes 983044
  173.6 9.3 %collective-permute-start.31 = (bf16[2,256,640]{2,1,0:T(8,128)(2,1)}, bf16[2,256,640]{2,1,0:T(8,128)(2,1)S(1)}, u32[]{:S(2)}, u32[]{:S(2)}) collective-permute-start(bf16[2,256,640]{2,1,0:T(8,128)(2,1)} %pad_maximum_fusion.12), channel_id=1, source_target_pairs={{0,8},{8,0},{16,24},{24,16},{32,40},{40,32},{48,56},{56,48},{64,72... | collective-permute-start | bytes 1966088 | tf_op jit(solution)/shard_map/ppermute | solution.py:189
  175.8 25.2 %collective-permute-start.29 = (bf16[64,8192]{1,0:T(8,128)(2,1)S(1)}, bf16[64,8192]{1,0:T(8,128)(2,1)S(1)}, u32[]{:S(2)}, u32[]{:S(2)}) collective-permute-start(bf16[64,8192]{1,0:T(8,128)(2,1)S(1)} %get-tuple-element.115), channel_id=1, source_target_pairs={{0,1},{1,0},{2,3},{3,2},{4,5},{5,4},{6,7},{7,6},{8,9},{9,8},{10,11... | collective-permute-start | bytes 3145736 | tf_op jit(solution)/shard_map/ppermute | solution.py:186
  177.3 26.0 %collective-permute-start.27 = (bf16[64,8192]{1,0:T(8,128)(2,1)S(1)}, bf16[64,8192]{1,0:T(8,128)(2,1)S(1)}, u32[]{:S(2)}, u32[]{:S(2)}) collective-permute-start(bf16[64,8192]{1,0:T(8,128)(2,1)S(1)} %get-tuple-element.116), channel_id=1, source_target_pairs={{0,2},{1,3},{2,4},{3,5},{4,6},{5,7},{6,0},{7,1},{8,10},{9,11},{10,... | collective-permute-start | bytes 3145736 | tf_op jit(solution)/shard_map/ppermute | solution.py:180
  177.3 26.0 %collective-permute-start.28 = (bf16[64,8192]{1,0:T(8,128)(2,1)S(1)}, bf16[64,8192]{1,0:T(8,128)(2,1)S(1)}, u32[]{:S(2)}, u32[]{:S(2)}) collective-permute-start(bf16[64,8192]{1,0:T(8,128)(2,1)S(1)} %get-tuple-element.117), channel_id=1, source_target_pairs={{0,6},{1,7},{2,0},{3,1},{4,2},{5,3},{6,4},{7,5},{8,14},{9,15},{10,... | collective-permute-start | bytes 3145736 | tf_op jit(solution)/shard_map/ppermute | solution.py:183
  182.9 5.0 %copy-start.12 = (bf16[64,8192]{1,0:T(8,128)(2,1)S(1)}, bf16[64,8192]{1,0:T(8,128)(2,1)}, u32[]{:S(2)}) copy-start(bf16[64,8192]{1,0:T(8,128)(2,1)} %copy-done.11) | copy-start | bytes 3145732
  182.9 5.0 %copy-start.19 = (bf16[64,8192]{1,0:T(8,128)(2,1)S(1)}, bf16[64,8192]{1,0:T(8,128)(2,1)}, u32[]{:S(2)}) copy-start(bf16[64,8192]{1,0:T(8,128)(2,1)} %copy-done.18) | copy-start | bytes 3145732
  182.9 5.0 %copy-start.21 = (bf16[64,8192]{1,0:T(8,128)(2,1)S(1)}, bf16[64,8192]{1,0:T(8,128)(2,1)}, u32[]{:S(2)}) copy-start(bf16[64,8192]{1,0:T(8,128)(2,1)} %copy-done.20) | copy-start | bytes 3145732
  203.4 11.6 %collective-permute-start.32 = (bf16[16,8192]{1,0:T(8,128)(2,1)S(1)}, bf16[16,8192]{1,0:T(8,128)(2,1)S(1)}, u32[]{:S(2)}, u32[]{:S(2)}) collective-permute-start(bf16[16,8192]{1,0:T(8,128)(2,1)S(1)} %slice.115), channel_id=1, source_target_pairs={{0,2},{1,3},{2,4},{3,5},{4,6},{5,7},{6,0},{7,1},{8,10},{9,11},{10,... | collective-permute-start | bytes 786440 | tf_op jit(solution)/shard_map/ppermute | solution.py:180
  203.5 11.5 %collective-permute-start.33 = (bf16[16,8192]{1,0:T(8,128)(2,1)S(1)}, bf16[16,8192]{1,0:T(8,128)(2,1)S(1)}, u32[]{:S(2)}, u32[]{:S(2)}) collective-permute-start(bf16[16,8192]{1,0:T(8,128)(2,1)S(1)} %slice.116), channel_id=1, source_target_pairs={{0,6},{1,7},{2,0},{3,1},{4,2},{5,3},{6,4},{7,5},{8,14},{9,15},{10,... | collective-permute-start | bytes 786440 | tf_op jit(solution)/shard_map/ppermute | solution.py:183
  206.8 12.1 %collective-permute-start.34 = (bf16[32,8192]{1,0:T(8,128)(2,1)S(1)}, bf16[32,8192]{1,0:T(8,128)(2,1)S(1)}, u32[]{:S(2)}, u32[]{:S(2)}) collective-permute-start(bf16[32,8192]{1,0:T(8,128)(2,1)S(1)} %slice.117), channel_id=1, source_target_pairs={{0,1},{1,0},{2,3},{3,2},{4,5},{5,4},{6,7},{7,6},{8,9},{9,8},{10,11... | collective-permute-start | bytes 1572872 | tf_op jit(solution)/shard_map/ppermute | solution.py:186

commit v2 on v1

--- a/solution.py
+++ b/solution.py
@@ -72,8 +72,8 @@
     empty = jnp.zeros((HEAD_SIZE - slots, HEAD_SIZE), jnp.bfloat16)
     query_columns = group // 2 * HEAD_SIZE
     contract_last = (((1,), (1,)), ((), ()))
-    score_scale = 1.0 / math.sqrt(HEAD_SIZE)
-    for head in range(KEY_VALUE_HEADS):
+    exp_scale = math.log2(math.e) / math.sqrt(HEAD_SIZE)
+    def prepare(head):
         queries = jnp.concatenate(
             [
                 packed[2 * head + g // 4, :, g % 4 * HEAD_SIZE : (g % 4 + 1) * HEAD_SIZE]
@@ -88,6 +88,9 @@
         fresh_value = jnp.where(low, pltpu.roll(first, HEAD_SIZE // 2, 1), second)
         fresh_key = jnp.concatenate([turned(fresh_key, k_gain[...], cos_one, sin_one), empty])
         fresh_value = jnp.concatenate([(fresh_value * inverse[...]).astype(jnp.bfloat16), empty])
+        return queries, fresh_key, fresh_value
+
+    def score(head, queries, fresh_key):
         columns = slice(head * HEAD_SIZE, (head + 1) * HEAD_SIZE)
         old = lax.dot_general(
             queries, keys[0, :, columns], contract_last, preferred_element_type=jnp.float32
@@ -95,12 +98,17 @@
         new = lax.dot_general(
             queries, fresh_key, contract_last, preferred_element_type=jnp.float32
         )
-        old = jnp.where(frame_live, old * score_scale, -1e30)
-        new = jnp.where(slot_live, new * score_scale, -1e30)
+        return old, new
+
+    def weigh(old, new):
+        old = jnp.where(frame_live, old, -1e30)
+        new = jnp.where(slot_live, new, -1e30)
         scores = jnp.concatenate([old, new], axis=1)
-        weights = jnp.exp(scores - jnp.max(scores, axis=-1, keepdims=True))
-        total = jnp.sum(weights, axis=-1, keepdims=True)
-        weights = weights.astype(jnp.bfloat16)
+        weights = jnp.exp2((scores - jnp.max(scores, axis=-1, keepdims=True)) * exp_scale)
+        return weights.astype(jnp.bfloat16), jnp.sum(weights, axis=-1, keepdims=True)
+
+    def mix(head, weights, total, fresh_value):
+        columns = slice(head * HEAD_SIZE, (head + 1) * HEAD_SIZE)
         mixed = jnp.dot(
             weights[:, :frames], values[0, :, columns], preferred_element_type=jnp.float32
         ) + jnp.dot(weights[:, frames:], fresh_value, preferred_element_type=jnp.float32)
@@ -108,6 +116,14 @@
         for g in range(group):
             start = (head * group + g) * HEAD_SIZE
             attended[:, start : start + HEAD_SIZE] = mixed[g * slots : (g + 1) * slots]
+
+    for pair in range(0, KEY_VALUE_HEADS, 2):
+        heads = (pair, pair + 1)
+        prepared = [prepare(head) for head in heads]
+        scored = [score(head, p[0], p[1]) for head, p in zip(heads, prepared)]
+        weighed = [weigh(*s) for s in scored]
+        for head, w, p in zip(heads, weighed, prepared):
+            mix(head, *w, p[2])
 
 
 def attend(packed, inverse, cosine, sine, q_gain, k_gain, keys, values, spans, fills):
@@ -213,7 +229,7 @@
             result[0] = pieces[piece][block * rows : (block + 1) * rows]
 
 
-def put(buffer, pieces, sources, places, blocks, rows, vmem_limit=24 << 20):
+def put(buffer, pieces, sources, places, blocks, rows, vmem_limit=13 << 20):
     columns = pieces[0].shape[1]
     aliased = 0 if buffer is None else 1
     held = () if buffer is None else (buffer,)
@@ -232,6 +248,28 @@
         cost_estimate=pl.CostEstimate(flops=0, bytes_accessed=rows, transcendentals=0),
         name="put",
     )(places, *held, *pieces)
+
+
+def order_kernel(sources, places, *refs):
+    pieces, result = refs[:-1], refs[-1]
+    rows = result.shape[1]
+    for i, (piece, block) in enumerate(sources):
+        result[places[i]] = pieces[piece][block * rows : (block + 1) * rows]
+
+
+def order(pieces, sources, places, blocks, rows):
+    columns = pieces[0].shape[1]
+    vmem = pl.BlockSpec(memory_space=pltpu.VMEM)
+    return pl.pallas_call(
+        functools.partial(order_kernel, sources),
+        grid_spec=pltpu.PrefetchScalarGridSpec(
+            num_scalar_prefetch=1, in_specs=[vmem] * len(pieces), out_specs=vmem
+        ),
+        out_shape=jax.ShapeDtypeStruct((blocks, rows, columns), pieces[0].dtype),
+        compiler_params=pltpu.CompilerParams(vmem_limit_bytes=8 << 20),
+        cost_estimate=pl.CostEstimate(flops=0, bytes_accessed=rows, transcendentals=0),
+        name="order",
+    )(places, *pieces)
 
 
 def pack_kernel(payloads, pieces, *refs):
@@ -388,7 +426,7 @@
             + tuple((i, 0, 3 * half_out) for i in (4, 5)),
         ),
         5,
-        12 << 20,
+        6 << 20,
     )
     other_far = jnp.stack([o_far_up, o_far_down])
     a_up, a_down, a_swap, o_far_up, o_far_down, o_near, other_far = barrier(
@@ -439,11 +477,11 @@
     b_up, b_down, b_swap, near_rows = barrier((b_up, b_down, b_swap, near_rows))
     c_up = narrow.up(b_up[:quarter])
     c_down = narrow.down(b_down[quarter:half_rows])
-    c_swap = narrow.swap(b_up[half_rows:])
+    c_swap = narrow.swap(b_up[half_rows : half_rows + quarter])
+    c_swap_last = narrow.swap(b_up[half_rows + quarter :])
     one, other = narrow.at_pair, 1 - narrow.at_pair
     place_of = lambda ring, pair, half: (narrow.ring(ring) * 2 + pair) * 2 + half
-    result = put(
-        None,
+    result = order(
         (near_rows, project_out(jnp.concatenate([b_swap, b_up, b_down]))),
         tuple((0, i) for i in range(8)) + tuple((1, i) for i in range(6)),
         jnp.stack(
@@ -467,10 +505,12 @@
         16,
         half_rows,
     )
-    result, c_up, c_down, c_swap = barrier((result, c_up, c_down, c_swap))
+    c_up, c_down, c_swap, c_swap_last, result = barrier(
+        (c_up, c_down, c_swap, c_swap_last, result)
+    )
     result = put(
         result,
-        (project_out(jnp.concatenate([c_swap, c_up, c_down])),),
+        (project_out(jnp.concatenate([c_swap, c_swap_last, c_up, c_down])),),
         ((0, 0), (0, 1)),
         jnp.stack([place_of(2, other, 0), place_of(2, other, 1)]),
         16,

time: 222 us -> 217 us (0.977)
  Pallas kernels: 32.8 us -> 25.7 us
    pallas_call x6 -> x5, Pallas kernels: 17.7 us -> 12.7 us  [put(): pl.pallas_call(functools.partial(put_kernel, sources, aliased), grid_spec...]
    ppermute x12, waiting for transfers between devices: 20.8 us -> 24.5 us  [down(): return lax.ppermute(block, self.axis, self.pairs(-1, 0, 0))]
    ppermute x12, waiting for transfers between devices: 17.8 us -> 14.2 us  [up(): return lax.ppermute(block, self.axis, self.pairs(1, 0, 0))]
    pallas_call x1, Pallas kernels: 11.3 us -> 7.88 us  [attend(): pl.pallas_call(attend_kernel, grid_spec=pltpu.PrefetchScalarGridSpec(num_...]
    ppermute x6 -> x7, waiting for transfers between devices: 14.4 us -> 15.5 us  [swap(): return lax.ppermute(block, self.axis, self.pairs(0, 1, 0))]
    ppermute x6 -> x7, starting transfers between devices: 9.44 us -> 9.53 us  [swap(): return lax.ppermute(block, self.axis, self.pairs(0, 1, 0))]
  transfers between devices with their start and end apart: 36 -> 37, of which waited for: 17 -> 16; matrix products, arithmetic and copies ran while one was open for 12% -> 12% of each run, Pallas kernels for 14% -> 11%
where the time goes in v2:
time: 217 us
  waiting for transfers between devices  76.2 us (35%)
  starting transfers between devices  48.8 us (22%)
  Pallas kernels  25.7 us (12%)
  blocking collectives  25.2 us (12%)
  local copies, waits for them, and re-layouts  18.4 us (8%)
  matrix products  17.6 us (8%)
  other arithmetic  4 us (2%)
    ppermute x12, starting transfers between devices, down(): return lax.ppermute(block, self.axis, self.pairs(-1, 0, 0))  27.9 us
    all_to_all x1, blocking collectives, shards(): lax.all_to_all(projected.reshape(wide_count, rows, -1), 'wide', split_axi...  25.2 us
    ppermute x12, waiting for transfers between devices, down(): return lax.ppermute(block, self.axis, self.pairs(-1, 0, 0))  24.5 us
    all_to_all x1, waiting for transfers between devices, shards(): lax.all_to_all(tokens, 'narrow', split_axis=0, concat_axis=1, tiled=True)  20.1 us
    ppermute x7, waiting for transfers between devices, swap(): return lax.ppermute(block, self.axis, self.pairs(0, 1, 0))  15.5 us
    ppermute x12, waiting for transfers between devices, up(): return lax.ppermute(block, self.axis, self.pairs(1, 0, 0))  14.2 us
    pallas_call x5, Pallas kernels, put(): pl.pallas_call(functools.partial(put_kernel, sources, aliased), grid_spec...  12.7 us
    ppermute x7, starting transfers between devices, swap(): return lax.ppermute(block, self.axis, self.pairs(0, 1, 0))  9.53 us
  transfers between devices with their start and end apart: 37, of which 16 were waited for; matrix products, arithmetic and copies ran while one was open for 12% of the time, Pallas kernels for 11%

profile of v2, /device:TPU:0, one launch (start us, length us, event | category | flops | bytes accessed | tf_op | source)
XLA Modules:
  0.0 216.9 jit_solution(10384566101450809496)
XLA Ops:
  0.0 3.1 %collective-permute-start.1 = (bf16[512,640]{1,0:T(8,128)(2,1)}, bf16[512,640]{1,0:T(8,128)(2,1)S(1)}, u32[]{:S(2)}, u32[]{:S(2)}) collective-permute-start(bf16[512,640]{1,0:T(8,128)(2,1)} %refs_0_.3), channel_id=1, source_target_pairs={{0,48},{8,56},{16,0},{24,8},{32,16},{40,24},{48,32},{56,40},{64,11... | collective-permute-start | bytes 1966088 | tf_op jit(solution)/shard_map/ppermute | solution.py:199
  3.1 1.9 collective-permute-start.3
  5.0 1.5 collective-permute-start.2
  6.5 2.1 collective-permute-start.4
  8.6 3.5 %all-to-all-start = ((bf16[8,64,640]{2,1,0:T(8,128)(2,1)}), bf16[8,64,640]{2,1,0:T(8,128)(2,1)S(1)}, u32[]{:S(2)}, u32[]{:S(2)}) async-start(bf16[8,64,640]{2,1,0:T(8,128)(2,1)} %bitcast.146), calls=%async_computation | async-start | bytes 1310720 | tf_op jit(solution)/shard_map/all_to_all | solution.py:320
  12.2 0.7 add_convert_fusion
  13.5 20.1 %all-to-all-done = bf16[8,64,640]{2,1,0:T(8,128)(2,1)S(1)} async-done(((bf16[8,64,640]{2,1,0:T(8,128)(2,1)}), bf16[8,64,640]{2,1,0:T(8,128)(2,1)S(1)}, u32[]{:S(2)}, u32[]{:S(2)}) %all-to-all-start) | async-done | bytes 655392 | tf_op jit(solution)/shard_map/all_to_all | solution.py:320
  34.0 2.9 %collective-permute-start.6 = (bf16[640,640]{1,0:T(8,128)(2,1)}, bf16[640,640]{1,0:T(8,128)(2,1)S(1)}, u32[]{:S(2)}, u32[]{:S(2)}) collective-permute-start(bf16[640,640]{1,0:T(8,128)(2,1)} %collective-permute-done.2.refs_3_), channel_id=1, source_target_pairs={{0,6},{1,7},{2,0},{3,1},{4,2},{5,3},{6,4},{7,5},{8,14},{9,15},{10,... | collective-permute-start | bytes 2457608 | tf_op jit(solution)/shard_map/ppermute | solution.py:199
  37.2 2.8 %collective-permute-start.9 = (bf16[64,5120]{1,0:T(8,128)(2,1)S(1)}, bf16[64,5120]{1,0:T(8,128)(2,1)S(1)}, u32[]{:S(2)}, u32[]{:S(2)}) collective-permute-start(bf16[64,5120]{1,0:T(8,128)(2,1)S(1)} %multiply_convert_fusion), channel_id=1, source_target_pairs={{0,64},{8,72},{16,80},{24,88},{32,96},{40,104},{48,112},{56,120},{... | collective-permute-start | bytes 1966088 | tf_op jit(solution)/shard_map/ppermute | solution.py:202
  40.0 3.0 %collective-permute-start.8 = (bf16[64,5120]{1,0:T(8,128)(2,1)S(1)}, bf16[64,5120]{1,0:T(8,128)(2,1)S(1)}, u32[]{:S(2)}, u32[]{:S(2)}) collective-permute-start(bf16[64,5120]{1,0:T(8,128)(2,1)S(1)} %multiply_convert_fusion), channel_id=1, source_target_pairs={{0,48},{8,56},{16,0},{24,8},{32,16},{40,24},{48,32},{56,40},{64,11... | collective-permute-start | bytes 1966088 | tf_op jit(solution)/shard_map/ppermute | solution.py:199
  43.0 1.1 slice.96
  44.1 5.3 %broadcast_in_dim.9 = bf16[2,4,2,2,32,5120]{5,4,3,2,1,0:T(8,128)(2,1)} broadcast(bf16[]{:T(256)} %constant.196.clone.1), dimensions={} | broadcast | bytes 10485762 | tf_op jit(solution)/shard_map/broadcast_in_dim | solution.py:335
  49.4 0.9 constant_dynamic-update-slice_fusion.11
  50.4 2.2 %collective-permute-done.9 = bf16[64,5120]{1,0:T(8,128)(2,1)S(1)} collective-permute-done((bf16[64,5120]{1,0:T(8,128)(2,1)S(1)}, bf16[64,5120]{1,0:T(8,128)(2,1)S(1)}, u32[]{:S(2)}, u32[]{:S(2)}) %collective-permute-start.9) | collective-permute-done | bytes 655392 | tf_op jit(solution)/shard_map/ppermute | solution.py:202
  52.6 3.0 %collective-permute-start.14 = (bf16[512,640]{1,0:T(8,128)(2,1)S(1)}, bf16[512,640]{1,0:T(8,128)(2,1)S(1)}, u32[]{:S(2)}, u32[]{:S(2)}) collective-permute-start(bf16[512,640]{1,0:T(8,128)(2,1)S(1)} %copy-done.3), channel_id=1, source_target_pairs={{0,64},{8,72},{16,80},{24,88},{32,96},{40,104},{48,112},{56,120},{... | collective-permute-start | bytes 1966088 | tf_op jit(solution)/shard_map/ppermute | solution.py:202
  55.6 1.8 collective-permute-done.7
  57.7 2.8 %collective-permute-start.11 = (bf16[640,640]{1,0:T(8,128)(2,1)S(1)}, bf16[640,640]{1,0:T(8,128)(2,1)S(1)}, u32[]{:S(2)}, u32[]{:S(2)}) collective-permute-start(bf16[640,640]{1,0:T(8,128)(2,1)S(1)} %pad_maximum_fusion.10), channel_id=1, source_target_pairs={{0,6},{1,7},{2,0},{3,1},{4,2},{5,3},{6,4},{7,5},{8,14},{9,15},{10,... | collective-permute-start | bytes 2457608 | tf_op jit(solution)/shard_map/ppermute | solution.py:199
  60.9 1.0 collective-permute-start.13
  61.9 1.1 collective-permute-start.12
  63.0 0.9 constant_dynamic-update-slice_fusion.10
  63.9 0.9 constant_dynamic-update-slice_fusion.9
  64.8 0.9 constant_dynamic-update-slice_fusion.8
  65.7 3.4 %put.5.refs_0_ = bf16[16,320,640]{2,1,0:T(8,128)(2,1)S(1)} custom-call(s32[12]{0:T(128)S(1)} %stack.240.places, bf16[640,640]{1,0:T(8,128)(2,1)S(1)} %copy-done.13, bf16[640,640]{1,0:T(8,128)(2,1)S(1)} %collective-permute-done.3.refs_1_, bf16[640,640]{1,0:T(8,128)(2,1)} %collective-permute-done.4.refs_2_, bf16[640,640]{1,0:T(8,128)(2,1)} %collective-permute-done.2.refs_3_, ...), custom_call_target="tpu_custom_call" | custom-call | bytes 320 | tf_op jit(solution)/shard_map/put/pallas_call | solution.py:236
  69.5 4.1 %collective-permute-done.11.refs_2_ = bf16[640,640]{1,0:T(8,128)(2,1)S(1)} collective-permute-done((bf16[640,640]{1,0:T(8,128)(2,1)S(1)}, bf16[640,640]{1,0:T(8,128)(2,1)S(1)}, u32[]{:S(2)}, u32[]{:S(2)}) %collective-permute-start.11) | collective-permute-done | bytes 819232 | tf_op jit(solution)/shard_map/ppermute | solution.py:199
  73.5 3.4 %collective-permute-done.10.refs_1_ = bf16[640,640]{1,0:T(8,128)(2,1)S(1)} collective-permute-done((bf16[640,640]{1,0:T(8,128)(2,1)S(1)}, bf16[640,640]{1,0:T(8,128)(2,1)S(1)}, u32[]{:S(2)}, u32[]{:S(2)}) %collective-permute-start.10) | collective-permute-done | bytes 819232 | tf_op jit(solution)/shard_map/ppermute | solution.py:196
  76.9 3.7 %collective-permute-done.13 = bf16[96,5120]{1,0:T(8,128)(2,1)S(1)} collective-permute-done((bf16[96,5120]{1,0:T(8,128)(2,1)S(1)}, bf16[96,5120]{1,0:T(8,128)(2,1)S(1)}, u32[]{:S(2)}, u32[]{:S(2)}) %collective-permute-start.13) | collective-permute-done | bytes 983072 | tf_op jit(solution)/shard_map/ppermute | solution.py:199
  80.7 2.7 %collective-permute-done.12 = bf16[96,5120]{1,0:T(8,128)(2,1)S(1)} collective-permute-done((bf16[96,5120]{1,0:T(8,128)(2,1)S(1)}, bf16[96,5120]{1,0:T(8,128)(2,1)S(1)}, u32[]{:S(2)}, u32[]{:S(2)}) %collective-permute-start.12) | collective-permute-done | bytes 983072 | tf_op jit(solution)/shard_map/ppermute | solution.py:196
  83.9 1.7 collective-permute-start.15
  86.6 0.8 put.6
  87.4 3.2 %collective-permute-done.16 = bf16[32,5120]{1,0:T(8,128)(2,1)S(1)} collective-permute-done((bf16[32,5120]{1,0:T(8,128)(2,1)S(1)}, bf16[32,5120]{1,0:T(8,128)(2,1)S(1)}, u32[]{:S(2)}, u32[]{:S(2)}) %collective-permute-start.16) | collective-permute-done | bytes 327712 | tf_op jit(solution)/shard_map/ppermute | solution.py:199
  90.6 1.5 collective-permute-done.15
  92.9 1.9 collective-permute-done.18
  95.3 8.3 %convolution_convert_fusion = bf16[1024,640]{1,0:T(8,128)(2,1)S(1)} fusion(bf16[1024,5120]{1,0:T(8,128)(2,1)S(1)} %bitcast.123, bf16[5120,640]{1,0:T(8,128)(2,1)S(1)} %bitcast.115), kind=kOutput, calls=%fused_computation.18 | convolution fusion | flops 6711541760 | bytes 18350080 | tf_op jit(solution)/shard_map/dot_general | solution.py:394
  103.6 25.2 %all_to_all.18.packed = bf16[16,64,640]{2,1,0:T(8,128)(2,1)S(1)} all-to-all(bf16[16,64,640]{2,1,0:T(8,128)(2,1)S(1)} %bitcast.143), channel_id=1, replica_groups=mesh['wide'=16,'narrow'=8] {'wide'}, dimensions={0} | all-to-all | bytes 2621440 | tf_op jit(solution)/shard_map/all_to_all | solution.py:395
  129.1 1.1 collective-permute-start.25
  130.1 1.0 collective-permute-start.23
  131.2 7.9 %attend.1 = bf16[64,8192]{1,0:T(8,128)(2,1)S(1)} custom-call(s32[4]{0:T(128)S(1)} %copy-done.14, s32[4]{0:T(128)S(1)} %copy-done.15, bf16[16,64,640]{2,1,0:T(8,128)(2,1)S(1)} %all_to_all.18.packed, f32[64,128]{1,0:T(8,128)S(1)} %broadcast_in_dim.8.inverse, f32[64,128]{1,0:T(8,128)S(1)} %get-tuple-element.79.cosine, f32[64,128]{1,0:T(8,128)S(1)} %get-tuple-element.80.sine, ...), custom_call_target="tpu_custom_call" | custom-call | flops 570425344 | bytes 6553600 | tf_op jit(solution)/shard_map/attend/pallas_call | solution.py:137
  139.2 2.5 %collective-permute-start.21 = (bf16[64,8192]{1,0:T(8,128)(2,1)S(1)}, bf16[64,8192]{1,0:T(8,128)(2,1)}, u32[]{:S(2)}, u32[]{:S(2)}) collective-permute-start(bf16[64,8192]{1,0:T(8,128)(2,1)S(1)} %attend.1), channel_id=1, source_target_pairs={{0,6},{1,7},{2,0},{3,1},{4,2},{5,3},{6,4},{7,5},{8,14},{9,15},{10,... | collective-permute-start | bytes 3145736 | tf_op jit(solution)/shard_map/ppermute | solution.py:199
  141.7 10.6 %collective-permute-done.25.refs_5_ = bf16[768,640]{1,0:T(8,128)(2,1)S(1)} collective-permute-done((bf16[768,640]{1,0:T(8,128)(2,1)S(1)}, bf16[768,640]{1,0:T(8,128)(2,1)S(1)}, u32[]{:S(2)}, u32[]{:S(2)}) %collective-permute-start.25) | collective-permute-done | bytes 983072 | tf_op jit(solution)/shard_map/ppermute | solution.py:199
  152.4 3.0 %collective-permute-start.26 = (bf16[256,640]{1,0:T(8,128)(2,1)S(1)}, bf16[256,640]{1,0:T(8,128)(2,1)S(1)}, u32[]{:S(2)}, u32[]{:S(2)}) collective-permute-start(bf16[256,640]{1,0:T(8,128)(2,1)S(1)} %slice.127), channel_id=1, source_target_pairs={{0,48},{8,56},{16,0},{24,8},{32,16},{40,24},{48,32},{56,40},{64,11... | collective-permute-start | bytes 983048 | tf_op jit(solution)/shard_map/ppermute | solution.py:199
  155.5 3.7 %pack.1 = bf16[3584,640]{1,0:T(8,128)(2,1)} custom-call(bf16[512,640]{1,0:T(8,128)(2,1)S(1)} %copy-done.3, bf16[512,640]{1,0:T(8,128)(2,1)S(1)} %copy-done.1, bf16[512,640]{1,0:T(8,128)(2,1)S(1)} %collective-permute-done.1.refs_2_, bf16[512,640]{1,0:T(8,128)(2,1)S(1)} %collective-permute-done.14.refs_3_, ...), custom_call_target="tpu_custom_call" | custom-call | bytes 3584 | tf_op jit(solution)/shard_map/pack/pallas_call | solution.py:287
  159.3 2.8 %collective-permute-done.26.refs_7_ = bf16[256,640]{1,0:T(8,128)(2,1)S(1)} collective-permute-done((bf16[256,640]{1,0:T(8,128)(2,1)S(1)}, bf16[256,640]{1,0:T(8,128)(2,1)S(1)}, u32[]{:S(2)}, u32[]{:S(2)}) %collective-permute-start.26) | collective-permute-done | bytes 327712 | tf_op jit(solution)/shard_map/ppermute | solution.py:199
  162.0 3.5 %collective-permute-done.24.refs_6_ = bf16[256,640]{1,0:T(8,128)(2,1)S(1)} collective-permute-done((bf16[256,640]{1,0:T(8,128)(2,1)S(1)}, bf16[256,640]{1,0:T(8,128)(2,1)S(1)}, u32[]{:S(2)}, u32[]{:S(2)}) %collective-permute-start.24) | collective-permute-done | bytes 327712 | tf_op jit(solution)/shard_map/ppermute | solution.py:196
  165.5 1.0 pad_maximum_fusion.12
  166.5 0.7 copy-done.7
  167.3 1.0 copy-done.18
  168.2 1.0 copy-done.20
  169.7 1.2 slice.114
  170.9 1.1 slice.115
  172.0 0.6 collective-permute-start.31
  172.6 1.3 fusion.39
  174.4 3.2 %collective-permute-start.28 = (bf16[64,8192]{1,0:T(8,128)(2,1)S(1)}, bf16[64,8192]{1,0:T(8,128)(2,1)S(1)}, u32[]{:S(2)}, u32[]{:S(2)}) collective-permute-start(bf16[64,8192]{1,0:T(8,128)(2,1)S(1)} %get-tuple-element.122), channel_id=1, source_target_pairs={{0,6},{1,7},{2,0},{3,1},{4,2},{5,3},{6,4},{7,5},{8,14},{9,15},{10,... | collective-permute-start | bytes 3145736 | tf_op jit(solution)/shard_map/ppermute | solution.py:199
  177.6 2.3 %put.7.refs_0_ = bf16[32,256,640]{2,1,0:T(8,128)(2,1)S(1)} custom-call(s32[16]{0:T(128)S(1)} %stack.286.places, bf16[512,640]{1,0:T(8,128)(2,1)S(1)} %copy-done.4, bf16[512,640]{1,0:T(8,128)(2,1)S(1)} %copy-done.2, bf16[512,640]{1,0:T(8,128)(2,1)S(1)} %collective-permute-done.1.refs_2_, bf16[512,640]{1,0:T(8,128)(2,1)S(1)} %collective-permute-done.14.refs_3_, ...), custom_call_target="tpu_custom_call" | custom-call | bytes 256 | tf_op jit(solution)/shard_map/put/pallas_call | solution.py:236
  180.0 4.9 %put.8 = bf16[32,256,640]{2,1,0:T(8,128)(2,1)S(1)} custom-call(s32[16]{0:T(128)S(1)} %stack.269.places, bf16[32,256,640]{2,1,0:T(8,128)(2,1)S(1)} %put.7.refs_0_, bf16[3584,640]{1,0:T(8,128)(2,1)} %collective-permute-done.30.refs_1_, bf16[512,640]{1,0:T(8,128)(2,1)S(1)} %bitcast.118), custom_call_target="tpu_custom_call", output_to_operand_aliasing={{}: (1, {})} | custom-call | bytes 256 | tf_op jit(solution)/shard_map/put/pallas_call | solution.py:236
  184.9 4.7 %fusion.15.refs_0_ = bf16[256,640]{1,0:T(8,128)(2,1)S(1)} fusion(bf16[8192,640]{1,0:T(8,128)(2,1)S(1)} %bitcast.112, bf16[64,8192]{1,0:T(8,128)(2,1)} %collective-permute-done.21, bf16[64,8192]{1,0:T(8,128)(2,1)S(1)} %copy-done.21, bf16[64,8192]{1,0:T(8,128)(2,1)S(1)} %copy-done.19, bf16[64,8192]{1,0:T(8,128)(2,1)S(1)} %copy-done.12), kind=kOutput, calls=%fused_computation.21 | convolution fusion | flops 2701295616 | bytes 15007744 | tf_op jit(solution)/shard_map/dot_general | solution.py:473
  189.7 9.7 %collective-permute-done.29 = bf16[64,8192]{1,0:T(8,128)(2,1)S(1)} collective-permute-done((bf16[64,8192]{1,0:T(8,128)(2,1)S(1)}, bf16[64,8192]{1,0:T(8,128)(2,1)S(1)}, u32[]{:S(2)}, u32[]{:S(2)}) %collective-permute-start.29) | collective-permute-done | bytes 1048608 | tf_op jit(solution)/shard_map/ppermute | solution.py:202
  199.4 1.3 collective-permute-done.27
  200.8 1.7 collective-permute-start.35
  203.3 2.8 %collective-permute-start.33 = (bf16[16,8192]{1,0:T(8,128)(2,1)S(1)}, bf16[16,8192]{1,0:T(8,128)(2,1)S(1)}, u32[]{:S(2)}, u32[]{:S(2)}) collective-permute-start(bf16[16,8192]{1,0:T(8,128)(2,1)S(1)} %slice.119), channel_id=1, source_target_pairs={{0,6},{1,7},{2,0},{3,1},{4,2},{5,3},{6,4},{7,5},{8,14},{9,15},{10,... | collective-permute-start | bytes 786440 | tf_op jit(solution)/shard_map/ppermute | solution.py:199
  206.1 2.7 %fusion.18.refs_1_ = bf16[192,640]{1,0:T(8,128)(2,1)S(1)} fusion(bf16[8192,640]{1,0:T(8,128)(2,1)S(1)} %bitcast.113, bf16[64,8192]{1,0:T(8,128)(2,1)S(1)} %collective-permute-done.28, bf16[64,8192]{1,0:T(8,128)(2,1)S(1)} %collective-permute-done.27, bf16[64,8192]{1,0:T(8,128)(2,1)S(1)} %collective-permute-done.29), kind=kOutput, calls=%fused_computation.22 | convolution fusion | flops 2022825984 | bytes 13877248 | tf_op jit(solution)/shard_map/dot_general | solution.py:473
  208.8 1.4 order.1.refs_0_
  210.2 3.6 %collective-permute-done.34 = bf16[16,8192]{1,0:T(8,128)(2,1)S(1)} collective-permute-done((bf16[16,8192]{1,0:T(8,128)(2,1)S(1)}, bf16[16,8192]{1,0:T(8,128)(2,1)S(1)}, u32[]{:S(2)}, u32[]{:S(2)}) %collective-permute-start.34) | collective-permute-done | bytes 262176 | tf_op jit(solution)/shard_map/ppermute | solution.py:202
  213.8 1.9 convolution_convert_fusion.1.refs_1_
  215.7 1.2 put.9
  (144 shorter events, 6.9 us)
Async XLA Ops:
  0.0 33.9 %copy-start.22 = (f32[5120]{0:T(1024)S(1)}, f32[5120]{0:T(1024)}, u32[]{:S(2)}) copy-start(f32[5120]{0:T(1024)} %param.11) | copy-start | bytes 61444
  0.0 34.0 %collective-permute-start.1 = (bf16[512,640]{1,0:T(8,128)(2,1)}, bf16[512,640]{1,0:T(8,128)(2,1)S(1)}, u32[]{:S(2)}, u32[]{:S(2)}) collective-permute-start(bf16[512,640]{1,0:T(8,128)(2,1)} %refs_0_.3), channel_id=1, source_target_pairs={{0,48},{8,56},{16,0},{24,8},{32,16},{40,24},{48,32},{56,40},{64,11... | collective-permute-start | bytes 1966088 | tf_op jit(solution)/shard_map/ppermute | solution.py:199
  3.1 30.9 %collective-permute-start = (bf16[512,640]{1,0:T(8,128)(2,1)}, bf16[512,640]{1,0:T(8,128)(2,1)S(1)}, u32[]{:S(2)}, u32[]{:S(2)}) collective-permute-start(bf16[512,640]{1,0:T(8,128)(2,1)} %refs_0_.3), channel_id=1, source_target_pairs={{0,16},{8,24},{16,32},{24,40},{32,48},{40,56},{48,0},{56,8},{64,80... | collective-permute-start | bytes 1966088 | tf_op jit(solution)/shard_map/ppermute | solution.py:196
  3.1 30.9 %collective-permute-start.3 = (bf16[640,640]{1,0:T(8,128)(2,1)}, bf16[640,640]{1,0:T(8,128)(2,1)S(1)}, u32[]{:S(2)}, u32[]{:S(2)}) collective-permute-start(bf16[640,640]{1,0:T(8,128)(2,1)} %refs_0_.1), channel_id=1, source_target_pairs={{0,2},{1,3},{2,4},{3,5},{4,6},{5,7},{6,0},{7,1},{8,10},{9,11},{10,... | collective-permute-start | bytes 2457608 | tf_op jit(solution)/shard_map/ppermute | solution.py:196
  5.0 29.0 %collective-permute-start.2 = (bf16[640,640]{1,0:T(8,128)(2,1)}, bf16[640,640]{1,0:T(8,128)(2,1)}, u32[]{:S(2)}, u32[]{:S(2)}) collective-permute-start(bf16[640,640]{1,0:T(8,128)(2,1)} %refs_0_.1), channel_id=1, source_target_pairs={{0,1},{1,0},{2,3},{3,2},{4,5},{5,4},{6,7},{7,6},{8,9},{9,8},{10,11... | collective-permute-start | bytes 2457608 | tf_op jit(solution)/shard_map/ppermute | solution.py:202
  6.5 27.5 %collective-permute-start.4 = (bf16[640,640]{1,0:T(8,128)(2,1)}, bf16[640,640]{1,0:T(8,128)(2,1)}, u32[]{:S(2)}, u32[]{:S(2)}) collective-permute-start(bf16[640,640]{1,0:T(8,128)(2,1)} %refs_0_.1), channel_id=1, source_target_pairs={{0,6},{1,7},{2,0},{3,1},{4,2},{5,3},{6,4},{7,5},{8,14},{9,15},{10,... | collective-permute-start | bytes 2457608 | tf_op jit(solution)/shard_map/ppermute | solution.py:199
  8.6 25.0 %all-to-all-start = ((bf16[8,64,640]{2,1,0:T(8,128)(2,1)}), bf16[8,64,640]{2,1,0:T(8,128)(2,1)S(1)}, u32[]{:S(2)}, u32[]{:S(2)}) async-start(bf16[8,64,640]{2,1,0:T(8,128)(2,1)} %bitcast.146), calls=%async_computation | async-start | bytes 1310720 | tf_op jit(solution)/shard_map/all_to_all | solution.py:320
  34.0 94.8 %copy-start = (bf16[512,640]{1,0:T(8,128)(2,1)}, bf16[512,640]{1,0:T(8,128)(2,1)S(1)}, u32[]{:S(2)}) copy-start(bf16[512,640]{1,0:T(8,128)(2,1)S(1)} %collective-permute-done.refs_1_) | copy-start | bytes 1966084
  34.0 23.3 %collective-permute-start.6 = (bf16[640,640]{1,0:T(8,128)(2,1)}, bf16[640,640]{1,0:T(8,128)(2,1)S(1)}, u32[]{:S(2)}, u32[]{:S(2)}) collective-permute-start(bf16[640,640]{1,0:T(8,128)(2,1)} %collective-permute-done.2.refs_3_), channel_id=1, source_target_pairs={{0,6},{1,7},{2,0},{3,1},{4,2},{5,3},{6,4},{7,5},{8,14},{9,15},{10,... | collective-permute-start | bytes 2457608 | tf_op jit(solution)/shard_map/ppermute | solution.py:199
  36.9 20.4 %collective-permute-start.5 = (bf16[640,640]{1,0:T(8,128)(2,1)}, bf16[640,640]{1,0:T(8,128)(2,1)S(1)}, u32[]{:S(2)}, u32[]{:S(2)}) collective-permute-start(bf16[640,640]{1,0:T(8,128)(2,1)} %collective-permute-done.2.refs_3_), channel_id=1, source_target_pairs={{0,2},{1,3},{2,4},{3,5},{4,6},{5,7},{6,0},{7,1},{8,10},{9,11},{10,... | collective-permute-start | bytes 2457608 | tf_op jit(solution)/shard_map/ppermute | solution.py:196
  37.2 15.4 %collective-permute-start.9 = (bf16[64,5120]{1,0:T(8,128)(2,1)S(1)}, bf16[64,5120]{1,0:T(8,128)(2,1)S(1)}, u32[]{:S(2)}, u32[]{:S(2)}) collective-permute-start(bf16[64,5120]{1,0:T(8,128)(2,1)S(1)} %multiply_convert_fusion), channel_id=1, source_target_pairs={{0,64},{8,72},{16,80},{24,88},{32,96},{40,104},{48,112},{56,120},{... | collective-permute-start | bytes 1966088 | tf_op jit(solution)/shard_map/ppermute | solution.py:202
  40.0 15.6 %collective-permute-start.8 = (bf16[64,5120]{1,0:T(8,128)(2,1)S(1)}, bf16[64,5120]{1,0:T(8,128)(2,1)S(1)}, u32[]{:S(2)}, u32[]{:S(2)}) collective-permute-start(bf16[64,5120]{1,0:T(8,128)(2,1)S(1)} %multiply_convert_fusion), channel_id=1, source_target_pairs={{0,48},{8,56},{16,0},{24,8},{32,16},{40,24},{48,32},{56,40},{64,11... | collective-permute-start | bytes 1966088 | tf_op jit(solution)/shard_map/ppermute | solution.py:199
  42.9 14.4 %collective-permute-start.7 = (bf16[64,5120]{1,0:T(8,128)(2,1)S(1)}, bf16[64,5120]{1,0:T(8,128)(2,1)S(1)}, u32[]{:S(2)}, u32[]{:S(2)}) collective-permute-start(bf16[64,5120]{1,0:T(8,128)(2,1)S(1)} %multiply_convert_fusion), channel_id=1, source_target_pairs={{0,16},{8,24},{16,32},{24,40},{32,48},{40,56},{48,0},{56,8},{64,80... | collective-permute-start | bytes 1966088 | tf_op jit(solution)/shard_map/ppermute | solution.py:196
  42.9 9.6 %copy-start.3 = (bf16[512,640]{1,0:T(8,128)(2,1)S(1)}, bf16[512,640]{1,0:T(8,128)(2,1)}, u32[]{:S(2)}) copy-start(bf16[512,640]{1,0:T(8,128)(2,1)} %refs_0_.3) | copy-start | bytes 1966084
  52.6 16.9 %collective-permute-start.14 = (bf16[512,640]{1,0:T(8,128)(2,1)S(1)}, bf16[512,640]{1,0:T(8,128)(2,1)S(1)}, u32[]{:S(2)}, u32[]{:S(2)}) collective-permute-start(bf16[512,640]{1,0:T(8,128)(2,1)S(1)} %copy-done.3), channel_id=1, source_target_pairs={{0,64},{8,72},{16,80},{24,88},{32,96},{40,104},{48,112},{56,120},{... | collective-permute-start | bytes 1966088 | tf_op jit(solution)/shard_map/ppermute | solution.py:202
  57.5 8.2 %copy-start.13 = (bf16[640,640]{1,0:T(8,128)(2,1)S(1)}, bf16[640,640]{1,0:T(8,128)(2,1)}, u32[]{:S(2)}) copy-start(bf16[640,640]{1,0:T(8,128)(2,1)} %refs_0_.1) | copy-start | bytes 2457604
  57.7 15.9 %collective-permute-start.11 = (bf16[640,640]{1,0:T(8,128)(2,1)S(1)}, bf16[640,640]{1,0:T(8,128)(2,1)S(1)}, u32[]{:S(2)}, u32[]{:S(2)}) collective-permute-start(bf16[640,640]{1,0:T(8,128)(2,1)S(1)} %pad_maximum_fusion.10), channel_id=1, source_target_pairs={{0,6},{1,7},{2,0},{3,1},{4,2},{5,3},{6,4},{7,5},{8,14},{9,15},{10,... | collective-permute-start | bytes 2457608 | tf_op jit(solution)/shard_map/ppermute | solution.py:199
  60.6 16.3 %collective-permute-start.10 = (bf16[640,640]{1,0:T(8,128)(2,1)S(1)}, bf16[640,640]{1,0:T(8,128)(2,1)S(1)}, u32[]{:S(2)}, u32[]{:S(2)}) collective-permute-start(bf16[640,640]{1,0:T(8,128)(2,1)S(1)} %pad_maximum_fusion.9), channel_id=1, source_target_pairs={{0,2},{1,3},{2,4},{3,5},{4,6},{5,7},{6,0},{7,1},{8,10},{9,11},{10,... | collective-permute-start | bytes 2457608 | tf_op jit(solution)/shard_map/ppermute | solution.py:196
  60.9 19.8 %collective-permute-start.13 = (bf16[96,5120]{1,0:T(8,128)(2,1)S(1)}, bf16[96,5120]{1,0:T(8,128)(2,1)S(1)}, u32[]{:S(2)}, u32[]{:S(2)}) collective-permute-start(bf16[96,5120]{1,0:T(8,128)(2,1)S(1)} %get-tuple-element.118), channel_id=1, source_target_pairs={{0,48},{8,56},{16,0},{24,8},{32,16},{40,24},{48,32},{56,40},{64,11... | collective-permute-start | bytes 2949128 | tf_op jit(solution)/shard_map/ppermute | solution.py:199
  61.9 21.4 %collective-permute-start.12 = (bf16[96,5120]{1,0:T(8,128)(2,1)S(1)}, bf16[96,5120]{1,0:T(8,128)(2,1)S(1)}, u32[]{:S(2)}, u32[]{:S(2)}) collective-permute-start(bf16[96,5120]{1,0:T(8,128)(2,1)S(1)} %get-tuple-element.119), channel_id=1, source_target_pairs={{0,16},{8,24},{16,32},{24,40},{32,48},{40,56},{48,0},{56,8},{64,80... | collective-permute-start | bytes 2949128 | tf_op jit(solution)/shard_map/ppermute | solution.py:196
  65.7 19.9 %slice-start = ((s8[10485760]{0:T(1024)(128)(4,1)}), s8[4194304]{0:T(1024)(128)(4,1)S(1)}, s32[]{:S(2)}) async-start(s8[10485760]{0:T(1024)(128)(4,1)} %bitcast.121), calls=%async_computation.2 | async-start | bytes 8388608
  65.7 19.9 %slice-start.1 = ((s8[10485760]{0:T(1024)(128)(4,1)}), s8[4194304]{0:T(1024)(128)(4,1)S(1)}, s32[]{:S(2)}) async-start(s8[10485760]{0:T(1024)(128)(4,1)} %bitcast.121), calls=%async_computation.3 | async-start | bytes 8388608
  69.1 16.5 %slice-start.2 = ((s8[10485760]{0:T(1024)(128)(4,1)}), s8[2097152]{0:T(1024)(128)(4,1)S(1)}, s32[]{:S(2)}) async-start(s8[10485760]{0:T(1024)(128)(4,1)} %bitcast.121), calls=%async_computation.4 | async-start | bytes 4194304
  83.5 7.1 %collective-permute-start.16 = (bf16[32,5120]{1,0:T(8,128)(2,1)S(1)}, bf16[32,5120]{1,0:T(8,128)(2,1)S(1)}, u32[]{:S(2)}, u32[]{:S(2)}) collective-permute-start(bf16[32,5120]{1,0:T(8,128)(2,1)S(1)} %slice.105), channel_id=1, source_target_pairs={{0,48},{8,56},{16,0},{24,8},{32,16},{40,24},{48,32},{56,40},{64,11... | collective-permute-start | bytes 983048 | tf_op jit(solution)/shard_map/ppermute | solution.py:199
  83.9 8.3 %collective-permute-start.15 = (bf16[32,5120]{1,0:T(8,128)(2,1)S(1)}, bf16[32,5120]{1,0:T(8,128)(2,1)S(1)}, u32[]{:S(2)}, u32[]{:S(2)}) collective-permute-start(bf16[32,5120]{1,0:T(8,128)(2,1)S(1)} %slice.104), channel_id=1, source_target_pairs={{0,16},{8,24},{16,32},{24,40},{32,48},{40,56},{48,0},{56,8},{64,80... | collective-permute-start | bytes 983048 | tf_op jit(solution)/shard_map/ppermute | solution.py:196
  86.0 6.6 %collective-permute-start.17 = (bf16[2,96,5120]{2,1,0:T(8,128)(2,1)S(1)}, bf16[2,96,5120]{2,1,0:T(8,128)(2,1)S(1)}, u32[]{:S(2)}, u32[]{:S(2)}) collective-permute-start(bf16[2,96,5120]{2,1,0:T(8,128)(2,1)S(1)} %pad_maximum_fusion.1), channel_id=1, source_target_pairs={{0,8},{8,0},{16,24},{24,16},{32,40},{40,32},{48,56},{56,48},{64,72... | collective-permute-start | bytes 5898248 | tf_op jit(solution)/shard_map/ppermute | solution.py:205
  86.1 8.7 %collective-permute-start.19 = (bf16[4,64,5120]{2,1,0:T(8,128)(2,1)S(1)}, bf16[4,64,5120]{2,1,0:T(8,128)(2,1)S(1)}, u32[]{:S(2)}, u32[]{:S(2)}) collective-permute-start(bf16[4,64,5120]{2,1,0:T(8,128)(2,1)S(1)} %pad_maximum_fusion), channel_id=1, source_target_pairs={{0,8},{8,0},{16,24},{24,16},{32,40},{40,32},{48,56},{56,48},{64,72... | collective-permute-start | bytes 7864328 | tf_op jit(solution)/shard_map/ppermute | solution.py:205
  92.2 2.5 %collective-permute-start.18 = (bf16[2,32,5120]{2,1,0:T(8,128)(2,1)S(1)}, bf16[2,32,5120]{2,1,0:T(8,128)(2,1)S(1)}, u32[]{:S(2)}, u32[]{:S(2)}) collective-permute-start(bf16[2,32,5120]{2,1,0:T(8,128)(2,1)S(1)} %pad_maximum_fusion.11), channel_id=1, source_target_pairs={{0,8},{8,0},{16,24},{24,16},{32,40},{40,32},{48,56},{56,48},{64,72... | collective-permute-start | bytes 1966088 | tf_op jit(solution)/shard_map/ppermute | solution.py:205
  103.5 27.6 %copy-start.5 = (bf16[4,256,1024]{2,1,0:T(8,128)(2,1)S(1)}, bf16[4,256,1024]{2,1,0:T(8,128)(2,1)}, u32[]{:S(2)}) copy-start(bf16[4,256,1024]{2,1,0:T(8,128)(2,1)} %keys.1) | copy-start | bytes 6291460
  103.5 27.6 %copy-start.6 = (bf16[4,256,1024]{2,1,0:T(8,128)(2,1)S(1)}, bf16[4,256,1024]{2,1,0:T(8,128)(2,1)}, u32[]{:S(2)}) copy-start(bf16[4,256,1024]{2,1,0:T(8,128)(2,1)} %values.1) | copy-start | bytes 6291460
  103.5 27.6 %copy-start.14 = (s32[4]{0:T(128)S(1)}, s32[4]{0:T(128)}, u32[]{:S(2)}) copy-start(s32[4]{0:T(128)} %fills.1) | copy-start | bytes 52
  103.6 27.6 %copy-start.15 = (s32[4]{0:T(128)S(1)}, s32[4]{0:T(128)}, u32[]{:S(2)}) copy-start(s32[4]{0:T(128)} %spans.1) | copy-start | bytes 52
  103.6 27.6 %copy-start.16 = (f32[128]{0:T(128)S(1)}, f32[128]{0:T(128)}, u32[]{:S(2)}) copy-start(f32[128]{0:T(128)} %param.13) | copy-start | bytes 1540
  103.6 27.6 %copy-start.17 = (f32[128]{0:T(128)S(1)}, f32[128]{0:T(128)}, u32[]{:S(2)}) copy-start(f32[128]{0:T(128)} %param.14) | copy-start | bytes 1540
  128.9 26.7 %copy-start.1 = (bf16[512,640]{1,0:T(8,128)(2,1)S(1)}, bf16[512,640]{1,0:T(8,128)(2,1)}, u32[]{:S(2)}) copy-start(bf16[512,640]{1,0:T(8,128)(2,1)} %copy-done) | copy-start | bytes 1966084
  129.1 23.3 %collective-permute-start.25 = (bf16[768,640]{1,0:T(8,128)(2,1)S(1)}, bf16[768,640]{1,0:T(8,128)(2,1)S(1)}, u32[]{:S(2)}, u32[]{:S(2)}) collective-permute-start(bf16[768,640]{1,0:T(8,128)(2,1)S(1)} %get-tuple-element.116), channel_id=1, source_target_pairs={{0,48},{8,56},{16,0},{24,8},{32,16},{40,24},{48,32},{56,40},{64,11... | collective-permute-start | bytes 2949128 | tf_op jit(solution)/shard_map/ppermute | solution.py:199
  130.1 25.3 %collective-permute-start.23 = (bf16[768,640]{1,0:T(8,128)(2,1)S(1)}, bf16[768,640]{1,0:T(8,128)(2,1)S(1)}, u32[]{:S(2)}, u32[]{:S(2)}) collective-permute-start(bf16[768,640]{1,0:T(8,128)(2,1)S(1)} %get-tuple-element.117), channel_id=1, source_target_pairs={{0,16},{8,24},{16,32},{24,40},{32,48},{40,56},{48,0},{56,8},{64,80... | collective-permute-start | bytes 2949128 | tf_op jit(solution)/shard_map/ppermute | solution.py:196
  139.1 28.2 %copy-start.11 = (bf16[64,8192]{1,0:T(8,128)(2,1)}, bf16[64,8192]{1,0:T(8,128)(2,1)S(1)}, u32[]{:S(2)}) copy-start(bf16[64,8192]{1,0:T(8,128)(2,1)S(1)} %attend.1) | copy-start | bytes 3145732
  139.1 28.1 %collective-permute-start.22 = (bf16[64,8192]{1,0:T(8,128)(2,1)S(1)}, bf16[64,8192]{1,0:T(8,128)(2,1)S(1)}, u32[]{:S(2)}, u32[]{:S(2)}) collective-permute-start(bf16[64,8192]{1,0:T(8,128)(2,1)S(1)} %attend.1), channel_id=1, source_target_pairs={{0,1},{1,0},{2,3},{3,2},{4,5},{5,4},{6,7},{7,6},{8,9},{9,8},{10,11... | collective-permute-start | bytes 3145736 | tf_op jit(solution)/shard_map/ppermute | solution.py:202
  139.2 28.1 %collective-permute-start.21 = (bf16[64,8192]{1,0:T(8,128)(2,1)S(1)}, bf16[64,8192]{1,0:T(8,128)(2,1)}, u32[]{:S(2)}, u32[]{:S(2)}) collective-permute-start(bf16[64,8192]{1,0:T(8,128)(2,1)S(1)} %attend.1), channel_id=1, source_target_pairs={{0,6},{1,7},{2,0},{3,1},{4,2},{5,3},{6,4},{7,5},{8,14},{9,15},{10,... | collective-permute-start | bytes 3145736 | tf_op jit(solution)/shard_map/ppermute | solution.py:199
  141.7 25.6 %collective-permute-start.20 = (bf16[64,8192]{1,0:T(8,128)(2,1)S(1)}, bf16[64,8192]{1,0:T(8,128)(2,1)S(1)}, u32[]{:S(2)}, u32[]{:S(2)}) collective-permute-start(bf16[64,8192]{1,0:T(8,128)(2,1)S(1)} %attend.1), channel_id=1, source_target_pairs={{0,2},{1,3},{2,4},{3,5},{4,6},{5,7},{6,0},{7,1},{8,10},{9,11},{10,... | collective-permute-start | bytes 3145736 | tf_op jit(solution)/shard_map/ppermute | solution.py:196
  152.4 9.7 %collective-permute-start.26 = (bf16[256,640]{1,0:T(8,128)(2,1)S(1)}, bf16[256,640]{1,0:T(8,128)(2,1)S(1)}, u32[]{:S(2)}, u32[]{:S(2)}) collective-permute-start(bf16[256,640]{1,0:T(8,128)(2,1)S(1)} %slice.127), channel_id=1, source_target_pairs={{0,48},{8,56},{16,0},{24,8},{32,16},{40,24},{48,32},{56,40},{64,11... | collective-permute-start | bytes 983048 | tf_op jit(solution)/shard_map/ppermute | solution.py:199
  155.4 10.1 %collective-permute-start.24 = (bf16[256,640]{1,0:T(8,128)(2,1)S(1)}, bf16[256,640]{1,0:T(8,128)(2,1)S(1)}, u32[]{:S(2)}, u32[]{:S(2)}) collective-permute-start(bf16[256,640]{1,0:T(8,128)(2,1)S(1)} %slice.126), channel_id=1, source_target_pairs={{0,16},{8,24},{16,32},{24,40},{32,48},{40,56},{48,0},{56,8},{64,80... | collective-permute-start | bytes 983048 | tf_op jit(solution)/shard_map/ppermute | solution.py:196
  165.5 1.0 copy-start.9
  166.5 0.7 copy-start.7
  167.2 1.0 copy-start.18
  168.2 1.0 copy-start.20
  169.3 10.7 %collective-permute-start.30 = (bf16[3584,640]{1,0:T(8,128)(2,1)}, bf16[3584,640]{1,0:T(8,128)(2,1)}, u32[]{:S(2)}, u32[]{:S(2)}) collective-permute-start(bf16[3584,640]{1,0:T(8,128)(2,1)} %pack.1), channel_id=1, source_target_pairs={{0,8},{8,0},{16,24},{24,16},{32,40},{40,32},{48,56},{56,48},{64,72... | collective-permute-start | bytes 13762568 | tf_op jit(solution)/shard_map/ppermute | solution.py:205
  169.6 8.0 %copy-start.2 = (bf16[512,640]{1,0:T(8,128)(2,1)S(1)}, bf16[512,640]{1,0:T(8,128)(2,1)}, u32[]{:S(2)}) copy-start(bf16[512,640]{1,0:T(8,128)(2,1)} %copy-done) | copy-start | bytes 1966084
  169.6 8.0 %copy-start.4 = (bf16[512,640]{1,0:T(8,128)(2,1)S(1)}, bf16[512,640]{1,0:T(8,128)(2,1)}, u32[]{:S(2)}) copy-start(bf16[512,640]{1,0:T(8,128)(2,1)} %refs_0_.3) | copy-start | bytes 1966084
  169.6 8.0 %copy-start.8 = (bf16[256,640]{1,0:T(8,128)(2,1)S(1)}, bf16[256,640]{1,0:T(8,128)(2,1)}, u32[]{:S(2)}) copy-start(bf16[256,640]{1,0:T(8,128)(2,1)} %copy-done.7) | copy-start | bytes 983044
  169.7 8.0 %copy-start.10 = (bf16[256,640]{1,0:T(8,128)(2,1)S(1)}, bf16[256,640]{1,0:T(8,128)(2,1)}, u32[]{:S(2)}) copy-start(bf16[256,640]{1,0:T(8,128)(2,1)} %copy-done.9) | copy-start | bytes 983044
  172.0 7.9 %collective-permute-start.31 = (bf16[2,256,640]{2,1,0:T(8,128)(2,1)}, bf16[2,256,640]{2,1,0:T(8,128)(2,1)S(1)}, u32[]{:S(2)}, u32[]{:S(2)}) collective-permute-start(bf16[2,256,640]{2,1,0:T(8,128)(2,1)} %pad_maximum_fusion.12), channel_id=1, source_target_pairs={{0,8},{8,0},{16,24},{24,16},{32,40},{40,32},{48,56},{56,48},{64,72... | collective-permute-start | bytes 1966088 | tf_op jit(solution)/shard_map/ppermute | solution.py:205
  174.2 25.2 %collective-permute-start.29 = (bf16[64,8192]{1,0:T(8,128)(2,1)S(1)}, bf16[64,8192]{1,0:T(8,128)(2,1)S(1)}, u32[]{:S(2)}, u32[]{:S(2)}) collective-permute-start(bf16[64,8192]{1,0:T(8,128)(2,1)S(1)} %get-tuple-element.120), channel_id=1, source_target_pairs={{0,1},{1,0},{2,3},{3,2},{4,5},{5,4},{6,7},{7,6},{8,9},{9,8},{10,11... | collective-permute-start | bytes 3145736 | tf_op jit(solution)/shard_map/ppermute | solution.py:202
  174.3 26.4 %collective-permute-start.27 = (bf16[64,8192]{1,0:T(8,128)(2,1)S(1)}, bf16[64,8192]{1,0:T(8,128)(2,1)S(1)}, u32[]{:S(2)}, u32[]{:S(2)}) collective-permute-start(bf16[64,8192]{1,0:T(8,128)(2,1)S(1)} %get-tuple-element.121), channel_id=1, source_target_pairs={{0,2},{1,3},{2,4},{3,5},{4,6},{5,7},{6,0},{7,1},{8,10},{9,11},{10,... | collective-permute-start | bytes 3145736 | tf_op jit(solution)/shard_map/ppermute | solution.py:196
  174.4 26.3 %collective-permute-start.28 = (bf16[64,8192]{1,0:T(8,128)(2,1)S(1)}, bf16[64,8192]{1,0:T(8,128)(2,1)S(1)}, u32[]{:S(2)}, u32[]{:S(2)}) collective-permute-start(bf16[64,8192]{1,0:T(8,128)(2,1)S(1)} %get-tuple-element.122), channel_id=1, source_target_pairs={{0,6},{1,7},{2,0},{3,1},{4,2},{5,3},{6,4},{7,5},{8,14},{9,15},{10,... | collective-permute-start | bytes 3145736 | tf_op jit(solution)/shard_map/ppermute | solution.py:199
  180.0 5.0 %copy-start.12 = (bf16[64,8192]{1,0:T(8,128)(2,1)S(1)}, bf16[64,8192]{1,0:T(8,128)(2,1)}, u32[]{:S(2)}) copy-start(bf16[64,8192]{1,0:T(8,128)(2,1)} %copy-done.11) | copy-start | bytes 3145732
  180.0 5.0 %copy-start.19 = (bf16[64,8192]{1,0:T(8,128)(2,1)S(1)}, bf16[64,8192]{1,0:T(8,128)(2,1)}, u32[]{:S(2)}) copy-start(bf16[64,8192]{1,0:T(8,128)(2,1)} %copy-done.18) | copy-start | bytes 3145732
  180.0 5.0 %copy-start.21 = (bf16[64,8192]{1,0:T(8,128)(2,1)S(1)}, bf16[64,8192]{1,0:T(8,128)(2,1)}, u32[]{:S(2)}) copy-start(bf16[64,8192]{1,0:T(8,128)(2,1)} %copy-done.20) | copy-start | bytes 3145732
  200.8 9.5 %collective-permute-start.35 = (bf16[16,8192]{1,0:T(8,128)(2,1)S(1)}, bf16[16,8192]{1,0:T(8,128)(2,1)S(1)}, u32[]{:S(2)}, u32[]{:S(2)}) collective-permute-start(bf16[16,8192]{1,0:T(8,128)(2,1)S(1)} %get-tuple-element.111), channel_id=1, source_target_pairs={{0,1},{1,0},{2,3},{3,2},{4,5},{5,4},{6,7},{7,6},{8,9},{9,8},{10,11... | collective-permute-start | bytes 786440 | tf_op jit(solution)/shard_map/ppermute | solution.py:202
  202.5 11.3 %collective-permute-start.34 = (bf16[16,8192]{1,0:T(8,128)(2,1)S(1)}, bf16[16,8192]{1,0:T(8,128)(2,1)S(1)}, u32[]{:S(2)}, u32[]{:S(2)}) collective-permute-start(bf16[16,8192]{1,0:T(8,128)(2,1)S(1)} %get-tuple-element.112), channel_id=1, source_target_pairs={{0,1},{1,0},{2,3},{3,2},{4,5},{5,4},{6,7},{7,6},{8,9},{9,8},{10,11... | collective-permute-start | bytes 786440 | tf_op jit(solution)/shard_map/ppermute | solution.py:202
  202.9 11.0 %collective-permute-start.32 = (bf16[16,8192]{1,0:T(8,128)(2,1)S(1)}, bf16[16,8192]{1,0:T(8,128)(2,1)S(1)}, u32[]{:S(2)}, u32[]{:S(2)}) collective-permute-start(bf16[16,8192]{1,0:T(8,128)(2,1)S(1)} %get-tuple-element.113), channel_id=1, source_target_pairs={{0,2},{1,3},{2,4},{3,5},{4,6},{5,7},{6,0},{7,1},{8,10},{9,11},{10,... | collective-permute-start | bytes 786440 | tf_op jit(solution)/shard_map/ppermute | solution.py:196
  203.3 10.5 %collective-permute-start.33 = (bf16[16,8192]{1,0:T(8,128)(2,1)S(1)}, bf16[16,8192]{1,0:T(8,128)(2,1)S(1)}, u32[]{:S(2)}, u32[]{:S(2)}) collective-permute-start(bf16[16,8192]{1,0:T(8,128)(2,1)S(1)} %slice.119), channel_id=1, source_target_pairs={{0,6},{1,7},{2,0},{3,1},{4,2},{5,3},{6,4},{7,5},{8,14},{9,15},{10,... | collective-permute-start | bytes 786440 | tf_op jit(solution)/shard_map/ppermute | solution.py:199

commit v3 on v2

--- a/solution.py
+++ b/solution.py
@@ -438,6 +438,8 @@
     b_swap = narrow.swap(jnp.concatenate([a_up[:half_rows], a_down[:half_rows]]))
     o_near = wide.cores(o_near)
     other_far = wide.cores(other_far).reshape(out_rows, -1)
+    near_rows = jnp.concatenate([attended, a_swap, a_up, a_down])
+    near_rows, o_near, other_far = barrier((near_rows, o_near, other_far))
     chips = tuple(
         (pair * 4 + wide.ring(ring)) * 2
         for ring, pair in (
@@ -473,7 +475,7 @@
         product = jnp.dot(part, every_w_out, preferred_element_type=jnp.float32)
         return product.astype(jnp.bfloat16)
 
-    near_rows = project_out(jnp.concatenate([attended, a_swap, a_up, a_down]))
+    near_rows = project_out(near_rows)
     b_up, b_down, b_swap, near_rows = barrier((b_up, b_down, b_swap, near_rows))
     c_up = narrow.up(b_up[:quarter])
     c_down = narrow.down(b_down[quarter:half_rows])

time: 217 us -> 215 us (level)
  local copies, waits for them, and re-layouts: 18.4 us -> 15.7 us
    unnamed x52 -> x44, local copies, waits for them, and re-layouts: 2.85 us -> 0.11 us
  transfers between devices with their start and end apart: 37 -> 37, of which waited for: 16 -> 16; matrix products, arithmetic and copies ran while one was open for 12% -> 13% of each run, Pallas kernels for 11% -> 11%
where the time goes in v3:
time: 215 us
  waiting for transfers between devices  75.3 us (35%)
  starting transfers between devices  50 us (23%)
  Pallas kernels  25.4 us (12%)
  blocking collectives  25.2 us (12%)
  matrix products  16.3 us (8%)
  local copies, waits for them, and re-layouts  15.7 us (7%)
  other arithmetic  6.05 us (3%)
    ppermute x12, starting transfers between devices, down(): return lax.ppermute(block, self.axis, self.pairs(-1, 0, 0))  28.3 us
    all_to_all x1, blocking collectives, shards(): lax.all_to_all(projected.reshape(wide_count, rows, -1), 'wide', split_axi...  25.2 us
    ppermute x12, waiting for transfers between devices, down(): return lax.ppermute(block, self.axis, self.pairs(-1, 0, 0))  24.6 us
    all_to_all x1, waiting for transfers between devices, shards(): lax.all_to_all(tokens, 'narrow', split_axis=0, concat_axis=1, tiled=True)  20.1 us
    ppermute x12, waiting for transfers between devices, up(): return lax.ppermute(block, self.axis, self.pairs(1, 0, 0))  14.8 us
    ppermute x7, waiting for transfers between devices, swap(): return lax.ppermute(block, self.axis, self.pairs(0, 1, 0))  13.8 us
    pallas_call x5, Pallas kernels, put(): pl.pallas_call(functools.partial(put_kernel, sources, aliased), grid_spec...  12.4 us
    ppermute x7, starting transfers between devices, swap(): return lax.ppermute(block, self.axis, self.pairs(0, 1, 0))  10.5 us
  transfers between devices with their start and end apart: 37, of which 16 were waited for; matrix products, arithmetic and copies ran while one was open for 13% of the time, Pallas kernels for 11%

profile of v3, /device:TPU:0, one launch (start us, length us, event | category | flops | bytes accessed | tf_op | source)
XLA Modules:
  0.0 214.9 jit_solution(3127072895263723577)
XLA Ops:
  0.0 3.1 %collective-permute-start.1 = (bf16[512,640]{1,0:T(8,128)(2,1)}, bf16[512,640]{1,0:T(8,128)(2,1)S(1)}, u32[]{:S(2)}, u32[]{:S(2)}) collective-permute-start(bf16[512,640]{1,0:T(8,128)(2,1)} %refs_0_.3), channel_id=1, source_target_pairs={{0,48},{8,56},{16,0},{24,8},{32,16},{40,24},{48,32},{56,40},{64,11... | collective-permute-start | bytes 1966088 | tf_op jit(solution)/shard_map/ppermute | solution.py:199
  3.1 1.9 collective-permute-start.3
  5.0 1.5 collective-permute-start.2
  6.5 2.1 collective-permute-start.4
  8.6 3.5 %all-to-all-start = ((bf16[8,64,640]{2,1,0:T(8,128)(2,1)}), bf16[8,64,640]{2,1,0:T(8,128)(2,1)S(1)}, u32[]{:S(2)}, u32[]{:S(2)}) async-start(bf16[8,64,640]{2,1,0:T(8,128)(2,1)} %bitcast.147), calls=%async_computation | async-start | bytes 1310720 | tf_op jit(solution)/shard_map/all_to_all | solution.py:320
  12.2 0.7 add_convert_fusion
  13.5 20.1 %all-to-all-done = bf16[8,64,640]{2,1,0:T(8,128)(2,1)S(1)} async-done(((bf16[8,64,640]{2,1,0:T(8,128)(2,1)}), bf16[8,64,640]{2,1,0:T(8,128)(2,1)S(1)}, u32[]{:S(2)}, u32[]{:S(2)}) %all-to-all-start) | async-done | bytes 655392 | tf_op jit(solution)/shard_map/all_to_all | solution.py:320
  34.0 2.9 %collective-permute-start.6 = (bf16[640,640]{1,0:T(8,128)(2,1)}, bf16[640,640]{1,0:T(8,128)(2,1)S(1)}, u32[]{:S(2)}, u32[]{:S(2)}) collective-permute-start(bf16[640,640]{1,0:T(8,128)(2,1)} %collective-permute-done.2.refs_3_), channel_id=1, source_target_pairs={{0,6},{1,7},{2,0},{3,1},{4,2},{5,3},{6,4},{7,5},{8,14},{9,15},{10,... | collective-permute-start | bytes 2457608 | tf_op jit(solution)/shard_map/ppermute | solution.py:199
  37.2 2.8 %collective-permute-start.9 = (bf16[64,5120]{1,0:T(8,128)(2,1)S(1)}, bf16[64,5120]{1,0:T(8,128)(2,1)S(1)}, u32[]{:S(2)}, u32[]{:S(2)}) collective-permute-start(bf16[64,5120]{1,0:T(8,128)(2,1)S(1)} %multiply_convert_fusion), channel_id=1, source_target_pairs={{0,64},{8,72},{16,80},{24,88},{32,96},{40,104},{48,112},{56,120},{... | collective-permute-start | bytes 1966088 | tf_op jit(solution)/shard_map/ppermute | solution.py:202
  40.0 3.0 %collective-permute-start.8 = (bf16[64,5120]{1,0:T(8,128)(2,1)S(1)}, bf16[64,5120]{1,0:T(8,128)(2,1)S(1)}, u32[]{:S(2)}, u32[]{:S(2)}) collective-permute-start(bf16[64,5120]{1,0:T(8,128)(2,1)S(1)} %multiply_convert_fusion), channel_id=1, source_target_pairs={{0,48},{8,56},{16,0},{24,8},{32,16},{40,24},{48,32},{56,40},{64,11... | collective-permute-start | bytes 1966088 | tf_op jit(solution)/shard_map/ppermute | solution.py:199
  43.0 1.1 slice.96
  44.1 5.3 %broadcast_in_dim.9 = bf16[2,4,2,2,32,5120]{5,4,3,2,1,0:T(8,128)(2,1)} broadcast(bf16[]{:T(256)} %constant.196.clone.1), dimensions={} | broadcast | bytes 10485762 | tf_op jit(solution)/shard_map/broadcast_in_dim | solution.py:335
  49.4 0.9 constant_dynamic-update-slice_fusion.11
  50.4 2.2 %collective-permute-done.9 = bf16[64,5120]{1,0:T(8,128)(2,1)S(1)} collective-permute-done((bf16[64,5120]{1,0:T(8,128)(2,1)S(1)}, bf16[64,5120]{1,0:T(8,128)(2,1)S(1)}, u32[]{:S(2)}, u32[]{:S(2)}) %collective-permute-start.9) | collective-permute-done | bytes 655392 | tf_op jit(solution)/shard_map/ppermute | solution.py:202
  52.6 3.0 %collective-permute-start.14 = (bf16[512,640]{1,0:T(8,128)(2,1)S(1)}, bf16[512,640]{1,0:T(8,128)(2,1)S(1)}, u32[]{:S(2)}, u32[]{:S(2)}) collective-permute-start(bf16[512,640]{1,0:T(8,128)(2,1)S(1)} %copy-done.5), channel_id=1, source_target_pairs={{0,64},{8,72},{16,80},{24,88},{32,96},{40,104},{48,112},{56,120},{... | collective-permute-start | bytes 1966088 | tf_op jit(solution)/shard_map/ppermute | solution.py:202
  55.6 1.8 collective-permute-done.7
  57.7 2.8 %collective-permute-start.11 = (bf16[640,640]{1,0:T(8,128)(2,1)S(1)}, bf16[640,640]{1,0:T(8,128)(2,1)S(1)}, u32[]{:S(2)}, u32[]{:S(2)}) collective-permute-start(bf16[640,640]{1,0:T(8,128)(2,1)S(1)} %pad_maximum_fusion.11), channel_id=1, source_target_pairs={{0,6},{1,7},{2,0},{3,1},{4,2},{5,3},{6,4},{7,5},{8,14},{9,15},{10,... | collective-permute-start | bytes 2457608 | tf_op jit(solution)/shard_map/ppermute | solution.py:199
  60.9 1.0 collective-permute-start.13
  61.9 1.1 collective-permute-start.12
  63.0 0.9 constant_dynamic-update-slice_fusion.10
  63.9 0.9 constant_dynamic-update-slice_fusion.9
  64.8 0.9 constant_dynamic-update-slice_fusion.8
  65.7 3.4 %put.5.refs_0_ = bf16[16,320,640]{2,1,0:T(8,128)(2,1)S(1)} custom-call(s32[12]{0:T(128)S(1)} %stack.240.places, bf16[640,640]{1,0:T(8,128)(2,1)S(1)} %copy-done.13, bf16[640,640]{1,0:T(8,128)(2,1)S(1)} %collective-permute-done.3.refs_1_, bf16[640,640]{1,0:T(8,128)(2,1)} %collective-permute-done.4.refs_2_, bf16[640,640]{1,0:T(8,128)(2,1)} %collective-permute-done.2.refs_3_, ...), custom_call_target="tpu_custom_call" | custom-call | bytes 320 | tf_op jit(solution)/shard_map/put/pallas_call | solution.py:236
  69.5 4.1 %collective-permute-done.11.refs_2_ = bf16[640,640]{1,0:T(8,128)(2,1)S(1)} collective-permute-done((bf16[640,640]{1,0:T(8,128)(2,1)S(1)}, bf16[640,640]{1,0:T(8,128)(2,1)S(1)}, u32[]{:S(2)}, u32[]{:S(2)}) %collective-permute-start.11) | collective-permute-done | bytes 819232 | tf_op jit(solution)/shard_map/ppermute | solution.py:199
  73.5 3.4 %collective-permute-done.10.refs_1_ = bf16[640,640]{1,0:T(8,128)(2,1)S(1)} collective-permute-done((bf16[640,640]{1,0:T(8,128)(2,1)S(1)}, bf16[640,640]{1,0:T(8,128)(2,1)S(1)}, u32[]{:S(2)}, u32[]{:S(2)}) %collective-permute-start.10) | collective-permute-done | bytes 819232 | tf_op jit(solution)/shard_map/ppermute | solution.py:196
  76.9 3.7 %collective-permute-done.13 = bf16[96,5120]{1,0:T(8,128)(2,1)S(1)} collective-permute-done((bf16[96,5120]{1,0:T(8,128)(2,1)S(1)}, bf16[96,5120]{1,0:T(8,128)(2,1)S(1)}, u32[]{:S(2)}, u32[]{:S(2)}) %collective-permute-start.13) | collective-permute-done | bytes 983072 | tf_op jit(solution)/shard_map/ppermute | solution.py:199
  80.7 2.7 %collective-permute-done.12 = bf16[96,5120]{1,0:T(8,128)(2,1)S(1)} collective-permute-done((bf16[96,5120]{1,0:T(8,128)(2,1)S(1)}, bf16[96,5120]{1,0:T(8,128)(2,1)S(1)}, u32[]{:S(2)}, u32[]{:S(2)}) %collective-permute-start.12) | collective-permute-done | bytes 983072 | tf_op jit(solution)/shard_map/ppermute | solution.py:196
  83.9 1.7 collective-permute-start.15
  86.6 0.8 put.6
  87.4 3.2 %collective-permute-done.16 = bf16[32,5120]{1,0:T(8,128)(2,1)S(1)} collective-permute-done((bf16[32,5120]{1,0:T(8,128)(2,1)S(1)}, bf16[32,5120]{1,0:T(8,128)(2,1)S(1)}, u32[]{:S(2)}, u32[]{:S(2)}) %collective-permute-start.16) | collective-permute-done | bytes 327712 | tf_op jit(solution)/shard_map/ppermute | solution.py:199
  90.6 1.5 collective-permute-done.15
  92.9 1.9 collective-permute-done.18
  95.3 8.3 %convolution_convert_fusion = bf16[1024,640]{1,0:T(8,128)(2,1)S(1)} fusion(bf16[1024,5120]{1,0:T(8,128)(2,1)S(1)} %bitcast.124, bf16[5120,640]{1,0:T(8,128)(2,1)S(1)} %bitcast.116), kind=kOutput, calls=%fused_computation.11 | convolution fusion | flops 6711541760 | bytes 18350080 | tf_op jit(solution)/shard_map/dot_general | solution.py:394
  103.6 25.2 %all_to_all.18.packed = bf16[16,64,640]{2,1,0:T(8,128)(2,1)S(1)} all-to-all(bf16[16,64,640]{2,1,0:T(8,128)(2,1)S(1)} %bitcast.144), channel_id=1, replica_groups=mesh['wide'=16,'narrow'=8] {'wide'}, dimensions={0} | all-to-all | bytes 2621440 | tf_op jit(solution)/shard_map/all_to_all | solution.py:395
  129.1 1.1 collective-permute-start.25
  130.1 1.0 collective-permute-start.23
  131.2 7.9 %attend.1 = bf16[64,8192]{1,0:T(8,128)(2,1)S(1)} custom-call(s32[4]{0:T(128)S(1)} %copy-done.14, s32[4]{0:T(128)S(1)} %copy-done.15, bf16[16,64,640]{2,1,0:T(8,128)(2,1)S(1)} %all_to_all.18.packed, f32[64,128]{1,0:T(8,128)S(1)} %broadcast_in_dim.8.inverse, f32[64,128]{1,0:T(8,128)S(1)} %get-tuple-element.82.cosine, f32[64,128]{1,0:T(8,128)S(1)} %get-tuple-element.83.sine, ...), custom_call_target="tpu_custom_call" | custom-call | flops 570425344 | bytes 6553600 | tf_op jit(solution)/shard_map/attend/pallas_call | solution.py:137
  139.2 2.5 %collective-permute-start.21 = (bf16[64,8192]{1,0:T(8,128)(2,1)S(1)}, bf16[64,8192]{1,0:T(8,128)(2,1)}, u32[]{:S(2)}, u32[]{:S(2)}) collective-permute-start(bf16[64,8192]{1,0:T(8,128)(2,1)S(1)} %attend.1), channel_id=1, source_target_pairs={{0,6},{1,7},{2,0},{3,1},{4,2},{5,3},{6,4},{7,5},{8,14},{9,15},{10,... | collective-permute-start | bytes 3145736 | tf_op jit(solution)/shard_map/ppermute | solution.py:199
  141.7 10.6 %collective-permute-done.25.refs_5_ = bf16[768,640]{1,0:T(8,128)(2,1)S(1)} collective-permute-done((bf16[768,640]{1,0:T(8,128)(2,1)S(1)}, bf16[768,640]{1,0:T(8,128)(2,1)S(1)}, u32[]{:S(2)}, u32[]{:S(2)}) %collective-permute-start.25) | collective-permute-done | bytes 983072 | tf_op jit(solution)/shard_map/ppermute | solution.py:199
  152.4 3.0 %collective-permute-start.26 = (bf16[256,640]{1,0:T(8,128)(2,1)S(1)}, bf16[256,640]{1,0:T(8,128)(2,1)S(1)}, u32[]{:S(2)}, u32[]{:S(2)}) collective-permute-start(bf16[256,640]{1,0:T(8,128)(2,1)S(1)} %slice.127), channel_id=1, source_target_pairs={{0,48},{8,56},{16,0},{24,8},{32,16},{40,24},{48,32},{56,40},{64,11... | collective-permute-start | bytes 983048 | tf_op jit(solution)/shard_map/ppermute | solution.py:199
  155.5 3.7 %pack.1 = bf16[3584,640]{1,0:T(8,128)(2,1)} custom-call(bf16[512,640]{1,0:T(8,128)(2,1)S(1)} %copy-done.5, bf16[512,640]{1,0:T(8,128)(2,1)S(1)} %copy-done.3, bf16[512,640]{1,0:T(8,128)(2,1)S(1)} %collective-permute-done.1.refs_2_, bf16[512,640]{1,0:T(8,128)(2,1)S(1)} %collective-permute-done.14.refs_3_, ...), custom_call_target="tpu_custom_call" | custom-call | bytes 3584 | tf_op jit(solution)/shard_map/pack/pallas_call | solution.py:287
  159.2 2.9 %collective-permute-done.26.refs_7_ = bf16[256,640]{1,0:T(8,128)(2,1)S(1)} collective-permute-done((bf16[256,640]{1,0:T(8,128)(2,1)S(1)}, bf16[256,640]{1,0:T(8,128)(2,1)S(1)}, u32[]{:S(2)}, u32[]{:S(2)}) %collective-permute-start.26) | collective-permute-done | bytes 327712 | tf_op jit(solution)/shard_map/ppermute | solution.py:199
  162.1 3.5 %collective-permute-done.24.refs_6_ = bf16[256,640]{1,0:T(8,128)(2,1)S(1)} collective-permute-done((bf16[256,640]{1,0:T(8,128)(2,1)S(1)}, bf16[256,640]{1,0:T(8,128)(2,1)S(1)}, u32[]{:S(2)}, u32[]{:S(2)}) %collective-permute-start.24) | collective-permute-done | bytes 327712 | tf_op jit(solution)/shard_map/ppermute | solution.py:196
  165.6 0.9 pad_maximum_fusion.13
  167.4 1.1 slice.114
  168.6 1.1 slice.115
  169.7 0.5 collective-permute-start.31
  170.2 1.3 fusion.27
  171.8 1.1 collective-permute-start.29
  172.9 3.2 %collective-permute-start.28 = (bf16[64,8192]{1,0:T(8,128)(2,1)S(1)}, bf16[64,8192]{1,0:T(8,128)(2,1)S(1)}, u32[]{:S(2)}, u32[]{:S(2)}) collective-permute-start(bf16[64,8192]{1,0:T(8,128)(2,1)S(1)} %get-tuple-element.128), channel_id=1, source_target_pairs={{0,6},{1,7},{2,0},{3,1},{4,2},{5,3},{6,4},{7,5},{8,14},{9,15},{10,... | collective-permute-start | bytes 3145736 | tf_op jit(solution)/shard_map/ppermute | solution.py:199
  176.2 2.1 pad_maximum_fusion
  178.3 2.3 %put.7.refs_0_ = bf16[32,256,640]{2,1,0:T(8,128)(2,1)S(1)} custom-call(s32[16]{0:T(128)S(1)} %stack.286.places, bf16[512,640]{1,0:T(8,128)(2,1)S(1)} %copy-done.6, bf16[512,640]{1,0:T(8,128)(2,1)S(1)} %copy-done.4, bf16[512,640]{1,0:T(8,128)(2,1)S(1)} %collective-permute-done.1.refs_2_, bf16[512,640]{1,0:T(8,128)(2,1)S(1)} %collective-permute-done.14.refs_3_, ...), custom_call_target="tpu_custom_call" | custom-call | bytes 256 | tf_op jit(solution)/shard_map/put/pallas_call | solution.py:236
  180.6 4.6 %put.8 = bf16[32,256,640]{2,1,0:T(8,128)(2,1)S(1)} custom-call(s32[16]{0:T(128)S(1)} %stack.269.places, bf16[32,256,640]{2,1,0:T(8,128)(2,1)S(1)} %put.7.refs_0_, bf16[3584,640]{1,0:T(8,128)(2,1)} %collective-permute-done.30.refs_1_, bf16[512,640]{1,0:T(8,128)(2,1)S(1)} %bitcast.119), custom_call_target="tpu_custom_call", output_to_operand_aliasing={{}: (1, {})} | custom-call | bytes 256 | tf_op jit(solution)/shard_map/put/pallas_call | solution.py:236
  185.2 3.5 %convolution_convert_fusion.1.refs_0_ = bf16[256,640]{1,0:T(8,128)(2,1)S(1)} fusion(bf16[256,8192]{1,0:T(8,128)(2,1)S(1)} %pad_maximum_fusion, bf16[8192,640]{1,0:T(8,128)(2,1)S(1)} %bitcast.113), kind=kOutput, calls=%fused_computation.14 | convolution fusion | flops 2684518400 | bytes 15007744 | tf_op jit(solution)/shard_map/dot_general | solution.py:475
  188.8 8.3 %collective-permute-done.29 = bf16[64,8192]{1,0:T(8,128)(2,1)S(1)} collective-permute-done((bf16[64,8192]{1,0:T(8,128)(2,1)S(1)}, bf16[64,8192]{1,0:T(8,128)(2,1)S(1)}, u32[]{:S(2)}, u32[]{:S(2)}) %collective-permute-start.29) | collective-permute-done | bytes 1048608 | tf_op jit(solution)/shard_map/ppermute | solution.py:202
  197.1 1.9 collective-permute-done.27
  199.1 1.1 collective-permute-start.35
  200.2 1.0 collective-permute-start.34
  201.2 3.2 %collective-permute-start.33 = (bf16[16,8192]{1,0:T(8,128)(2,1)S(1)}, bf16[16,8192]{1,0:T(8,128)(2,1)S(1)}, u32[]{:S(2)}, u32[]{:S(2)}) collective-permute-start(bf16[16,8192]{1,0:T(8,128)(2,1)S(1)} %slice.119), channel_id=1, source_target_pairs={{0,6},{1,7},{2,0},{3,1},{4,2},{5,3},{6,4},{7,5},{8,14},{9,15},{10,... | collective-permute-start | bytes 786440 | tf_op jit(solution)/shard_map/ppermute | solution.py:199
  204.4 2.7 %fusion.7.refs_1_ = bf16[192,640]{1,0:T(8,128)(2,1)S(1)} fusion(bf16[8192,640]{1,0:T(8,128)(2,1)S(1)} %bitcast.114, bf16[64,8192]{1,0:T(8,128)(2,1)S(1)} %collective-permute-done.28, bf16[64,8192]{1,0:T(8,128)(2,1)S(1)} %collective-permute-done.27, bf16[64,8192]{1,0:T(8,128)(2,1)S(1)} %collective-permute-done.29), kind=kOutput, calls=%fused_computation.15 | convolution fusion | flops 2022825984 | bytes 13877248 | tf_op jit(solution)/shard_map/dot_general | solution.py:475
  207.1 1.4 order.1.refs_0_
  208.5 3.3 %collective-permute-done.34 = bf16[16,8192]{1,0:T(8,128)(2,1)S(1)} collective-permute-done((bf16[16,8192]{1,0:T(8,128)(2,1)S(1)}, bf16[16,8192]{1,0:T(8,128)(2,1)S(1)}, u32[]{:S(2)}, u32[]{:S(2)}) %collective-permute-start.34) | collective-permute-done | bytes 262176 | tf_op jit(solution)/shard_map/ppermute | solution.py:202
  211.9 1.9 convolution_convert_fusion.2.refs_1_
  213.7 1.2 put.9
  (137 shorter events, 6.3 us)
Async XLA Ops:
  0.0 33.9 %copy-start.18 = (f32[5120]{0:T(1024)S(1)}, f32[5120]{0:T(1024)}, u32[]{:S(2)}) copy-start(f32[5120]{0:T(1024)} %param.11) | copy-start | bytes 61444
  0.0 34.0 %collective-permute-start.1 = (bf16[512,640]{1,0:T(8,128)(2,1)}, bf16[512,640]{1,0:T(8,128)(2,1)S(1)}, u32[]{:S(2)}, u32[]{:S(2)}) collective-permute-start(bf16[512,640]{1,0:T(8,128)(2,1)} %refs_0_.3), channel_id=1, source_target_pairs={{0,48},{8,56},{16,0},{24,8},{32,16},{40,24},{48,32},{56,40},{64,11... | collective-permute-start | bytes 1966088 | tf_op jit(solution)/shard_map/ppermute | solution.py:199
  3.1 30.9 %collective-permute-start = (bf16[512,640]{1,0:T(8,128)(2,1)}, bf16[512,640]{1,0:T(8,128)(2,1)S(1)}, u32[]{:S(2)}, u32[]{:S(2)}) collective-permute-start(bf16[512,640]{1,0:T(8,128)(2,1)} %refs_0_.3), channel_id=1, source_target_pairs={{0,16},{8,24},{16,32},{24,40},{32,48},{40,56},{48,0},{56,8},{64,80... | collective-permute-start | bytes 1966088 | tf_op jit(solution)/shard_map/ppermute | solution.py:196
  3.1 30.9 %collective-permute-start.3 = (bf16[640,640]{1,0:T(8,128)(2,1)}, bf16[640,640]{1,0:T(8,128)(2,1)S(1)}, u32[]{:S(2)}, u32[]{:S(2)}) collective-permute-start(bf16[640,640]{1,0:T(8,128)(2,1)} %refs_0_.1), channel_id=1, source_target_pairs={{0,2},{1,3},{2,4},{3,5},{4,6},{5,7},{6,0},{7,1},{8,10},{9,11},{10,... | collective-permute-start | bytes 2457608 | tf_op jit(solution)/shard_map/ppermute | solution.py:196
  5.0 29.0 %collective-permute-start.2 = (bf16[640,640]{1,0:T(8,128)(2,1)}, bf16[640,640]{1,0:T(8,128)(2,1)}, u32[]{:S(2)}, u32[]{:S(2)}) collective-permute-start(bf16[640,640]{1,0:T(8,128)(2,1)} %refs_0_.1), channel_id=1, source_target_pairs={{0,1},{1,0},{2,3},{3,2},{4,5},{5,4},{6,7},{7,6},{8,9},{9,8},{10,11... | collective-permute-start | bytes 2457608 | tf_op jit(solution)/shard_map/ppermute | solution.py:202
  6.5 27.5 %collective-permute-start.4 = (bf16[640,640]{1,0:T(8,128)(2,1)}, bf16[640,640]{1,0:T(8,128)(2,1)}, u32[]{:S(2)}, u32[]{:S(2)}) collective-permute-start(bf16[640,640]{1,0:T(8,128)(2,1)} %refs_0_.1), channel_id=1, source_target_pairs={{0,6},{1,7},{2,0},{3,1},{4,2},{5,3},{6,4},{7,5},{8,14},{9,15},{10,... | collective-permute-start | bytes 2457608 | tf_op jit(solution)/shard_map/ppermute | solution.py:199
  8.6 25.0 %all-to-all-start = ((bf16[8,64,640]{2,1,0:T(8,128)(2,1)}), bf16[8,64,640]{2,1,0:T(8,128)(2,1)S(1)}, u32[]{:S(2)}, u32[]{:S(2)}) async-start(bf16[8,64,640]{2,1,0:T(8,128)(2,1)} %bitcast.147), calls=%async_computation | async-start | bytes 1310720 | tf_op jit(solution)/shard_map/all_to_all | solution.py:320
  34.0 94.8 %copy-start.2 = (bf16[512,640]{1,0:T(8,128)(2,1)}, bf16[512,640]{1,0:T(8,128)(2,1)S(1)}, u32[]{:S(2)}) copy-start(bf16[512,640]{1,0:T(8,128)(2,1)S(1)} %collective-permute-done.refs_1_) | copy-start | bytes 1966084
  34.0 23.3 %collective-permute-start.6 = (bf16[640,640]{1,0:T(8,128)(2,1)}, bf16[640,640]{1,0:T(8,128)(2,1)S(1)}, u32[]{:S(2)}, u32[]{:S(2)}) collective-permute-start(bf16[640,640]{1,0:T(8,128)(2,1)} %collective-permute-done.2.refs_3_), channel_id=1, source_target_pairs={{0,6},{1,7},{2,0},{3,1},{4,2},{5,3},{6,4},{7,5},{8,14},{9,15},{10,... | collective-permute-start | bytes 2457608 | tf_op jit(solution)/shard_map/ppermute | solution.py:199
  36.9 20.4 %collective-permute-start.5 = (bf16[640,640]{1,0:T(8,128)(2,1)}, bf16[640,640]{1,0:T(8,128)(2,1)S(1)}, u32[]{:S(2)}, u32[]{:S(2)}) collective-permute-start(bf16[640,640]{1,0:T(8,128)(2,1)} %collective-permute-done.2.refs_3_), channel_id=1, source_target_pairs={{0,2},{1,3},{2,4},{3,5},{4,6},{5,7},{6,0},{7,1},{8,10},{9,11},{10,... | collective-permute-start | bytes 2457608 | tf_op jit(solution)/shard_map/ppermute | solution.py:196
  37.2 15.4 %collective-permute-start.9 = (bf16[64,5120]{1,0:T(8,128)(2,1)S(1)}, bf16[64,5120]{1,0:T(8,128)(2,1)S(1)}, u32[]{:S(2)}, u32[]{:S(2)}) collective-permute-start(bf16[64,5120]{1,0:T(8,128)(2,1)S(1)} %multiply_convert_fusion), channel_id=1, source_target_pairs={{0,64},{8,72},{16,80},{24,88},{32,96},{40,104},{48,112},{56,120},{... | collective-permute-start | bytes 1966088 | tf_op jit(solution)/shard_map/ppermute | solution.py:202
  40.0 15.6 %collective-permute-start.8 = (bf16[64,5120]{1,0:T(8,128)(2,1)S(1)}, bf16[64,5120]{1,0:T(8,128)(2,1)S(1)}, u32[]{:S(2)}, u32[]{:S(2)}) collective-permute-start(bf16[64,5120]{1,0:T(8,128)(2,1)S(1)} %multiply_convert_fusion), channel_id=1, source_target_pairs={{0,48},{8,56},{16,0},{24,8},{32,16},{40,24},{48,32},{56,40},{64,11... | collective-permute-start | bytes 1966088 | tf_op jit(solution)/shard_map/ppermute | solution.py:199
  42.9 14.4 %collective-permute-start.7 = (bf16[64,5120]{1,0:T(8,128)(2,1)S(1)}, bf16[64,5120]{1,0:T(8,128)(2,1)S(1)}, u32[]{:S(2)}, u32[]{:S(2)}) collective-permute-start(bf16[64,5120]{1,0:T(8,128)(2,1)S(1)} %multiply_convert_fusion), channel_id=1, source_target_pairs={{0,16},{8,24},{16,32},{24,40},{32,48},{40,56},{48,0},{56,8},{64,80... | collective-permute-start | bytes 1966088 | tf_op jit(solution)/shard_map/ppermute | solution.py:196
  42.9 9.6 %copy-start.5 = (bf16[512,640]{1,0:T(8,128)(2,1)S(1)}, bf16[512,640]{1,0:T(8,128)(2,1)}, u32[]{:S(2)}) copy-start(bf16[512,640]{1,0:T(8,128)(2,1)} %refs_0_.3) | copy-start | bytes 1966084
  52.6 16.9 %collective-permute-start.14 = (bf16[512,640]{1,0:T(8,128)(2,1)S(1)}, bf16[512,640]{1,0:T(8,128)(2,1)S(1)}, u32[]{:S(2)}, u32[]{:S(2)}) collective-permute-start(bf16[512,640]{1,0:T(8,128)(2,1)S(1)} %copy-done.5), channel_id=1, source_target_pairs={{0,64},{8,72},{16,80},{24,88},{32,96},{40,104},{48,112},{56,120},{... | collective-permute-start | bytes 1966088 | tf_op jit(solution)/shard_map/ppermute | solution.py:202
  57.5 8.2 %copy-start.13 = (bf16[640,640]{1,0:T(8,128)(2,1)S(1)}, bf16[640,640]{1,0:T(8,128)(2,1)}, u32[]{:S(2)}) copy-start(bf16[640,640]{1,0:T(8,128)(2,1)} %refs_0_.1) | copy-start | bytes 2457604
  57.7 15.9 %collective-permute-start.11 = (bf16[640,640]{1,0:T(8,128)(2,1)S(1)}, bf16[640,640]{1,0:T(8,128)(2,1)S(1)}, u32[]{:S(2)}, u32[]{:S(2)}) collective-permute-start(bf16[640,640]{1,0:T(8,128)(2,1)S(1)} %pad_maximum_fusion.11), channel_id=1, source_target_pairs={{0,6},{1,7},{2,0},{3,1},{4,2},{5,3},{6,4},{7,5},{8,14},{9,15},{10,... | collective-permute-start | bytes 2457608 | tf_op jit(solution)/shard_map/ppermute | solution.py:199
  60.6 16.3 %collective-permute-start.10 = (bf16[640,640]{1,0:T(8,128)(2,1)S(1)}, bf16[640,640]{1,0:T(8,128)(2,1)S(1)}, u32[]{:S(2)}, u32[]{:S(2)}) collective-permute-start(bf16[640,640]{1,0:T(8,128)(2,1)S(1)} %pad_maximum_fusion.10), channel_id=1, source_target_pairs={{0,2},{1,3},{2,4},{3,5},{4,6},{5,7},{6,0},{7,1},{8,10},{9,11},{10,... | collective-permute-start | bytes 2457608 | tf_op jit(solution)/shard_map/ppermute | solution.py:196
  60.9 19.8 %collective-permute-start.13 = (bf16[96,5120]{1,0:T(8,128)(2,1)S(1)}, bf16[96,5120]{1,0:T(8,128)(2,1)S(1)}, u32[]{:S(2)}, u32[]{:S(2)}) collective-permute-start(bf16[96,5120]{1,0:T(8,128)(2,1)S(1)} %get-tuple-element.124), channel_id=1, source_target_pairs={{0,48},{8,56},{16,0},{24,8},{32,16},{40,24},{48,32},{56,40},{64,11... | collective-permute-start | bytes 2949128 | tf_op jit(solution)/shard_map/ppermute | solution.py:199
  61.9 21.4 %collective-permute-start.12 = (bf16[96,5120]{1,0:T(8,128)(2,1)S(1)}, bf16[96,5120]{1,0:T(8,128)(2,1)S(1)}, u32[]{:S(2)}, u32[]{:S(2)}) collective-permute-start(bf16[96,5120]{1,0:T(8,128)(2,1)S(1)} %get-tuple-element.125), channel_id=1, source_target_pairs={{0,16},{8,24},{16,32},{24,40},{32,48},{40,56},{48,0},{56,8},{64,80... | collective-permute-start | bytes 2949128 | tf_op jit(solution)/shard_map/ppermute | solution.py:196
  65.7 19.9 %slice-start = ((s8[10485760]{0:T(1024)(128)(4,1)}), s8[4194304]{0:T(1024)(128)(4,1)S(1)}, s32[]{:S(2)}) async-start(s8[10485760]{0:T(1024)(128)(4,1)} %bitcast.122), calls=%async_computation.2 | async-start | bytes 8388608
  65.7 19.9 %slice-start.1 = ((s8[10485760]{0:T(1024)(128)(4,1)}), s8[4194304]{0:T(1024)(128)(4,1)S(1)}, s32[]{:S(2)}) async-start(s8[10485760]{0:T(1024)(128)(4,1)} %bitcast.122), calls=%async_computation.3 | async-start | bytes 8388608
  69.1 16.5 %slice-start.2 = ((s8[10485760]{0:T(1024)(128)(4,1)}), s8[2097152]{0:T(1024)(128)(4,1)S(1)}, s32[]{:S(2)}) async-start(s8[10485760]{0:T(1024)(128)(4,1)} %bitcast.122), calls=%async_computation.4 | async-start | bytes 4194304
  83.5 7.1 %collective-permute-start.16 = (bf16[32,5120]{1,0:T(8,128)(2,1)S(1)}, bf16[32,5120]{1,0:T(8,128)(2,1)S(1)}, u32[]{:S(2)}, u32[]{:S(2)}) collective-permute-start(bf16[32,5120]{1,0:T(8,128)(2,1)S(1)} %slice.105), channel_id=1, source_target_pairs={{0,48},{8,56},{16,0},{24,8},{32,16},{40,24},{48,32},{56,40},{64,11... | collective-permute-start | bytes 983048 | tf_op jit(solution)/shard_map/ppermute | solution.py:199
  83.9 8.3 %collective-permute-start.15 = (bf16[32,5120]{1,0:T(8,128)(2,1)S(1)}, bf16[32,5120]{1,0:T(8,128)(2,1)S(1)}, u32[]{:S(2)}, u32[]{:S(2)}) collective-permute-start(bf16[32,5120]{1,0:T(8,128)(2,1)S(1)} %slice.104), channel_id=1, source_target_pairs={{0,16},{8,24},{16,32},{24,40},{32,48},{40,56},{48,0},{56,8},{64,80... | collective-permute-start | bytes 983048 | tf_op jit(solution)/shard_map/ppermute | solution.py:196
  86.0 6.6 %collective-permute-start.17 = (bf16[2,96,5120]{2,1,0:T(8,128)(2,1)S(1)}, bf16[2,96,5120]{2,1,0:T(8,128)(2,1)S(1)}, u32[]{:S(2)}, u32[]{:S(2)}) collective-permute-start(bf16[2,96,5120]{2,1,0:T(8,128)(2,1)S(1)} %pad_maximum_fusion.2), channel_id=1, source_target_pairs={{0,8},{8,0},{16,24},{24,16},{32,40},{40,32},{48,56},{56,48},{64,72... | collective-permute-start | bytes 5898248 | tf_op jit(solution)/shard_map/ppermute | solution.py:205
  86.1 8.7 %collective-permute-start.19 = (bf16[4,64,5120]{2,1,0:T(8,128)(2,1)S(1)}, bf16[4,64,5120]{2,1,0:T(8,128)(2,1)S(1)}, u32[]{:S(2)}, u32[]{:S(2)}) collective-permute-start(bf16[4,64,5120]{2,1,0:T(8,128)(2,1)S(1)} %pad_maximum_fusion.1), channel_id=1, source_target_pairs={{0,8},{8,0},{16,24},{24,16},{32,40},{40,32},{48,56},{56,48},{64,72... | collective-permute-start | bytes 7864328 | tf_op jit(solution)/shard_map/ppermute | solution.py:205
  92.2 2.5 %collective-permute-start.18 = (bf16[2,32,5120]{2,1,0:T(8,128)(2,1)S(1)}, bf16[2,32,5120]{2,1,0:T(8,128)(2,1)S(1)}, u32[]{:S(2)}, u32[]{:S(2)}) collective-permute-start(bf16[2,32,5120]{2,1,0:T(8,128)(2,1)S(1)} %pad_maximum_fusion.12), channel_id=1, source_target_pairs={{0,8},{8,0},{16,24},{24,16},{32,40},{40,32},{48,56},{56,48},{64,72... | collective-permute-start | bytes 1966088 | tf_op jit(solution)/shard_map/ppermute | solution.py:205
  103.5 27.6 %copy-start.7 = (bf16[4,256,1024]{2,1,0:T(8,128)(2,1)S(1)}, bf16[4,256,1024]{2,1,0:T(8,128)(2,1)}, u32[]{:S(2)}) copy-start(bf16[4,256,1024]{2,1,0:T(8,128)(2,1)} %keys.1) | copy-start | bytes 6291460
  103.5 27.6 %copy-start.8 = (bf16[4,256,1024]{2,1,0:T(8,128)(2,1)S(1)}, bf16[4,256,1024]{2,1,0:T(8,128)(2,1)}, u32[]{:S(2)}) copy-start(bf16[4,256,1024]{2,1,0:T(8,128)(2,1)} %values.1) | copy-start | bytes 6291460
  103.5 27.6 %copy-start.14 = (s32[4]{0:T(128)S(1)}, s32[4]{0:T(128)}, u32[]{:S(2)}) copy-start(s32[4]{0:T(128)} %fills.1) | copy-start | bytes 52
  103.6 27.6 %copy-start.15 = (s32[4]{0:T(128)S(1)}, s32[4]{0:T(128)}, u32[]{:S(2)}) copy-start(s32[4]{0:T(128)} %spans.1) | copy-start | bytes 52
  103.6 27.6 %copy-start.16 = (f32[128]{0:T(128)S(1)}, f32[128]{0:T(128)}, u32[]{:S(2)}) copy-start(f32[128]{0:T(128)} %param.13) | copy-start | bytes 1540
  103.6 27.6 %copy-start.17 = (f32[128]{0:T(128)S(1)}, f32[128]{0:T(128)}, u32[]{:S(2)}) copy-start(f32[128]{0:T(128)} %param.14) | copy-start | bytes 1540
  128.9 26.7 %copy-start.3 = (bf16[512,640]{1,0:T(8,128)(2,1)S(1)}, bf16[512,640]{1,0:T(8,128)(2,1)}, u32[]{:S(2)}) copy-start(bf16[512,640]{1,0:T(8,128)(2,1)} %copy-done.2) | copy-start | bytes 1966084
  129.1 23.3 %collective-permute-start.25 = (bf16[768,640]{1,0:T(8,128)(2,1)S(1)}, bf16[768,640]{1,0:T(8,128)(2,1)S(1)}, u32[]{:S(2)}, u32[]{:S(2)}) collective-permute-start(bf16[768,640]{1,0:T(8,128)(2,1)S(1)} %get-tuple-element.122), channel_id=1, source_target_pairs={{0,48},{8,56},{16,0},{24,8},{32,16},{40,24},{48,32},{56,40},{64,11... | collective-permute-start | bytes 2949128 | tf_op jit(solution)/shard_map/ppermute | solution.py:199
  130.1 25.3 %collective-permute-start.23 = (bf16[768,640]{1,0:T(8,128)(2,1)S(1)}, bf16[768,640]{1,0:T(8,128)(2,1)S(1)}, u32[]{:S(2)}, u32[]{:S(2)}) collective-permute-start(bf16[768,640]{1,0:T(8,128)(2,1)S(1)} %get-tuple-element.123), channel_id=1, source_target_pairs={{0,16},{8,24},{16,32},{24,40},{32,48},{40,56},{48,0},{56,8},{64,80... | collective-permute-start | bytes 2949128 | tf_op jit(solution)/shard_map/ppermute | solution.py:196
  139.1 16.3 %copy-start = (bf16[64,8192]{1,0:T(8,128)(2,1)}, bf16[64,8192]{1,0:T(8,128)(2,1)S(1)}, u32[]{:S(2)}) copy-start(bf16[64,8192]{1,0:T(8,128)(2,1)S(1)} %attend.1) | copy-start | bytes 3145732
  139.1 27.5 %collective-permute-start.22 = (bf16[64,8192]{1,0:T(8,128)(2,1)S(1)}, bf16[64,8192]{1,0:T(8,128)(2,1)}, u32[]{:S(2)}, u32[]{:S(2)}) collective-permute-start(bf16[64,8192]{1,0:T(8,128)(2,1)S(1)} %attend.1), channel_id=1, source_target_pairs={{0,1},{1,0},{2,3},{3,2},{4,5},{5,4},{6,7},{7,6},{8,9},{9,8},{10,11... | collective-permute-start | bytes 3145736 | tf_op jit(solution)/shard_map/ppermute | solution.py:202
  139.2 27.4 %collective-permute-start.21 = (bf16[64,8192]{1,0:T(8,128)(2,1)S(1)}, bf16[64,8192]{1,0:T(8,128)(2,1)}, u32[]{:S(2)}, u32[]{:S(2)}) collective-permute-start(bf16[64,8192]{1,0:T(8,128)(2,1)S(1)} %attend.1), channel_id=1, source_target_pairs={{0,6},{1,7},{2,0},{3,1},{4,2},{5,3},{6,4},{7,5},{8,14},{9,15},{10,... | collective-permute-start | bytes 3145736 | tf_op jit(solution)/shard_map/ppermute | solution.py:199
  141.7 24.9 %collective-permute-start.20 = (bf16[64,8192]{1,0:T(8,128)(2,1)S(1)}, bf16[64,8192]{1,0:T(8,128)(2,1)}, u32[]{:S(2)}, u32[]{:S(2)}) collective-permute-start(bf16[64,8192]{1,0:T(8,128)(2,1)S(1)} %attend.1), channel_id=1, source_target_pairs={{0,2},{1,3},{2,4},{3,5},{4,6},{5,7},{6,0},{7,1},{8,10},{9,11},{10,... | collective-permute-start | bytes 3145736 | tf_op jit(solution)/shard_map/ppermute | solution.py:196
  152.4 9.8 %collective-permute-start.26 = (bf16[256,640]{1,0:T(8,128)(2,1)S(1)}, bf16[256,640]{1,0:T(8,128)(2,1)S(1)}, u32[]{:S(2)}, u32[]{:S(2)}) collective-permute-start(bf16[256,640]{1,0:T(8,128)(2,1)S(1)} %slice.127), channel_id=1, source_target_pairs={{0,48},{8,56},{16,0},{24,8},{32,16},{40,24},{48,32},{56,40},{64,11... | collective-permute-start | bytes 983048 | tf_op jit(solution)/shard_map/ppermute | solution.py:199
  155.4 10.2 %collective-permute-start.24 = (bf16[256,640]{1,0:T(8,128)(2,1)S(1)}, bf16[256,640]{1,0:T(8,128)(2,1)S(1)}, u32[]{:S(2)}, u32[]{:S(2)}) collective-permute-start(bf16[256,640]{1,0:T(8,128)(2,1)S(1)} %slice.126), channel_id=1, source_target_pairs={{0,16},{8,24},{16,32},{24,40},{32,48},{40,56},{48,0},{56,8},{64,80... | collective-permute-start | bytes 983048 | tf_op jit(solution)/shard_map/ppermute | solution.py:196
  162.1 4.5 %copy-start.9 = (bf16[256,640]{1,0:T(8,128)(2,1)}, bf16[256,640]{1,0:T(8,128)(2,1)S(1)}, u32[]{:S(2)}) copy-start(bf16[256,640]{1,0:T(8,128)(2,1)S(1)} %collective-permute-done.26.refs_7_) | copy-start | bytes 983044
  165.6 1.0 copy-start.11
  166.6 14.0 %collective-permute-start.30 = (bf16[3584,640]{1,0:T(8,128)(2,1)}, bf16[3584,640]{1,0:T(8,128)(2,1)}, u32[]{:S(2)}, u32[]{:S(2)}) collective-permute-start(bf16[3584,640]{1,0:T(8,128)(2,1)} %pack.1), channel_id=1, source_target_pairs={{0,8},{8,0},{16,24},{24,16},{32,40},{40,32},{48,56},{56,48},{64,72... | collective-permute-start | bytes 13762568 | tf_op jit(solution)/shard_map/ppermute | solution.py:205
  167.3 8.8 %copy-start.1 = (bf16[64,8192]{1,0:T(8,128)(2,1)S(1)}, bf16[64,8192]{1,0:T(8,128)(2,1)}, u32[]{:S(2)}) copy-start(bf16[64,8192]{1,0:T(8,128)(2,1)} %copy-done) | copy-start | bytes 3145732
  169.7 10.9 %collective-permute-start.31 = (bf16[2,256,640]{2,1,0:T(8,128)(2,1)}, bf16[2,256,640]{2,1,0:T(8,128)(2,1)S(1)}, u32[]{:S(2)}, u32[]{:S(2)}) collective-permute-start(bf16[2,256,640]{2,1,0:T(8,128)(2,1)} %pad_maximum_fusion.13), channel_id=1, source_target_pairs={{0,8},{8,0},{16,24},{24,16},{32,40},{40,32},{48,56},{56,48},{64,72... | collective-permute-start | bytes 1966088 | tf_op jit(solution)/shard_map/ppermute | solution.py:205
  171.5 6.8 %copy-start.4 = (bf16[512,640]{1,0:T(8,128)(2,1)S(1)}, bf16[512,640]{1,0:T(8,128)(2,1)}, u32[]{:S(2)}) copy-start(bf16[512,640]{1,0:T(8,128)(2,1)} %copy-done.2) | copy-start | bytes 1966084
  171.5 6.8 %copy-start.6 = (bf16[512,640]{1,0:T(8,128)(2,1)S(1)}, bf16[512,640]{1,0:T(8,128)(2,1)}, u32[]{:S(2)}) copy-start(bf16[512,640]{1,0:T(8,128)(2,1)} %refs_0_.3) | copy-start | bytes 1966084
  171.5 6.8 %copy-start.10 = (bf16[256,640]{1,0:T(8,128)(2,1)S(1)}, bf16[256,640]{1,0:T(8,128)(2,1)}, u32[]{:S(2)}) copy-start(bf16[256,640]{1,0:T(8,128)(2,1)} %copy-done.9) | copy-start | bytes 983044
  171.5 6.8 %copy-start.12 = (bf16[256,640]{1,0:T(8,128)(2,1)S(1)}, bf16[256,640]{1,0:T(8,128)(2,1)}, u32[]{:S(2)}) copy-start(bf16[256,640]{1,0:T(8,128)(2,1)} %copy-done.11) | copy-start | bytes 983044
  171.8 25.2 %collective-permute-start.29 = (bf16[64,8192]{1,0:T(8,128)(2,1)S(1)}, bf16[64,8192]{1,0:T(8,128)(2,1)S(1)}, u32[]{:S(2)}, u32[]{:S(2)}) collective-permute-start(bf16[64,8192]{1,0:T(8,128)(2,1)S(1)} %get-tuple-element.126), channel_id=1, source_target_pairs={{0,1},{1,0},{2,3},{3,2},{4,5},{5,4},{6,7},{7,6},{8,9},{9,8},{10,11... | collective-permute-start | bytes 3145736 | tf_op jit(solution)/shard_map/ppermute | solution.py:202
  172.9 26.0 %collective-permute-start.27 = (bf16[64,8192]{1,0:T(8,128)(2,1)S(1)}, bf16[64,8192]{1,0:T(8,128)(2,1)S(1)}, u32[]{:S(2)}, u32[]{:S(2)}) collective-permute-start(bf16[64,8192]{1,0:T(8,128)(2,1)S(1)} %get-tuple-element.127), channel_id=1, source_target_pairs={{0,2},{1,3},{2,4},{3,5},{4,6},{5,7},{6,0},{7,1},{8,10},{9,11},{10,... | collective-permute-start | bytes 3145736 | tf_op jit(solution)/shard_map/ppermute | solution.py:196
  172.9 26.0 %collective-permute-start.28 = (bf16[64,8192]{1,0:T(8,128)(2,1)S(1)}, bf16[64,8192]{1,0:T(8,128)(2,1)S(1)}, u32[]{:S(2)}, u32[]{:S(2)}) collective-permute-start(bf16[64,8192]{1,0:T(8,128)(2,1)S(1)} %get-tuple-element.128), channel_id=1, source_target_pairs={{0,6},{1,7},{2,0},{3,1},{4,2},{5,3},{6,4},{7,5},{8,14},{9,15},{10,... | collective-permute-start | bytes 3145736 | tf_op jit(solution)/shard_map/ppermute | solution.py:199
  199.1 9.5 %collective-permute-start.35 = (bf16[16,8192]{1,0:T(8,128)(2,1)S(1)}, bf16[16,8192]{1,0:T(8,128)(2,1)S(1)}, u32[]{:S(2)}, u32[]{:S(2)}) collective-permute-start(bf16[16,8192]{1,0:T(8,128)(2,1)S(1)} %get-tuple-element.117), channel_id=1, source_target_pairs={{0,1},{1,0},{2,3},{3,2},{4,5},{5,4},{6,7},{7,6},{8,9},{9,8},{10,11... | collective-permute-start | bytes 786440 | tf_op jit(solution)/shard_map/ppermute | solution.py:202
  200.2 11.7 %collective-permute-start.34 = (bf16[16,8192]{1,0:T(8,128)(2,1)S(1)}, bf16[16,8192]{1,0:T(8,128)(2,1)S(1)}, u32[]{:S(2)}, u32[]{:S(2)}) collective-permute-start(bf16[16,8192]{1,0:T(8,128)(2,1)S(1)} %get-tuple-element.118), channel_id=1, source_target_pairs={{0,1},{1,0},{2,3},{3,2},{4,5},{5,4},{6,7},{7,6},{8,9},{9,8},{10,11... | collective-permute-start | bytes 786440 | tf_op jit(solution)/shard_map/ppermute | solution.py:202
  201.2 10.7 %collective-permute-start.32 = (bf16[16,8192]{1,0:T(8,128)(2,1)S(1)}, bf16[16,8192]{1,0:T(8,128)(2,1)S(1)}, u32[]{:S(2)}, u32[]{:S(2)}) collective-permute-start(bf16[16,8192]{1,0:T(8,128)(2,1)S(1)} %get-tuple-element.119), channel_id=1, source_target_pairs={{0,2},{1,3},{2,4},{3,5},{4,6},{5,7},{6,0},{7,1},{8,10},{9,11},{10,... | collective-permute-start | bytes 786440 | tf_op jit(solution)/shard_map/ppermute | solution.py:196
  201.2 10.7 %collective-permute-start.33 = (bf16[16,8192]{1,0:T(8,128)(2,1)S(1)}, bf16[16,8192]{1,0:T(8,128)(2,1)S(1)}, u32[]{:S(2)}, u32[]{:S(2)}) collective-permute-start(bf16[16,8192]{1,0:T(8,128)(2,1)S(1)} %slice.119), channel_id=1, source_target_pairs={{0,6},{1,7},{2,0},{3,1},{4,2},{5,3},{6,4},{7,5},{8,14},{9,15},{10,... | collective-permute-start | bytes 786440 | tf_op jit(solution)/shard_map/ppermute | solution.py:199

commit v4 on v3

--- a/solution.py
+++ b/solution.py
@@ -433,9 +433,10 @@
         (a_up, a_down, a_swap, o_far_up, o_far_down, o_near, other_far)
     )
 
-    b_up = narrow.up(jnp.concatenate([a_swap[half_rows:], a_up[:half_rows]]))
-    b_down = narrow.down(jnp.concatenate([a_swap[half_rows:], a_down[half_rows:]]))
-    b_swap = narrow.swap(jnp.concatenate([a_up[:half_rows], a_down[:half_rows]]))
+    low = lax.broadcasted_iota(jnp.int32, (rows, 1), 0) < half_rows
+    b_up = narrow.up(jnp.where(low, a_up, a_swap))
+    b_down = narrow.down(jnp.where(low, a_swap, a_down))
+    b_swap = narrow.swap(jnp.where(low, a_up, a_down))
     o_near = wide.cores(o_near)
     other_far = wide.cores(other_far).reshape(out_rows, -1)
     near_rows = jnp.concatenate([attended, a_swap, a_up, a_down])
@@ -477,10 +478,10 @@
 
     near_rows = project_out(near_rows)
     b_up, b_down, b_swap, near_rows = barrier((b_up, b_down, b_swap, near_rows))
-    c_up = narrow.up(b_up[:quarter])
-    c_down = narrow.down(b_down[quarter:half_rows])
-    c_swap = narrow.swap(b_up[half_rows : half_rows + quarter])
-    c_swap_last = narrow.swap(b_up[half_rows + quarter :])
+    c_up = narrow.up(b_up[half_rows : half_rows + quarter])
+    c_down = narrow.down(b_swap[half_rows + quarter :])
+    c_swap = narrow.swap(b_up[:quarter])
+    c_swap_last = narrow.swap(b_up[quarter:half_rows])
     one, other = narrow.at_pair, 1 - narrow.at_pair
     place_of = lambda ring, pair, half: (narrow.ring(ring) * 2 + pair) * 2 + half
     result = order(
@@ -496,10 +497,10 @@
                 place_of(*place)
                 for place in (
                     (3, other, 0),
+                    (1, other, 1),
+                    (2, one, 0),
+                    (3, other, 1),
                     (1, other, 0),
-                    (3, other, 1),
-                    (2, one, 0),
-                    (1, other, 1),
                     (2, one, 1),
                 )
             ]
@@ -511,12 +512,12 @@
         (c_up, c_down, c_swap, c_swap_last, result)
     )
     result = put(
-        result,
+        result.reshape(8, rows, -1),
         (project_out(jnp.concatenate([c_swap, c_swap_last, c_up, c_down])),),
-        ((0, 0), (0, 1)),
-        jnp.stack([place_of(2, other, 0), place_of(2, other, 1)]),
-        16,
-        half_rows,
+        ((0, 0),),
+        jnp.stack([narrow.ring(2) * 2 + other]),
+        8,
+        rows,
     )
     return result.reshape(-1, result.shape[-1])
 

time: 215 us -> 215 us (level)
  other arithmetic: 6.05 us -> 8.83 us
  local copies, waits for them, and re-layouts: 15.7 us -> 13.1 us
    slice x5 -> x2, local copies, waits for them, and re-layouts: 3.56 us -> 0.07 us  [the longest x1 0.05 us: shards(): c_swap_last = narrow.swap(b_up[quarter:half_rows])]
  transfers between devices with their start and end apart: 37 -> 37, of which waited for: 16 -> 17; matrix products, arithmetic and copies ran while one was open for 13% -> 12% of each run, Pallas kernels for 11% -> 11%
where the time goes in v4:
time: 215 us
  waiting for transfers between devices  77.1 us (36%)
  starting transfers between devices  48.9 us (23%)
  blocking collectives  25.2 us (12%)
  Pallas kernels  24.9 us (12%)
  matrix products  16.1 us (7%)
  local copies, waits for them, and re-layouts  13.1 us (6%)
  other arithmetic  8.83 us (4%)
    ppermute x12, starting transfers between devices, down(): return lax.ppermute(block, self.axis, self.pairs(-1, 0, 0))  26.4 us
    ppermute x12, waiting for transfers between devices, down(): return lax.ppermute(block, self.axis, self.pairs(-1, 0, 0))  25.4 us
    all_to_all x1, blocking collectives, shards(): lax.all_to_all(projected.reshape(wide_count, rows, -1), 'wide', split_axi...  25.2 us
    all_to_all x1, waiting for transfers between devices, shards(): lax.all_to_all(tokens, 'narrow', split_axis=0, concat_axis=1, tiled=True)  20.1 us
    ppermute x12, waiting for transfers between devices, up(): return lax.ppermute(block, self.axis, self.pairs(1, 0, 0))  15.1 us
    ppermute x7, waiting for transfers between devices, swap(): return lax.ppermute(block, self.axis, self.pairs(0, 1, 0))  14.6 us
    pallas_call x5, Pallas kernels, put(): pl.pallas_call(functools.partial(put_kernel, sources, aliased), grid_spec...  11.8 us
    ppermute x7, starting transfers between devices, swap(): return lax.ppermute(block, self.axis, self.pairs(0, 1, 0))  10.8 us
  transfers between devices with their start and end apart: 37, of which 17 were waited for; matrix products, arithmetic and copies ran while one was open for 12% of the time, Pallas kernels for 11%

profile of v4, /device:TPU:0, one launch (start us, length us, event | category | flops | bytes accessed | tf_op | source)
XLA Modules:
  0.0 215.1 jit_solution(16443299533161087193)
XLA Ops:
  0.0 3.1 %collective-permute-start.1 = (bf16[512,640]{1,0:T(8,128)(2,1)}, bf16[512,640]{1,0:T(8,128)(2,1)S(1)}, u32[]{:S(2)}, u32[]{:S(2)}) collective-permute-start(bf16[512,640]{1,0:T(8,128)(2,1)} %refs_0_.3), channel_id=1, source_target_pairs={{0,48},{8,56},{16,0},{24,8},{32,16},{40,24},{48,32},{56,40},{64,11... | collective-permute-start | bytes 1966088 | tf_op jit(solution)/shard_map/ppermute | solution.py:199
  3.1 1.9 collective-permute-start.3
  5.0 1.5 collective-permute-start.2
  6.5 2.1 collective-permute-start.4
  8.6 3.5 %all-to-all-start = ((bf16[8,64,640]{2,1,0:T(8,128)(2,1)}), bf16[8,64,640]{2,1,0:T(8,128)(2,1)S(1)}, u32[]{:S(2)}, u32[]{:S(2)}) async-start(bf16[8,64,640]{2,1,0:T(8,128)(2,1)} %bitcast.150), calls=%async_computation | async-start | bytes 1310720 | tf_op jit(solution)/shard_map/all_to_all | solution.py:320
  12.2 0.7 add_convert_fusion
  13.5 20.1 %all-to-all-done = bf16[8,64,640]{2,1,0:T(8,128)(2,1)S(1)} async-done(((bf16[8,64,640]{2,1,0:T(8,128)(2,1)}), bf16[8,64,640]{2,1,0:T(8,128)(2,1)S(1)}, u32[]{:S(2)}, u32[]{:S(2)}) %all-to-all-start) | async-done | bytes 655392 | tf_op jit(solution)/shard_map/all_to_all | solution.py:320
  33.9 0.9 multiply_convert_fusion
  34.8 2.9 %collective-permute-start.6 = (bf16[640,640]{1,0:T(8,128)(2,1)}, bf16[640,640]{1,0:T(8,128)(2,1)S(1)}, u32[]{:S(2)}, u32[]{:S(2)}) collective-permute-start(bf16[640,640]{1,0:T(8,128)(2,1)} %collective-permute-done.2.refs_3_), channel_id=1, source_target_pairs={{0,6},{1,7},{2,0},{3,1},{4,2},{5,3},{6,4},{7,5},{8,14},{9,15},{10,... | collective-permute-start | bytes 2457608 | tf_op jit(solution)/shard_map/ppermute | solution.py:199
  38.0 2.8 %collective-permute-start.9 = (bf16[64,5120]{1,0:T(8,128)(2,1)S(1)}, bf16[64,5120]{1,0:T(8,128)(2,1)S(1)}, u32[]{:S(2)}, u32[]{:S(2)}) collective-permute-start(bf16[64,5120]{1,0:T(8,128)(2,1)S(1)} %multiply_convert_fusion), channel_id=1, source_target_pairs={{0,64},{8,72},{16,80},{24,88},{32,96},{40,104},{48,112},{56,120},{... | collective-permute-start | bytes 1966088 | tf_op jit(solution)/shard_map/ppermute | solution.py:202
  40.8 3.0 %collective-permute-start.8 = (bf16[64,5120]{1,0:T(8,128)(2,1)S(1)}, bf16[64,5120]{1,0:T(8,128)(2,1)S(1)}, u32[]{:S(2)}, u32[]{:S(2)}) collective-permute-start(bf16[64,5120]{1,0:T(8,128)(2,1)S(1)} %multiply_convert_fusion), channel_id=1, source_target_pairs={{0,48},{8,56},{16,0},{24,8},{32,16},{40,24},{48,32},{56,40},{64,11... | collective-permute-start | bytes 1966088 | tf_op jit(solution)/shard_map/ppermute | solution.py:199
  43.8 1.0 slice.82
  44.8 5.3 %broadcast_in_dim.40 = bf16[2,4,2,2,32,5120]{5,4,3,2,1,0:T(8,128)(2,1)} broadcast(bf16[]{:T(256)} %constant.196.clone.1), dimensions={} | broadcast | bytes 10485762 | tf_op jit(solution)/shard_map/broadcast_in_dim | solution.py:335
  50.2 0.9 constant_dynamic-update-slice_fusion.11
  51.1 2.3 %collective-permute-done.9 = bf16[64,5120]{1,0:T(8,128)(2,1)S(1)} collective-permute-done((bf16[64,5120]{1,0:T(8,128)(2,1)S(1)}, bf16[64,5120]{1,0:T(8,128)(2,1)S(1)}, u32[]{:S(2)}, u32[]{:S(2)}) %collective-permute-start.9) | collective-permute-done | bytes 655392 | tf_op jit(solution)/shard_map/ppermute | solution.py:202
  53.4 3.0 %collective-permute-start.14 = (bf16[512,640]{1,0:T(8,128)(2,1)S(1)}, bf16[512,640]{1,0:T(8,128)(2,1)S(1)}, u32[]{:S(2)}, u32[]{:S(2)}) collective-permute-start(bf16[512,640]{1,0:T(8,128)(2,1)S(1)} %copy-done.4), channel_id=1, source_target_pairs={{0,64},{8,72},{16,80},{24,88},{32,96},{40,104},{48,112},{56,120},{... | collective-permute-start | bytes 1966088 | tf_op jit(solution)/shard_map/ppermute | solution.py:202
  56.3 1.8 collective-permute-done.7
  58.4 2.8 %collective-permute-start.11 = (bf16[640,640]{1,0:T(8,128)(2,1)S(1)}, bf16[640,640]{1,0:T(8,128)(2,1)S(1)}, u32[]{:S(2)}, u32[]{:S(2)}) collective-permute-start(bf16[640,640]{1,0:T(8,128)(2,1)S(1)} %pad_maximum_fusion.8), channel_id=1, source_target_pairs={{0,6},{1,7},{2,0},{3,1},{4,2},{5,3},{6,4},{7,5},{8,14},{9,15},{10,... | collective-permute-start | bytes 2457608 | tf_op jit(solution)/shard_map/ppermute | solution.py:199
  61.7 1.0 collective-permute-start.13
  62.7 1.1 collective-permute-start.12
  63.8 0.9 constant_dynamic-update-slice_fusion.10
  64.7 0.9 constant_dynamic-update-slice_fusion.9
  65.6 0.9 constant_dynamic-update-slice_fusion.8
  66.5 3.4 %put.5.refs_0_ = bf16[16,320,640]{2,1,0:T(8,128)(2,1)S(1)} custom-call(s32[12]{0:T(128)S(1)} %stack.236.places, bf16[640,640]{1,0:T(8,128)(2,1)S(1)} %copy-done.12, bf16[640,640]{1,0:T(8,128)(2,1)S(1)} %collective-permute-done.3.refs_1_, bf16[640,640]{1,0:T(8,128)(2,1)} %collective-permute-done.4.refs_2_, bf16[640,640]{1,0:T(8,128)(2,1)} %collective-permute-done.2.refs_3_, ...), custom_call_target="tpu_custom_call" | custom-call | bytes 320 | tf_op jit(solution)/shard_map/put/pallas_call | solution.py:236
  70.2 4.1 %collective-permute-done.11.refs_2_ = bf16[640,640]{1,0:T(8,128)(2,1)S(1)} collective-permute-done((bf16[640,640]{1,0:T(8,128)(2,1)S(1)}, bf16[640,640]{1,0:T(8,128)(2,1)S(1)}, u32[]{:S(2)}, u32[]{:S(2)}) %collective-permute-start.11) | collective-permute-done | bytes 819232 | tf_op jit(solution)/shard_map/ppermute | solution.py:199
  74.3 3.4 %collective-permute-done.10.refs_1_ = bf16[640,640]{1,0:T(8,128)(2,1)S(1)} collective-permute-done((bf16[640,640]{1,0:T(8,128)(2,1)S(1)}, bf16[640,640]{1,0:T(8,128)(2,1)S(1)}, u32[]{:S(2)}, u32[]{:S(2)}) %collective-permute-start.10) | collective-permute-done | bytes 819232 | tf_op jit(solution)/shard_map/ppermute | solution.py:196
  77.7 3.7 %collective-permute-done.13 = bf16[96,5120]{1,0:T(8,128)(2,1)S(1)} collective-permute-done((bf16[96,5120]{1,0:T(8,128)(2,1)S(1)}, bf16[96,5120]{1,0:T(8,128)(2,1)S(1)}, u32[]{:S(2)}, u32[]{:S(2)}) %collective-permute-start.13) | collective-permute-done | bytes 983072 | tf_op jit(solution)/shard_map/ppermute | solution.py:199
  81.4 2.7 %collective-permute-done.12 = bf16[96,5120]{1,0:T(8,128)(2,1)S(1)} collective-permute-done((bf16[96,5120]{1,0:T(8,128)(2,1)S(1)}, bf16[96,5120]{1,0:T(8,128)(2,1)S(1)}, u32[]{:S(2)}, u32[]{:S(2)}) %collective-permute-start.12) | collective-permute-done | bytes 983072 | tf_op jit(solution)/shard_map/ppermute | solution.py:196
  84.6 1.7 collective-permute-start.15
  87.4 0.8 put.6
  88.2 3.2 %collective-permute-done.16 = bf16[32,5120]{1,0:T(8,128)(2,1)S(1)} collective-permute-done((bf16[32,5120]{1,0:T(8,128)(2,1)S(1)}, bf16[32,5120]{1,0:T(8,128)(2,1)S(1)}, u32[]{:S(2)}, u32[]{:S(2)}) %collective-permute-start.16) | collective-permute-done | bytes 327712 | tf_op jit(solution)/shard_map/ppermute | solution.py:199
  91.4 1.5 collective-permute-done.15
  93.6 1.9 collective-permute-done.18
  96.1 8.3 %convolution_convert_fusion = bf16[1024,640]{1,0:T(8,128)(2,1)S(1)} fusion(bf16[1024,5120]{1,0:T(8,128)(2,1)S(1)} %bitcast.126, bf16[5120,640]{1,0:T(8,128)(2,1)S(1)} %bitcast.118), kind=kOutput, calls=%fused_computation.11 | convolution fusion | flops 6711541760 | bytes 18350080 | tf_op jit(solution)/shard_map/dot_general | solution.py:394
  104.4 25.2 %all_to_all.18.packed = bf16[16,64,640]{2,1,0:T(8,128)(2,1)S(1)} all-to-all(bf16[16,64,640]{2,1,0:T(8,128)(2,1)S(1)} %bitcast.147), channel_id=1, replica_groups=mesh['wide'=16,'narrow'=8] {'wide'}, dimensions={0} | all-to-all | bytes 2621440 | tf_op jit(solution)/shard_map/all_to_all | solution.py:395
  129.8 1.1 collective-permute-start.25
  130.9 1.0 collective-permute-start.23
  132.0 7.9 %attend.1 = bf16[64,8192]{1,0:T(8,128)(2,1)S(1)} custom-call(s32[4]{0:T(128)S(1)} %copy-done.13, s32[4]{0:T(128)S(1)} %copy-done.14, bf16[16,64,640]{2,1,0:T(8,128)(2,1)S(1)} %all_to_all.18.packed, f32[64,128]{1,0:T(8,128)S(1)} %broadcast_in_dim.39.inverse, f32[64,128]{1,0:T(8,128)S(1)} %get-tuple-element.82.cosine, f32[64,128]{1,0:T(8,128)S(1)} %get-tuple-element.83.sine, ...), custom_call_target="tpu_custom_call" | custom-call | flops 570425344 | bytes 6553600 | tf_op jit(solution)/shard_map/attend/pallas_call | solution.py:137
  139.9 2.5 %collective-permute-start.21 = (bf16[64,8192]{1,0:T(8,128)(2,1)S(1)}, bf16[64,8192]{1,0:T(8,128)(2,1)}, u32[]{:S(2)}, u32[]{:S(2)}) collective-permute-start(bf16[64,8192]{1,0:T(8,128)(2,1)S(1)} %attend.1), channel_id=1, source_target_pairs={{0,6},{1,7},{2,0},{3,1},{4,2},{5,3},{6,4},{7,5},{8,14},{9,15},{10,... | collective-permute-start | bytes 3145736 | tf_op jit(solution)/shard_map/ppermute | solution.py:199
  142.4 10.6 %collective-permute-done.25.refs_5_ = bf16[768,640]{1,0:T(8,128)(2,1)S(1)} collective-permute-done((bf16[768,640]{1,0:T(8,128)(2,1)S(1)}, bf16[768,640]{1,0:T(8,128)(2,1)S(1)}, u32[]{:S(2)}, u32[]{:S(2)}) %collective-permute-start.25) | collective-permute-done | bytes 983072 | tf_op jit(solution)/shard_map/ppermute | solution.py:199
  153.1 3.0 %collective-permute-start.26 = (bf16[256,640]{1,0:T(8,128)(2,1)S(1)}, bf16[256,640]{1,0:T(8,128)(2,1)S(1)}, u32[]{:S(2)}, u32[]{:S(2)}) collective-permute-start(bf16[256,640]{1,0:T(8,128)(2,1)S(1)} %slice.109), channel_id=1, source_target_pairs={{0,48},{8,56},{16,0},{24,8},{32,16},{40,24},{48,32},{56,40},{64,11... | collective-permute-start | bytes 983048 | tf_op jit(solution)/shard_map/ppermute | solution.py:199
  156.3 3.8 %pack.1 = bf16[3584,640]{1,0:T(8,128)(2,1)} custom-call(bf16[512,640]{1,0:T(8,128)(2,1)S(1)} %copy-done.4, bf16[512,640]{1,0:T(8,128)(2,1)S(1)} %copy-done.2, bf16[512,640]{1,0:T(8,128)(2,1)S(1)} %collective-permute-done.1.refs_2_, bf16[512,640]{1,0:T(8,128)(2,1)S(1)} %collective-permute-done.14.refs_3_, ...), custom_call_target="tpu_custom_call" | custom-call | bytes 3584 | tf_op jit(solution)/shard_map/pack/pallas_call | solution.py:287
  160.1 2.7 %collective-permute-done.26.refs_7_ = bf16[256,640]{1,0:T(8,128)(2,1)S(1)} collective-permute-done((bf16[256,640]{1,0:T(8,128)(2,1)S(1)}, bf16[256,640]{1,0:T(8,128)(2,1)S(1)}, u32[]{:S(2)}, u32[]{:S(2)}) %collective-permute-start.26) | collective-permute-done | bytes 327712 | tf_op jit(solution)/shard_map/ppermute | solution.py:199
  162.8 3.5 %collective-permute-done.24.refs_6_ = bf16[256,640]{1,0:T(8,128)(2,1)S(1)} collective-permute-done((bf16[256,640]{1,0:T(8,128)(2,1)S(1)}, bf16[256,640]{1,0:T(8,128)(2,1)S(1)}, u32[]{:S(2)}, u32[]{:S(2)}) %collective-permute-start.24) | collective-permute-done | bytes 327712 | tf_op jit(solution)/shard_map/ppermute | solution.py:196
  166.3 0.9 pad_maximum_fusion.10
  167.3 1.0 copy-done.17
  169.3 2.1 broadcast_select_fusion
  171.4 1.4 collective-permute-start.29
  172.8 1.3 collective-permute-start.28
  174.1 0.7 collective-permute-start.27
  174.8 2.3 %pad_maximum_fusion = bf16[256,8192]{1,0:T(8,128)(2,1)S(1)} fusion(bf16[64,8192]{1,0:T(8,128)(2,1)} %collective-permute-done.21, bf16[64,8192]{1,0:T(8,128)(2,1)} %copy-done.17, bf16[64,8192]{1,0:T(8,128)(2,1)} %collective-permute-done.22, bf16[64,8192]{1,0:T(8,128)(2,1)} %copy-done), kind=kLoop, calls=%fused_computation | loop fusion | flops 16777216 | bytes 8388608 | tf_op jit(solution)/shard_map/concatenate | solution.py:442
  177.2 2.3 %put.7.refs_0_ = bf16[32,256,640]{2,1,0:T(8,128)(2,1)S(1)} custom-call(s32[16]{0:T(128)S(1)} %stack.284.places, bf16[512,640]{1,0:T(8,128)(2,1)S(1)} %copy-done.5, bf16[512,640]{1,0:T(8,128)(2,1)S(1)} %copy-done.3, bf16[512,640]{1,0:T(8,128)(2,1)S(1)} %collective-permute-done.1.refs_2_, bf16[512,640]{1,0:T(8,128)(2,1)S(1)} %collective-permute-done.14.refs_3_, ...), custom_call_target="tpu_custom_call" | custom-call | bytes 256 | tf_op jit(solution)/shard_map/put/pallas_call | solution.py:236
  179.5 4.6 %put.8 = bf16[32,256,640]{2,1,0:T(8,128)(2,1)S(1)} custom-call(s32[16]{0:T(128)S(1)} %stack.267.places, bf16[32,256,640]{2,1,0:T(8,128)(2,1)S(1)} %put.7.refs_0_, bf16[3584,640]{1,0:T(8,128)(2,1)} %collective-permute-done.30.refs_1_, bf16[512,640]{1,0:T(8,128)(2,1)S(1)} %bitcast.121), custom_call_target="tpu_custom_call", output_to_operand_aliasing={{}: (1, {})} | custom-call | bytes 256 | tf_op jit(solution)/shard_map/put/pallas_call | solution.py:236
  184.2 3.4 %convolution_convert_fusion.1.refs_0_ = bf16[256,640]{1,0:T(8,128)(2,1)S(1)} fusion(bf16[256,8192]{1,0:T(8,128)(2,1)S(1)} %pad_maximum_fusion, bf16[8192,640]{1,0:T(8,128)(2,1)S(1)} %bitcast.115), kind=kOutput, calls=%fused_computation.14 | convolution fusion | flops 2684518400 | bytes 15007744 | tf_op jit(solution)/shard_map/dot_general | solution.py:476
  187.6 9.1 %collective-permute-done.29 = bf16[64,8192]{1,0:T(8,128)(2,1)S(1)} collective-permute-done((bf16[64,8192]{1,0:T(8,128)(2,1)S(1)}, bf16[64,8192]{1,0:T(8,128)(2,1)S(1)}, u32[]{:S(2)}, u32[]{:S(2)}) %collective-permute-start.29) | collective-permute-done | bytes 1048608 | tf_op jit(solution)/shard_map/ppermute | solution.py:202
  196.7 1.0 collective-permute-done.28
  197.7 2.2 %collective-permute-done.27 = bf16[64,8192]{1,0:T(8,128)(2,1)S(1)} collective-permute-done((bf16[64,8192]{1,0:T(8,128)(2,1)S(1)}, bf16[64,8192]{1,0:T(8,128)(2,1)S(1)}, u32[]{:S(2)}, u32[]{:S(2)}) %collective-permute-start.27) | collective-permute-done | bytes 1048608 | tf_op jit(solution)/shard_map/ppermute | solution.py:196
  200.0 1.5 collective-permute-start.35
  202.1 3.2 %collective-permute-start.33 = (bf16[16,8192]{1,0:T(8,128)(2,1)S(1)}, bf16[16,8192]{1,0:T(8,128)(2,1)S(1)}, u32[]{:S(2)}, u32[]{:S(2)}) collective-permute-start(bf16[16,8192]{1,0:T(8,128)(2,1)S(1)} %slice.101), channel_id=1, source_target_pairs={{0,6},{1,7},{2,0},{3,1},{4,2},{5,3},{6,4},{7,5},{8,14},{9,15},{10,... | collective-permute-start | bytes 786440 | tf_op jit(solution)/shard_map/ppermute | solution.py:199
  205.3 2.6 %fusion.7.refs_1_ = bf16[192,640]{1,0:T(8,128)(2,1)S(1)} fusion(bf16[8192,640]{1,0:T(8,128)(2,1)S(1)} %bitcast.116, bf16[64,8192]{1,0:T(8,128)(2,1)S(1)} %collective-permute-done.28, bf16[64,8192]{1,0:T(8,128)(2,1)S(1)} %collective-permute-done.27, bf16[64,8192]{1,0:T(8,128)(2,1)S(1)} %collective-permute-done.29), kind=kOutput, calls=%fused_computation.15 | convolution fusion | flops 2022825984 | bytes 13877248 | tf_op jit(solution)/shard_map/dot_general | solution.py:476
  208.0 1.4 order.1
  209.4 3.2 %collective-permute-done.34 = bf16[16,8192]{1,0:T(8,128)(2,1)S(1)} collective-permute-done((bf16[16,8192]{1,0:T(8,128)(2,1)S(1)}, bf16[16,8192]{1,0:T(8,128)(2,1)S(1)}, u32[]{:S(2)}, u32[]{:S(2)}) %collective-permute-start.34) | collective-permute-done | bytes 262176 | tf_op jit(solution)/shard_map/ppermute | solution.py:202
  212.6 1.8 convolution_convert_fusion.2.refs_1_
  214.4 0.6 put.9
  (132 shorter events, 6.6 us)
Async XLA Ops:
  0.0 34.8 %collective-permute-start.1 = (bf16[512,640]{1,0:T(8,128)(2,1)}, bf16[512,640]{1,0:T(8,128)(2,1)S(1)}, u32[]{:S(2)}, u32[]{:S(2)}) collective-permute-start(bf16[512,640]{1,0:T(8,128)(2,1)} %refs_0_.3), channel_id=1, source_target_pairs={{0,48},{8,56},{16,0},{24,8},{32,16},{40,24},{48,32},{56,40},{64,11... | collective-permute-start | bytes 1966088 | tf_op jit(solution)/shard_map/ppermute | solution.py:199
  3.1 31.7 %collective-permute-start = (bf16[512,640]{1,0:T(8,128)(2,1)}, bf16[512,640]{1,0:T(8,128)(2,1)S(1)}, u32[]{:S(2)}, u32[]{:S(2)}) collective-permute-start(bf16[512,640]{1,0:T(8,128)(2,1)} %refs_0_.3), channel_id=1, source_target_pairs={{0,16},{8,24},{16,32},{24,40},{32,48},{40,56},{48,0},{56,8},{64,80... | collective-permute-start | bytes 1966088 | tf_op jit(solution)/shard_map/ppermute | solution.py:196
  3.1 31.7 %collective-permute-start.3 = (bf16[640,640]{1,0:T(8,128)(2,1)}, bf16[640,640]{1,0:T(8,128)(2,1)S(1)}, u32[]{:S(2)}, u32[]{:S(2)}) collective-permute-start(bf16[640,640]{1,0:T(8,128)(2,1)} %refs_0_.1), channel_id=1, source_target_pairs={{0,2},{1,3},{2,4},{3,5},{4,6},{5,7},{6,0},{7,1},{8,10},{9,11},{10,... | collective-permute-start | bytes 2457608 | tf_op jit(solution)/shard_map/ppermute | solution.py:196
  5.0 29.8 %collective-permute-start.2 = (bf16[640,640]{1,0:T(8,128)(2,1)}, bf16[640,640]{1,0:T(8,128)(2,1)}, u32[]{:S(2)}, u32[]{:S(2)}) collective-permute-start(bf16[640,640]{1,0:T(8,128)(2,1)} %refs_0_.1), channel_id=1, source_target_pairs={{0,1},{1,0},{2,3},{3,2},{4,5},{5,4},{6,7},{7,6},{8,9},{9,8},{10,11... | collective-permute-start | bytes 2457608 | tf_op jit(solution)/shard_map/ppermute | solution.py:202
  6.5 28.3 %collective-permute-start.4 = (bf16[640,640]{1,0:T(8,128)(2,1)}, bf16[640,640]{1,0:T(8,128)(2,1)}, u32[]{:S(2)}, u32[]{:S(2)}) collective-permute-start(bf16[640,640]{1,0:T(8,128)(2,1)} %refs_0_.1), channel_id=1, source_target_pairs={{0,6},{1,7},{2,0},{3,1},{4,2},{5,3},{6,4},{7,5},{8,14},{9,15},{10,... | collective-permute-start | bytes 2457608 | tf_op jit(solution)/shard_map/ppermute | solution.py:199
  8.6 25.0 %all-to-all-start = ((bf16[8,64,640]{2,1,0:T(8,128)(2,1)}), bf16[8,64,640]{2,1,0:T(8,128)(2,1)S(1)}, u32[]{:S(2)}, u32[]{:S(2)}) async-start(bf16[8,64,640]{2,1,0:T(8,128)(2,1)} %bitcast.150), calls=%async_computation | async-start | bytes 1310720 | tf_op jit(solution)/shard_map/all_to_all | solution.py:320
  33.9 19.5 %copy-start.4 = (bf16[512,640]{1,0:T(8,128)(2,1)S(1)}, bf16[512,640]{1,0:T(8,128)(2,1)}, u32[]{:S(2)}) copy-start(bf16[512,640]{1,0:T(8,128)(2,1)} %refs_0_.3) | copy-start | bytes 1966084
  34.8 94.8 %copy-start.1 = (bf16[512,640]{1,0:T(8,128)(2,1)}, bf16[512,640]{1,0:T(8,128)(2,1)S(1)}, u32[]{:S(2)}) copy-start(bf16[512,640]{1,0:T(8,128)(2,1)S(1)} %collective-permute-done.refs_1_) | copy-start | bytes 1966084
  34.8 23.3 %collective-permute-start.6 = (bf16[640,640]{1,0:T(8,128)(2,1)}, bf16[640,640]{1,0:T(8,128)(2,1)S(1)}, u32[]{:S(2)}, u32[]{:S(2)}) collective-permute-start(bf16[640,640]{1,0:T(8,128)(2,1)} %collective-permute-done.2.refs_3_), channel_id=1, source_target_pairs={{0,6},{1,7},{2,0},{3,1},{4,2},{5,3},{6,4},{7,5},{8,14},{9,15},{10,... | collective-permute-start | bytes 2457608 | tf_op jit(solution)/shard_map/ppermute | solution.py:199
  37.7 20.4 %collective-permute-start.5 = (bf16[640,640]{1,0:T(8,128)(2,1)}, bf16[640,640]{1,0:T(8,128)(2,1)S(1)}, u32[]{:S(2)}, u32[]{:S(2)}) collective-permute-start(bf16[640,640]{1,0:T(8,128)(2,1)} %collective-permute-done.2.refs_3_), channel_id=1, source_target_pairs={{0,2},{1,3},{2,4},{3,5},{4,6},{5,7},{6,0},{7,1},{8,10},{9,11},{10,... | collective-permute-start | bytes 2457608 | tf_op jit(solution)/shard_map/ppermute | solution.py:196
  38.0 15.4 %collective-permute-start.9 = (bf16[64,5120]{1,0:T(8,128)(2,1)S(1)}, bf16[64,5120]{1,0:T(8,128)(2,1)S(1)}, u32[]{:S(2)}, u32[]{:S(2)}) collective-permute-start(bf16[64,5120]{1,0:T(8,128)(2,1)S(1)} %multiply_convert_fusion), channel_id=1, source_target_pairs={{0,64},{8,72},{16,80},{24,88},{32,96},{40,104},{48,112},{56,120},{... | collective-permute-start | bytes 1966088 | tf_op jit(solution)/shard_map/ppermute | solution.py:202
  40.8 15.6 %collective-permute-start.8 = (bf16[64,5120]{1,0:T(8,128)(2,1)S(1)}, bf16[64,5120]{1,0:T(8,128)(2,1)S(1)}, u32[]{:S(2)}, u32[]{:S(2)}) collective-permute-start(bf16[64,5120]{1,0:T(8,128)(2,1)S(1)} %multiply_convert_fusion), channel_id=1, source_target_pairs={{0,48},{8,56},{16,0},{24,8},{32,16},{40,24},{48,32},{56,40},{64,11... | collective-permute-start | bytes 1966088 | tf_op jit(solution)/shard_map/ppermute | solution.py:199
  43.7 14.4 %collective-permute-start.7 = (bf16[64,5120]{1,0:T(8,128)(2,1)S(1)}, bf16[64,5120]{1,0:T(8,128)(2,1)S(1)}, u32[]{:S(2)}, u32[]{:S(2)}) collective-permute-start(bf16[64,5120]{1,0:T(8,128)(2,1)S(1)} %multiply_convert_fusion), channel_id=1, source_target_pairs={{0,16},{8,24},{16,32},{24,40},{32,48},{40,56},{48,0},{56,8},{64,80... | collective-permute-start | bytes 1966088 | tf_op jit(solution)/shard_map/ppermute | solution.py:196
  50.2 16.3 %copy-start.12 = (bf16[640,640]{1,0:T(8,128)(2,1)S(1)}, bf16[640,640]{1,0:T(8,128)(2,1)}, u32[]{:S(2)}) copy-start(bf16[640,640]{1,0:T(8,128)(2,1)} %refs_0_.1) | copy-start | bytes 2457604
  53.4 16.9 %collective-permute-start.14 = (bf16[512,640]{1,0:T(8,128)(2,1)S(1)}, bf16[512,640]{1,0:T(8,128)(2,1)S(1)}, u32[]{:S(2)}, u32[]{:S(2)}) collective-permute-start(bf16[512,640]{1,0:T(8,128)(2,1)S(1)} %copy-done.4), channel_id=1, source_target_pairs={{0,64},{8,72},{16,80},{24,88},{32,96},{40,104},{48,112},{56,120},{... | collective-permute-start | bytes 1966088 | tf_op jit(solution)/shard_map/ppermute | solution.py:202
  58.4 15.9 %collective-permute-start.11 = (bf16[640,640]{1,0:T(8,128)(2,1)S(1)}, bf16[640,640]{1,0:T(8,128)(2,1)S(1)}, u32[]{:S(2)}, u32[]{:S(2)}) collective-permute-start(bf16[640,640]{1,0:T(8,128)(2,1)S(1)} %pad_maximum_fusion.8), channel_id=1, source_target_pairs={{0,6},{1,7},{2,0},{3,1},{4,2},{5,3},{6,4},{7,5},{8,14},{9,15},{10,... | collective-permute-start | bytes 2457608 | tf_op jit(solution)/shard_map/ppermute | solution.py:199
  61.4 16.3 %collective-permute-start.10 = (bf16[640,640]{1,0:T(8,128)(2,1)S(1)}, bf16[640,640]{1,0:T(8,128)(2,1)S(1)}, u32[]{:S(2)}, u32[]{:S(2)}) collective-permute-start(bf16[640,640]{1,0:T(8,128)(2,1)S(1)} %pad_maximum_fusion.7), channel_id=1, source_target_pairs={{0,2},{1,3},{2,4},{3,5},{4,6},{5,7},{6,0},{7,1},{8,10},{9,11},{10,... | collective-permute-start | bytes 2457608 | tf_op jit(solution)/shard_map/ppermute | solution.py:196
  61.7 19.8 %collective-permute-start.13 = (bf16[96,5120]{1,0:T(8,128)(2,1)S(1)}, bf16[96,5120]{1,0:T(8,128)(2,1)S(1)}, u32[]{:S(2)}, u32[]{:S(2)}) collective-permute-start(bf16[96,5120]{1,0:T(8,128)(2,1)S(1)} %get-tuple-element.125), channel_id=1, source_target_pairs={{0,48},{8,56},{16,0},{24,8},{32,16},{40,24},{48,32},{56,40},{64,11... | collective-permute-start | bytes 2949128 | tf_op jit(solution)/shard_map/ppermute | solution.py:199
  62.7 21.4 %collective-permute-start.12 = (bf16[96,5120]{1,0:T(8,128)(2,1)S(1)}, bf16[96,5120]{1,0:T(8,128)(2,1)S(1)}, u32[]{:S(2)}, u32[]{:S(2)}) collective-permute-start(bf16[96,5120]{1,0:T(8,128)(2,1)S(1)} %get-tuple-element.126), channel_id=1, source_target_pairs={{0,16},{8,24},{16,32},{24,40},{32,48},{40,56},{48,0},{56,8},{64,80... | collective-permute-start | bytes 2949128 | tf_op jit(solution)/shard_map/ppermute | solution.py:196
  66.4 19.9 %slice-start = ((s8[10485760]{0:T(1024)(128)(4,1)}), s8[4194304]{0:T(1024)(128)(4,1)S(1)}, s32[]{:S(2)}) async-start(s8[10485760]{0:T(1024)(128)(4,1)} %bitcast.124), calls=%async_computation.2 | async-start | bytes 8388608
  66.4 19.9 %slice-start.1 = ((s8[10485760]{0:T(1024)(128)(4,1)}), s8[4194304]{0:T(1024)(128)(4,1)S(1)}, s32[]{:S(2)}) async-start(s8[10485760]{0:T(1024)(128)(4,1)} %bitcast.124), calls=%async_computation.3 | async-start | bytes 8388608
  69.9 16.5 %slice-start.2 = ((s8[10485760]{0:T(1024)(128)(4,1)}), s8[2097152]{0:T(1024)(128)(4,1)S(1)}, s32[]{:S(2)}) async-start(s8[10485760]{0:T(1024)(128)(4,1)} %bitcast.124), calls=%async_computation.4 | async-start | bytes 4194304
  84.3 7.1 %collective-permute-start.16 = (bf16[32,5120]{1,0:T(8,128)(2,1)S(1)}, bf16[32,5120]{1,0:T(8,128)(2,1)S(1)}, u32[]{:S(2)}, u32[]{:S(2)}) collective-permute-start(bf16[32,5120]{1,0:T(8,128)(2,1)S(1)} %slice.91), channel_id=1, source_target_pairs={{0,48},{8,56},{16,0},{24,8},{32,16},{40,24},{48,32},{56,40},{64,11... | collective-permute-start | bytes 983048 | tf_op jit(solution)/shard_map/ppermute | solution.py:199
  84.6 8.3 %collective-permute-start.15 = (bf16[32,5120]{1,0:T(8,128)(2,1)S(1)}, bf16[32,5120]{1,0:T(8,128)(2,1)S(1)}, u32[]{:S(2)}, u32[]{:S(2)}) collective-permute-start(bf16[32,5120]{1,0:T(8,128)(2,1)S(1)} %slice.90), channel_id=1, source_target_pairs={{0,16},{8,24},{16,32},{24,40},{32,48},{40,56},{48,0},{56,8},{64,80... | collective-permute-start | bytes 983048 | tf_op jit(solution)/shard_map/ppermute | solution.py:196
  86.8 6.6 %collective-permute-start.17 = (bf16[2,96,5120]{2,1,0:T(8,128)(2,1)S(1)}, bf16[2,96,5120]{2,1,0:T(8,128)(2,1)S(1)}, u32[]{:S(2)}, u32[]{:S(2)}) collective-permute-start(bf16[2,96,5120]{2,1,0:T(8,128)(2,1)S(1)} %pad_maximum_fusion.2), channel_id=1, source_target_pairs={{0,8},{8,0},{16,24},{24,16},{32,40},{40,32},{48,56},{56,48},{64,72... | collective-permute-start | bytes 5898248 | tf_op jit(solution)/shard_map/ppermute | solution.py:205
  86.9 8.7 %collective-permute-start.19 = (bf16[4,64,5120]{2,1,0:T(8,128)(2,1)S(1)}, bf16[4,64,5120]{2,1,0:T(8,128)(2,1)S(1)}, u32[]{:S(2)}, u32[]{:S(2)}) collective-permute-start(bf16[4,64,5120]{2,1,0:T(8,128)(2,1)S(1)} %pad_maximum_fusion.1), channel_id=1, source_target_pairs={{0,8},{8,0},{16,24},{24,16},{32,40},{40,32},{48,56},{56,48},{64,72... | collective-permute-start | bytes 7864328 | tf_op jit(solution)/shard_map/ppermute | solution.py:205
  93.0 2.5 %collective-permute-start.18 = (bf16[2,32,5120]{2,1,0:T(8,128)(2,1)S(1)}, bf16[2,32,5120]{2,1,0:T(8,128)(2,1)S(1)}, u32[]{:S(2)}, u32[]{:S(2)}) collective-permute-start(bf16[2,32,5120]{2,1,0:T(8,128)(2,1)S(1)} %pad_maximum_fusion.9), channel_id=1, source_target_pairs={{0,8},{8,0},{16,24},{24,16},{32,40},{40,32},{48,56},{56,48},{64,72... | collective-permute-start | bytes 1966088 | tf_op jit(solution)/shard_map/ppermute | solution.py:205
  96.0 35.9 %copy-start.13 = (s32[4]{0:T(128)S(1)}, s32[4]{0:T(128)}, u32[]{:S(2)}) copy-start(s32[4]{0:T(128)} %fills.1) | copy-start | bytes 52
  96.0 35.9 %copy-start.14 = (s32[4]{0:T(128)S(1)}, s32[4]{0:T(128)}, u32[]{:S(2)}) copy-start(s32[4]{0:T(128)} %spans.1) | copy-start | bytes 52
  96.0 35.9 %copy-start.15 = (f32[128]{0:T(128)S(1)}, f32[128]{0:T(128)}, u32[]{:S(2)}) copy-start(f32[128]{0:T(128)} %param.13) | copy-start | bytes 1540
  96.1 35.9 %copy-start.16 = (f32[128]{0:T(128)S(1)}, f32[128]{0:T(128)}, u32[]{:S(2)}) copy-start(f32[128]{0:T(128)} %param.14) | copy-start | bytes 1540
  104.3 27.6 %copy-start.6 = (bf16[4,256,1024]{2,1,0:T(8,128)(2,1)S(1)}, bf16[4,256,1024]{2,1,0:T(8,128)(2,1)}, u32[]{:S(2)}) copy-start(bf16[4,256,1024]{2,1,0:T(8,128)(2,1)} %keys.1) | copy-start | bytes 6291460
  104.4 27.6 %copy-start.7 = (bf16[4,256,1024]{2,1,0:T(8,128)(2,1)S(1)}, bf16[4,256,1024]{2,1,0:T(8,128)(2,1)}, u32[]{:S(2)}) copy-start(bf16[4,256,1024]{2,1,0:T(8,128)(2,1)} %values.1) | copy-start | bytes 6291460
  129.6 26.7 %copy-start.2 = (bf16[512,640]{1,0:T(8,128)(2,1)S(1)}, bf16[512,640]{1,0:T(8,128)(2,1)}, u32[]{:S(2)}) copy-start(bf16[512,640]{1,0:T(8,128)(2,1)} %copy-done.1) | copy-start | bytes 1966084
  129.8 23.3 %collective-permute-start.25 = (bf16[768,640]{1,0:T(8,128)(2,1)S(1)}, bf16[768,640]{1,0:T(8,128)(2,1)S(1)}, u32[]{:S(2)}, u32[]{:S(2)}) collective-permute-start(bf16[768,640]{1,0:T(8,128)(2,1)S(1)} %get-tuple-element.123), channel_id=1, source_target_pairs={{0,48},{8,56},{16,0},{24,8},{32,16},{40,24},{48,32},{56,40},{64,11... | collective-permute-start | bytes 2949128 | tf_op jit(solution)/shard_map/ppermute | solution.py:199
  130.9 25.3 %collective-permute-start.23 = (bf16[768,640]{1,0:T(8,128)(2,1)S(1)}, bf16[768,640]{1,0:T(8,128)(2,1)S(1)}, u32[]{:S(2)}, u32[]{:S(2)}) collective-permute-start(bf16[768,640]{1,0:T(8,128)(2,1)S(1)} %get-tuple-element.124), channel_id=1, source_target_pairs={{0,16},{8,24},{16,32},{24,40},{32,48},{40,56},{48,0},{56,8},{64,80... | collective-permute-start | bytes 2949128 | tf_op jit(solution)/shard_map/ppermute | solution.py:196
  139.8 16.3 %copy-start = (bf16[64,8192]{1,0:T(8,128)(2,1)}, bf16[64,8192]{1,0:T(8,128)(2,1)S(1)}, u32[]{:S(2)}) copy-start(bf16[64,8192]{1,0:T(8,128)(2,1)S(1)} %attend.1) | copy-start | bytes 3145732
  139.9 27.4 %collective-permute-start.22 = (bf16[64,8192]{1,0:T(8,128)(2,1)S(1)}, bf16[64,8192]{1,0:T(8,128)(2,1)}, u32[]{:S(2)}, u32[]{:S(2)}) collective-permute-start(bf16[64,8192]{1,0:T(8,128)(2,1)S(1)} %attend.1), channel_id=1, source_target_pairs={{0,1},{1,0},{2,3},{3,2},{4,5},{5,4},{6,7},{7,6},{8,9},{9,8},{10,11... | collective-permute-start | bytes 3145736 | tf_op jit(solution)/shard_map/ppermute | solution.py:202
  139.9 27.3 %collective-permute-start.21 = (bf16[64,8192]{1,0:T(8,128)(2,1)S(1)}, bf16[64,8192]{1,0:T(8,128)(2,1)}, u32[]{:S(2)}, u32[]{:S(2)}) collective-permute-start(bf16[64,8192]{1,0:T(8,128)(2,1)S(1)} %attend.1), channel_id=1, source_target_pairs={{0,6},{1,7},{2,0},{3,1},{4,2},{5,3},{6,4},{7,5},{8,14},{9,15},{10,... | collective-permute-start | bytes 3145736 | tf_op jit(solution)/shard_map/ppermute | solution.py:199
  142.4 24.8 %collective-permute-start.20 = (bf16[64,8192]{1,0:T(8,128)(2,1)S(1)}, bf16[64,8192]{1,0:T(8,128)(2,1)S(1)}, u32[]{:S(2)}, u32[]{:S(2)}) collective-permute-start(bf16[64,8192]{1,0:T(8,128)(2,1)S(1)} %attend.1), channel_id=1, source_target_pairs={{0,2},{1,3},{2,4},{3,5},{4,6},{5,7},{6,0},{7,1},{8,10},{9,11},{10,... | collective-permute-start | bytes 3145736 | tf_op jit(solution)/shard_map/ppermute | solution.py:196
  153.1 9.7 %collective-permute-start.26 = (bf16[256,640]{1,0:T(8,128)(2,1)S(1)}, bf16[256,640]{1,0:T(8,128)(2,1)S(1)}, u32[]{:S(2)}, u32[]{:S(2)}) collective-permute-start(bf16[256,640]{1,0:T(8,128)(2,1)S(1)} %slice.109), channel_id=1, source_target_pairs={{0,48},{8,56},{16,0},{24,8},{32,16},{40,24},{48,32},{56,40},{64,11... | collective-permute-start | bytes 983048 | tf_op jit(solution)/shard_map/ppermute | solution.py:199
  156.2 10.1 %collective-permute-start.24 = (bf16[256,640]{1,0:T(8,128)(2,1)S(1)}, bf16[256,640]{1,0:T(8,128)(2,1)S(1)}, u32[]{:S(2)}, u32[]{:S(2)}) collective-permute-start(bf16[256,640]{1,0:T(8,128)(2,1)S(1)} %slice.108), channel_id=1, source_target_pairs={{0,16},{8,24},{16,32},{24,40},{32,48},{40,56},{48,0},{56,8},{64,80... | collective-permute-start | bytes 983048 | tf_op jit(solution)/shard_map/ppermute | solution.py:196
  162.8 4.5 %copy-start.8 = (bf16[256,640]{1,0:T(8,128)(2,1)}, bf16[256,640]{1,0:T(8,128)(2,1)S(1)}, u32[]{:S(2)}) copy-start(bf16[256,640]{1,0:T(8,128)(2,1)S(1)} %collective-permute-done.26.refs_7_) | copy-start | bytes 983044
  166.3 1.0 copy-start.10
  167.3 1.0 copy-start.17
  168.3 11.2 %collective-permute-start.30 = (bf16[3584,640]{1,0:T(8,128)(2,1)}, bf16[3584,640]{1,0:T(8,128)(2,1)}, u32[]{:S(2)}, u32[]{:S(2)}) collective-permute-start(bf16[3584,640]{1,0:T(8,128)(2,1)} %pack.1), channel_id=1, source_target_pairs={{0,8},{8,0},{16,24},{24,16},{32,40},{40,32},{48,56},{56,48},{64,72... | collective-permute-start | bytes 13762568 | tf_op jit(solution)/shard_map/ppermute | solution.py:205
  168.6 8.5 %copy-start.3 = (bf16[512,640]{1,0:T(8,128)(2,1)S(1)}, bf16[512,640]{1,0:T(8,128)(2,1)}, u32[]{:S(2)}) copy-start(bf16[512,640]{1,0:T(8,128)(2,1)} %copy-done.1) | copy-start | bytes 1966084
  168.6 8.5 %copy-start.5 = (bf16[512,640]{1,0:T(8,128)(2,1)S(1)}, bf16[512,640]{1,0:T(8,128)(2,1)}, u32[]{:S(2)}) copy-start(bf16[512,640]{1,0:T(8,128)(2,1)} %refs_0_.3) | copy-start | bytes 1966084
  168.6 8.5 %copy-start.9 = (bf16[256,640]{1,0:T(8,128)(2,1)S(1)}, bf16[256,640]{1,0:T(8,128)(2,1)}, u32[]{:S(2)}) copy-start(bf16[256,640]{1,0:T(8,128)(2,1)} %copy-done.8) | copy-start | bytes 983044
  168.6 8.5 %copy-start.11 = (bf16[256,640]{1,0:T(8,128)(2,1)S(1)}, bf16[256,640]{1,0:T(8,128)(2,1)}, u32[]{:S(2)}) copy-start(bf16[256,640]{1,0:T(8,128)(2,1)} %copy-done.10) | copy-start | bytes 983044
  168.7 10.8 %collective-permute-start.31 = (bf16[2,256,640]{2,1,0:T(8,128)(2,1)}, bf16[2,256,640]{2,1,0:T(8,128)(2,1)S(1)}, u32[]{:S(2)}, u32[]{:S(2)}) collective-permute-start(bf16[2,256,640]{2,1,0:T(8,128)(2,1)} %pad_maximum_fusion.10), channel_id=1, source_target_pairs={{0,8},{8,0},{16,24},{24,16},{32,40},{40,32},{48,56},{56,48},{64,72... | collective-permute-start | bytes 1966088 | tf_op jit(solution)/shard_map/ppermute | solution.py:205
  171.4 25.3 %collective-permute-start.29 = (bf16[64,8192]{1,0:T(8,128)(2,1)S(1)}, bf16[64,8192]{1,0:T(8,128)(2,1)S(1)}, u32[]{:S(2)}, u32[]{:S(2)}) collective-permute-start(bf16[64,8192]{1,0:T(8,128)(2,1)S(1)} %get-tuple-element.117), channel_id=1, source_target_pairs={{0,1},{1,0},{2,3},{3,2},{4,5},{5,4},{6,7},{7,6},{8,9},{9,8},{10,11... | collective-permute-start | bytes 3145736 | tf_op jit(solution)/shard_map/ppermute | solution.py:202
  172.8 24.9 %collective-permute-start.28 = (bf16[64,8192]{1,0:T(8,128)(2,1)S(1)}, bf16[64,8192]{1,0:T(8,128)(2,1)S(1)}, u32[]{:S(2)}, u32[]{:S(2)}) collective-permute-start(bf16[64,8192]{1,0:T(8,128)(2,1)S(1)} %get-tuple-element.118), channel_id=1, source_target_pairs={{0,6},{1,7},{2,0},{3,1},{4,2},{5,3},{6,4},{7,5},{8,14},{9,15},{10,... | collective-permute-start | bytes 3145736 | tf_op jit(solution)/shard_map/ppermute | solution.py:199
  174.1 25.8 %collective-permute-start.27 = (bf16[64,8192]{1,0:T(8,128)(2,1)S(1)}, bf16[64,8192]{1,0:T(8,128)(2,1)S(1)}, u32[]{:S(2)}, u32[]{:S(2)}) collective-permute-start(bf16[64,8192]{1,0:T(8,128)(2,1)S(1)} %get-tuple-element.119), channel_id=1, source_target_pairs={{0,2},{1,3},{2,4},{3,5},{4,6},{5,7},{6,0},{7,1},{8,10},{9,11},{10,... | collective-permute-start | bytes 3145736 | tf_op jit(solution)/shard_map/ppermute | solution.py:196
  200.0 9.4 %collective-permute-start.35 = (bf16[16,8192]{1,0:T(8,128)(2,1)S(1)}, bf16[16,8192]{1,0:T(8,128)(2,1)S(1)}, u32[]{:S(2)}, u32[]{:S(2)}) collective-permute-start(bf16[16,8192]{1,0:T(8,128)(2,1)S(1)} %get-tuple-element.120), channel_id=1, source_target_pairs={{0,1},{1,0},{2,3},{3,2},{4,5},{5,4},{6,7},{7,6},{8,9},{9,8},{10,11... | collective-permute-start | bytes 786440 | tf_op jit(solution)/shard_map/ppermute | solution.py:202
  201.5 11.1 %collective-permute-start.34 = (bf16[16,8192]{1,0:T(8,128)(2,1)S(1)}, bf16[16,8192]{1,0:T(8,128)(2,1)S(1)}, u32[]{:S(2)}, u32[]{:S(2)}) collective-permute-start(bf16[16,8192]{1,0:T(8,128)(2,1)S(1)} %get-tuple-element.121), channel_id=1, source_target_pairs={{0,1},{1,0},{2,3},{3,2},{4,5},{5,4},{6,7},{7,6},{8,9},{9,8},{10,11... | collective-permute-start | bytes 786440 | tf_op jit(solution)/shard_map/ppermute | solution.py:202
  202.1 10.5 %collective-permute-start.32 = (bf16[16,8192]{1,0:T(8,128)(2,1)S(1)}, bf16[16,8192]{1,0:T(8,128)(2,1)S(1)}, u32[]{:S(2)}, u32[]{:S(2)}) collective-permute-start(bf16[16,8192]{1,0:T(8,128)(2,1)S(1)} %get-tuple-element.122), channel_id=1, source_target_pairs={{0,2},{1,3},{2,4},{3,5},{4,6},{5,7},{6,0},{7,1},{8,10},{9,11},{10,... | collective-permute-start | bytes 786440 | tf_op jit(solution)/shard_map/ppermute | solution.py:196
  202.1 10.5 %collective-permute-start.33 = (bf16[16,8192]{1,0:T(8,128)(2,1)S(1)}, bf16[16,8192]{1,0:T(8,128)(2,1)S(1)}, u32[]{:S(2)}, u32[]{:S(2)}) collective-permute-start(bf16[16,8192]{1,0:T(8,128)(2,1)S(1)} %slice.101), channel_id=1, source_target_pairs={{0,6},{1,7},{2,0},{3,1},{4,2},{5,3},{6,4},{7,5},{8,14},{9,15},{10,... | collective-permute-start | bytes 786440 | tf_op jit(solution)/shard_map/ppermute | solution.py:199

commit v5 on v3

--- a/solution.py
+++ b/solution.py
@@ -511,12 +511,12 @@
         (c_up, c_down, c_swap, c_swap_last, result)
     )
     result = put(
-        result,
+        result.reshape(8, rows, -1),
         (project_out(jnp.concatenate([c_swap, c_swap_last, c_up, c_down])),),
-        ((0, 0), (0, 1)),
-        jnp.stack([place_of(2, other, 0), place_of(2, other, 1)]),
-        16,
-        half_rows,
+        ((0, 0),),
+        jnp.stack([narrow.ring(2) * 2 + other]),
+        8,
+        rows,
     )
     return result.reshape(-1, result.shape[-1])
 

time: 215 us -> 215 us (level)
  transfers between devices with their start and end apart: 37 -> 37, of which waited for: 16 -> 16; matrix products, arithmetic and copies ran while one was open for 13% -> 12% of each run, Pallas kernels for 11% -> 11%
where the time goes in v5:
time: 215 us; the launch traced here: 214 us
  waiting for transfers between devices  75.5 us (35%)
  starting transfers between devices  50 us (23%)
  blocking collectives  25.2 us (12%)
  Pallas kernels  24.8 us (12%)
  matrix products  16.1 us (7%)
  local copies, waits for them, and re-layouts  15.7 us (7%)
  other arithmetic  5.94 us (3%)
    ppermute x12, starting transfers between devices, down(): return lax.ppermute(block, self.axis, self.pairs(-1, 0, 0))  28.3 us
    all_to_all x1, blocking collectives, shards(): lax.all_to_all(projected.reshape(wide_count, rows, -1), 'wide', split_axi...  25.2 us
    ppermute x12, waiting for transfers between devices, down(): return lax.ppermute(block, self.axis, self.pairs(-1, 0, 0))  24.6 us
    all_to_all x1, waiting for transfers between devices, shards(): lax.all_to_all(tokens, 'narrow', split_axis=0, concat_axis=1, tiled=True)  20.1 us
    ppermute x12, waiting for transfers between devices, up(): return lax.ppermute(block, self.axis, self.pairs(1, 0, 0))  14.8 us
    ppermute x7, waiting for transfers between devices, swap(): return lax.ppermute(block, self.axis, self.pairs(0, 1, 0))  14.1 us
    pallas_call x5, Pallas kernels, put(): pl.pallas_call(functools.partial(put_kernel, sources, aliased), grid_spec...  11.8 us
    ppermute x7, starting transfers between devices, swap(): return lax.ppermute(block, self.axis, self.pairs(0, 1, 0))  10.5 us
  transfers between devices with their start and end apart: 37, of which 16 were waited for; matrix products, arithmetic and copies ran while one was open for 12% of the time, Pallas kernels for 11%

profile of v5, /device:TPU:0, one launch (start us, length us, event | category | flops | bytes accessed | tf_op | source)
XLA Modules:
  0.0 214.3 jit_solution(3263558492437051561)
XLA Ops:
  0.0 3.1 %collective-permute-start.1 = (bf16[512,640]{1,0:T(8,128)(2,1)}, bf16[512,640]{1,0:T(8,128)(2,1)S(1)}, u32[]{:S(2)}, u32[]{:S(2)}) collective-permute-start(bf16[512,640]{1,0:T(8,128)(2,1)} %refs_0_.3), channel_id=1, source_target_pairs={{0,48},{8,56},{16,0},{24,8},{32,16},{40,24},{48,32},{56,40},{64,11... | collective-permute-start | bytes 1966088 | tf_op jit(solution)/shard_map/ppermute | solution.py:199
  3.1 1.9 collective-permute-start.3
  5.0 1.5 collective-permute-start.2
  6.5 2.1 collective-permute-start.4
  8.6 3.5 %all-to-all-start = ((bf16[8,64,640]{2,1,0:T(8,128)(2,1)}), bf16[8,64,640]{2,1,0:T(8,128)(2,1)S(1)}, u32[]{:S(2)}, u32[]{:S(2)}) async-start(bf16[8,64,640]{2,1,0:T(8,128)(2,1)} %bitcast.150), calls=%async_computation | async-start | bytes 1310720 | tf_op jit(solution)/shard_map/all_to_all | solution.py:320
  12.2 0.7 add_convert_fusion
  13.5 20.1 %all-to-all-done = bf16[8,64,640]{2,1,0:T(8,128)(2,1)S(1)} async-done(((bf16[8,64,640]{2,1,0:T(8,128)(2,1)}), bf16[8,64,640]{2,1,0:T(8,128)(2,1)S(1)}, u32[]{:S(2)}, u32[]{:S(2)}) %all-to-all-start) | async-done | bytes 655392 | tf_op jit(solution)/shard_map/all_to_all | solution.py:320
  34.0 2.9 %collective-permute-start.6 = (bf16[640,640]{1,0:T(8,128)(2,1)}, bf16[640,640]{1,0:T(8,128)(2,1)S(1)}, u32[]{:S(2)}, u32[]{:S(2)}) collective-permute-start(bf16[640,640]{1,0:T(8,128)(2,1)} %collective-permute-done.2.refs_3_), channel_id=1, source_target_pairs={{0,6},{1,7},{2,0},{3,1},{4,2},{5,3},{6,4},{7,5},{8,14},{9,15},{10,... | collective-permute-start | bytes 2457608 | tf_op jit(solution)/shard_map/ppermute | solution.py:199
  37.2 2.8 %collective-permute-start.9 = (bf16[64,5120]{1,0:T(8,128)(2,1)S(1)}, bf16[64,5120]{1,0:T(8,128)(2,1)S(1)}, u32[]{:S(2)}, u32[]{:S(2)}) collective-permute-start(bf16[64,5120]{1,0:T(8,128)(2,1)S(1)} %multiply_convert_fusion), channel_id=1, source_target_pairs={{0,64},{8,72},{16,80},{24,88},{32,96},{40,104},{48,112},{56,120},{... | collective-permute-start | bytes 1966088 | tf_op jit(solution)/shard_map/ppermute | solution.py:202
  40.0 3.0 %collective-permute-start.8 = (bf16[64,5120]{1,0:T(8,128)(2,1)S(1)}, bf16[64,5120]{1,0:T(8,128)(2,1)S(1)}, u32[]{:S(2)}, u32[]{:S(2)}) collective-permute-start(bf16[64,5120]{1,0:T(8,128)(2,1)S(1)} %multiply_convert_fusion), channel_id=1, source_target_pairs={{0,48},{8,56},{16,0},{24,8},{32,16},{40,24},{48,32},{56,40},{64,11... | collective-permute-start | bytes 1966088 | tf_op jit(solution)/shard_map/ppermute | solution.py:199
  43.0 1.1 slice.96
  44.1 5.3 %broadcast_in_dim.9 = bf16[2,4,2,2,32,5120]{5,4,3,2,1,0:T(8,128)(2,1)} broadcast(bf16[]{:T(256)} %constant.194.clone.1), dimensions={} | broadcast | bytes 10485762 | tf_op jit(solution)/shard_map/broadcast_in_dim | solution.py:335
  49.4 0.9 constant_dynamic-update-slice_fusion.11
  50.4 2.2 %collective-permute-done.9 = bf16[64,5120]{1,0:T(8,128)(2,1)S(1)} collective-permute-done((bf16[64,5120]{1,0:T(8,128)(2,1)S(1)}, bf16[64,5120]{1,0:T(8,128)(2,1)S(1)}, u32[]{:S(2)}, u32[]{:S(2)}) %collective-permute-start.9) | collective-permute-done | bytes 655392 | tf_op jit(solution)/shard_map/ppermute | solution.py:202
  52.6 3.0 %collective-permute-start.14 = (bf16[512,640]{1,0:T(8,128)(2,1)S(1)}, bf16[512,640]{1,0:T(8,128)(2,1)S(1)}, u32[]{:S(2)}, u32[]{:S(2)}) collective-permute-start(bf16[512,640]{1,0:T(8,128)(2,1)S(1)} %copy-done.5), channel_id=1, source_target_pairs={{0,64},{8,72},{16,80},{24,88},{32,96},{40,104},{48,112},{56,120},{... | collective-permute-start | bytes 1966088 | tf_op jit(solution)/shard_map/ppermute | solution.py:202
  55.6 1.8 collective-permute-done.7
  57.7 2.8 %collective-permute-start.11 = (bf16[640,640]{1,0:T(8,128)(2,1)S(1)}, bf16[640,640]{1,0:T(8,128)(2,1)S(1)}, u32[]{:S(2)}, u32[]{:S(2)}) collective-permute-start(bf16[640,640]{1,0:T(8,128)(2,1)S(1)} %pad_maximum_fusion.11), channel_id=1, source_target_pairs={{0,6},{1,7},{2,0},{3,1},{4,2},{5,3},{6,4},{7,5},{8,14},{9,15},{10,... | collective-permute-start | bytes 2457608 | tf_op jit(solution)/shard_map/ppermute | solution.py:199
  60.9 1.0 collective-permute-start.13
  61.9 1.1 collective-permute-start.12
  63.0 0.9 constant_dynamic-update-slice_fusion.10
  63.9 0.9 constant_dynamic-update-slice_fusion.9
  64.8 0.9 constant_dynamic-update-slice_fusion.8
  65.7 3.4 %put.5.refs_0_ = bf16[16,320,640]{2,1,0:T(8,128)(2,1)S(1)} custom-call(s32[12]{0:T(128)S(1)} %stack.236.places, bf16[640,640]{1,0:T(8,128)(2,1)S(1)} %copy-done.13, bf16[640,640]{1,0:T(8,128)(2,1)S(1)} %collective-permute-done.3.refs_1_, bf16[640,640]{1,0:T(8,128)(2,1)} %collective-permute-done.4.refs_2_, bf16[640,640]{1,0:T(8,128)(2,1)} %collective-permute-done.2.refs_3_, ...), custom_call_target="tpu_custom_call" | custom-call | bytes 320 | tf_op jit(solution)/shard_map/put/pallas_call | solution.py:236
  69.5 4.1 %collective-permute-done.11.refs_2_ = bf16[640,640]{1,0:T(8,128)(2,1)S(1)} collective-permute-done((bf16[640,640]{1,0:T(8,128)(2,1)S(1)}, bf16[640,640]{1,0:T(8,128)(2,1)S(1)}, u32[]{:S(2)}, u32[]{:S(2)}) %collective-permute-start.11) | collective-permute-done | bytes 819232 | tf_op jit(solution)/shard_map/ppermute | solution.py:199
  73.5 3.4 %collective-permute-done.10.refs_1_ = bf16[640,640]{1,0:T(8,128)(2,1)S(1)} collective-permute-done((bf16[640,640]{1,0:T(8,128)(2,1)S(1)}, bf16[640,640]{1,0:T(8,128)(2,1)S(1)}, u32[]{:S(2)}, u32[]{:S(2)}) %collective-permute-start.10) | collective-permute-done | bytes 819232 | tf_op jit(solution)/shard_map/ppermute | solution.py:196
  76.9 3.7 %collective-permute-done.13 = bf16[96,5120]{1,0:T(8,128)(2,1)S(1)} collective-permute-done((bf16[96,5120]{1,0:T(8,128)(2,1)S(1)}, bf16[96,5120]{1,0:T(8,128)(2,1)S(1)}, u32[]{:S(2)}, u32[]{:S(2)}) %collective-permute-start.13) | collective-permute-done | bytes 983072 | tf_op jit(solution)/shard_map/ppermute | solution.py:199
  80.7 2.7 %collective-permute-done.12 = bf16[96,5120]{1,0:T(8,128)(2,1)S(1)} collective-permute-done((bf16[96,5120]{1,0:T(8,128)(2,1)S(1)}, bf16[96,5120]{1,0:T(8,128)(2,1)S(1)}, u32[]{:S(2)}, u32[]{:S(2)}) %collective-permute-start.12) | collective-permute-done | bytes 983072 | tf_op jit(solution)/shard_map/ppermute | solution.py:196
  83.9 1.7 collective-permute-start.15
  86.6 0.8 put.6
  87.4 3.2 %collective-permute-done.16 = bf16[32,5120]{1,0:T(8,128)(2,1)S(1)} collective-permute-done((bf16[32,5120]{1,0:T(8,128)(2,1)S(1)}, bf16[32,5120]{1,0:T(8,128)(2,1)S(1)}, u32[]{:S(2)}, u32[]{:S(2)}) %collective-permute-start.16) | collective-permute-done | bytes 327712 | tf_op jit(solution)/shard_map/ppermute | solution.py:199
  90.6 1.5 collective-permute-done.15
  92.9 1.9 collective-permute-done.18
  95.3 8.3 %convolution_convert_fusion = bf16[1024,640]{1,0:T(8,128)(2,1)S(1)} fusion(bf16[1024,5120]{1,0:T(8,128)(2,1)S(1)} %bitcast.126, bf16[5120,640]{1,0:T(8,128)(2,1)S(1)} %bitcast.118), kind=kOutput, calls=%fused_computation.11 | convolution fusion | flops 6711541760 | bytes 18350080 | tf_op jit(solution)/shard_map/dot_general | solution.py:394
  103.6 25.2 %all_to_all.18.packed = bf16[16,64,640]{2,1,0:T(8,128)(2,1)S(1)} all-to-all(bf16[16,64,640]{2,1,0:T(8,128)(2,1)S(1)} %bitcast.147), channel_id=1, replica_groups=mesh['wide'=16,'narrow'=8] {'wide'}, dimensions={0} | all-to-all | bytes 2621440 | tf_op jit(solution)/shard_map/all_to_all | solution.py:395
  129.1 1.1 collective-permute-start.25
  130.1 1.0 collective-permute-start.23
  131.2 7.9 %attend.1 = bf16[64,8192]{1,0:T(8,128)(2,1)S(1)} custom-call(s32[4]{0:T(128)S(1)} %copy-done.14, s32[4]{0:T(128)S(1)} %copy-done.15, bf16[16,64,640]{2,1,0:T(8,128)(2,1)S(1)} %all_to_all.18.packed, f32[64,128]{1,0:T(8,128)S(1)} %broadcast_in_dim.8.inverse, f32[64,128]{1,0:T(8,128)S(1)} %get-tuple-element.82.cosine, f32[64,128]{1,0:T(8,128)S(1)} %get-tuple-element.83.sine, ...), custom_call_target="tpu_custom_call" | custom-call | flops 570425344 | bytes 6553600 | tf_op jit(solution)/shard_map/attend/pallas_call | solution.py:137
  139.2 2.5 %collective-permute-start.21 = (bf16[64,8192]{1,0:T(8,128)(2,1)S(1)}, bf16[64,8192]{1,0:T(8,128)(2,1)}, u32[]{:S(2)}, u32[]{:S(2)}) collective-permute-start(bf16[64,8192]{1,0:T(8,128)(2,1)S(1)} %attend.1), channel_id=1, source_target_pairs={{0,6},{1,7},{2,0},{3,1},{4,2},{5,3},{6,4},{7,5},{8,14},{9,15},{10,... | collective-permute-start | bytes 3145736 | tf_op jit(solution)/shard_map/ppermute | solution.py:199
  141.7 10.6 %collective-permute-done.25.refs_5_ = bf16[768,640]{1,0:T(8,128)(2,1)S(1)} collective-permute-done((bf16[768,640]{1,0:T(8,128)(2,1)S(1)}, bf16[768,640]{1,0:T(8,128)(2,1)S(1)}, u32[]{:S(2)}, u32[]{:S(2)}) %collective-permute-start.25) | collective-permute-done | bytes 983072 | tf_op jit(solution)/shard_map/ppermute | solution.py:199
  152.4 3.0 %collective-permute-start.26 = (bf16[256,640]{1,0:T(8,128)(2,1)S(1)}, bf16[256,640]{1,0:T(8,128)(2,1)S(1)}, u32[]{:S(2)}, u32[]{:S(2)}) collective-permute-start(bf16[256,640]{1,0:T(8,128)(2,1)S(1)} %slice.127), channel_id=1, source_target_pairs={{0,48},{8,56},{16,0},{24,8},{32,16},{40,24},{48,32},{56,40},{64,11... | collective-permute-start | bytes 983048 | tf_op jit(solution)/shard_map/ppermute | solution.py:199
  155.5 3.7 %pack.1 = bf16[3584,640]{1,0:T(8,128)(2,1)} custom-call(bf16[512,640]{1,0:T(8,128)(2,1)S(1)} %copy-done.5, bf16[512,640]{1,0:T(8,128)(2,1)S(1)} %copy-done.3, bf16[512,640]{1,0:T(8,128)(2,1)S(1)} %collective-permute-done.1.refs_2_, bf16[512,640]{1,0:T(8,128)(2,1)S(1)} %collective-permute-done.14.refs_3_, ...), custom_call_target="tpu_custom_call" | custom-call | bytes 3584 | tf_op jit(solution)/shard_map/pack/pallas_call | solution.py:287
  159.2 2.9 %collective-permute-done.26.refs_7_ = bf16[256,640]{1,0:T(8,128)(2,1)S(1)} collective-permute-done((bf16[256,640]{1,0:T(8,128)(2,1)S(1)}, bf16[256,640]{1,0:T(8,128)(2,1)S(1)}, u32[]{:S(2)}, u32[]{:S(2)}) %collective-permute-start.26) | collective-permute-done | bytes 327712 | tf_op jit(solution)/shard_map/ppermute | solution.py:199
  162.1 3.5 %collective-permute-done.24.refs_6_ = bf16[256,640]{1,0:T(8,128)(2,1)S(1)} collective-permute-done((bf16[256,640]{1,0:T(8,128)(2,1)S(1)}, bf16[256,640]{1,0:T(8,128)(2,1)S(1)}, u32[]{:S(2)}, u32[]{:S(2)}) %collective-permute-start.24) | collective-permute-done | bytes 327712 | tf_op jit(solution)/shard_map/ppermute | solution.py:196
  165.6 0.9 pad_maximum_fusion.13
  167.3 1.2 slice.114
  168.5 1.1 slice.115
  169.6 0.5 collective-permute-start.31
  170.1 1.3 fusion.27
  171.8 1.1 collective-permute-start.29
  172.8 3.2 %collective-permute-start.28 = (bf16[64,8192]{1,0:T(8,128)(2,1)S(1)}, bf16[64,8192]{1,0:T(8,128)(2,1)S(1)}, u32[]{:S(2)}, u32[]{:S(2)}) collective-permute-start(bf16[64,8192]{1,0:T(8,128)(2,1)S(1)} %get-tuple-element.128), channel_id=1, source_target_pairs={{0,6},{1,7},{2,0},{3,1},{4,2},{5,3},{6,4},{7,5},{8,14},{9,15},{10,... | collective-permute-start | bytes 3145736 | tf_op jit(solution)/shard_map/ppermute | solution.py:199
  176.1 2.0 pad_maximum_fusion
  178.2 2.3 %put.7.refs_0_ = bf16[32,256,640]{2,1,0:T(8,128)(2,1)S(1)} custom-call(s32[16]{0:T(128)S(1)} %stack.284.places, bf16[512,640]{1,0:T(8,128)(2,1)S(1)} %copy-done.6, bf16[512,640]{1,0:T(8,128)(2,1)S(1)} %copy-done.4, bf16[512,640]{1,0:T(8,128)(2,1)S(1)} %collective-permute-done.1.refs_2_, bf16[512,640]{1,0:T(8,128)(2,1)S(1)} %collective-permute-done.14.refs_3_, ...), custom_call_target="tpu_custom_call" | custom-call | bytes 256 | tf_op jit(solution)/shard_map/put/pallas_call | solution.py:236
  180.5 4.6 %put.8 = bf16[32,256,640]{2,1,0:T(8,128)(2,1)S(1)} custom-call(s32[16]{0:T(128)S(1)} %stack.267.places, bf16[32,256,640]{2,1,0:T(8,128)(2,1)S(1)} %put.7.refs_0_, bf16[3584,640]{1,0:T(8,128)(2,1)} %collective-permute-done.30.refs_1_, bf16[512,640]{1,0:T(8,128)(2,1)S(1)} %bitcast.121), custom_call_target="tpu_custom_call", output_to_operand_aliasing={{}: (1, {})} | custom-call | bytes 256 | tf_op jit(solution)/shard_map/put/pallas_call | solution.py:236
  185.1 3.4 %convolution_convert_fusion.1.refs_0_ = bf16[256,640]{1,0:T(8,128)(2,1)S(1)} fusion(bf16[256,8192]{1,0:T(8,128)(2,1)S(1)} %pad_maximum_fusion, bf16[8192,640]{1,0:T(8,128)(2,1)S(1)} %bitcast.115), kind=kOutput, calls=%fused_computation.14 | convolution fusion | flops 2684518400 | bytes 15007744 | tf_op jit(solution)/shard_map/dot_general | solution.py:475
  188.6 8.4 %collective-permute-done.29 = bf16[64,8192]{1,0:T(8,128)(2,1)S(1)} collective-permute-done((bf16[64,8192]{1,0:T(8,128)(2,1)S(1)}, bf16[64,8192]{1,0:T(8,128)(2,1)S(1)}, u32[]{:S(2)}, u32[]{:S(2)}) %collective-permute-start.29) | collective-permute-done | bytes 1048608 | tf_op jit(solution)/shard_map/ppermute | solution.py:202
  197.0 1.9 collective-permute-done.27
  199.0 1.1 collective-permute-start.35
  200.1 1.0 collective-permute-start.34
  201.1 3.2 %collective-permute-start.33 = (bf16[16,8192]{1,0:T(8,128)(2,1)S(1)}, bf16[16,8192]{1,0:T(8,128)(2,1)S(1)}, u32[]{:S(2)}, u32[]{:S(2)}) collective-permute-start(bf16[16,8192]{1,0:T(8,128)(2,1)S(1)} %slice.119), channel_id=1, source_target_pairs={{0,6},{1,7},{2,0},{3,1},{4,2},{5,3},{6,4},{7,5},{8,14},{9,15},{10,... | collective-permute-start | bytes 786440 | tf_op jit(solution)/shard_map/ppermute | solution.py:199
  204.3 2.6 %fusion.7.refs_1_ = bf16[192,640]{1,0:T(8,128)(2,1)S(1)} fusion(bf16[8192,640]{1,0:T(8,128)(2,1)S(1)} %bitcast.116, bf16[64,8192]{1,0:T(8,128)(2,1)S(1)} %collective-permute-done.28, bf16[64,8192]{1,0:T(8,128)(2,1)S(1)} %collective-permute-done.27, bf16[64,8192]{1,0:T(8,128)(2,1)S(1)} %collective-permute-done.29), kind=kOutput, calls=%fused_computation.15 | convolution fusion | flops 2022825984 | bytes 13877248 | tf_op jit(solution)/shard_map/dot_general | solution.py:475
  206.9 1.4 order.1
  208.4 3.4 %collective-permute-done.34 = bf16[16,8192]{1,0:T(8,128)(2,1)S(1)} collective-permute-done((bf16[16,8192]{1,0:T(8,128)(2,1)S(1)}, bf16[16,8192]{1,0:T(8,128)(2,1)S(1)}, u32[]{:S(2)}, u32[]{:S(2)}) %collective-permute-start.34) | collective-permute-done | bytes 262176 | tf_op jit(solution)/shard_map/ppermute | solution.py:202
  211.8 1.8 convolution_convert_fusion.2.refs_1_
  213.6 0.6 put.9
  (136 shorter events, 6.2 us)
Async XLA Ops:
  0.0 33.9 %copy-start.18 = (f32[5120]{0:T(1024)S(1)}, f32[5120]{0:T(1024)}, u32[]{:S(2)}) copy-start(f32[5120]{0:T(1024)} %param.11) | copy-start | bytes 61444
  0.0 34.0 %collective-permute-start.1 = (bf16[512,640]{1,0:T(8,128)(2,1)}, bf16[512,640]{1,0:T(8,128)(2,1)S(1)}, u32[]{:S(2)}, u32[]{:S(2)}) collective-permute-start(bf16[512,640]{1,0:T(8,128)(2,1)} %refs_0_.3), channel_id=1, source_target_pairs={{0,48},{8,56},{16,0},{24,8},{32,16},{40,24},{48,32},{56,40},{64,11... | collective-permute-start | bytes 1966088 | tf_op jit(solution)/shard_map/ppermute | solution.py:199
  3.1 30.9 %collective-permute-start = (bf16[512,640]{1,0:T(8,128)(2,1)}, bf16[512,640]{1,0:T(8,128)(2,1)S(1)}, u32[]{:S(2)}, u32[]{:S(2)}) collective-permute-start(bf16[512,640]{1,0:T(8,128)(2,1)} %refs_0_.3), channel_id=1, source_target_pairs={{0,16},{8,24},{16,32},{24,40},{32,48},{40,56},{48,0},{56,8},{64,80... | collective-permute-start | bytes 1966088 | tf_op jit(solution)/shard_map/ppermute | solution.py:196
  3.1 30.9 %collective-permute-start.3 = (bf16[640,640]{1,0:T(8,128)(2,1)}, bf16[640,640]{1,0:T(8,128)(2,1)S(1)}, u32[]{:S(2)}, u32[]{:S(2)}) collective-permute-start(bf16[640,640]{1,0:T(8,128)(2,1)} %refs_0_.1), channel_id=1, source_target_pairs={{0,2},{1,3},{2,4},{3,5},{4,6},{5,7},{6,0},{7,1},{8,10},{9,11},{10,... | collective-permute-start | bytes 2457608 | tf_op jit(solution)/shard_map/ppermute | solution.py:196
  5.0 29.0 %collective-permute-start.2 = (bf16[640,640]{1,0:T(8,128)(2,1)}, bf16[640,640]{1,0:T(8,128)(2,1)}, u32[]{:S(2)}, u32[]{:S(2)}) collective-permute-start(bf16[640,640]{1,0:T(8,128)(2,1)} %refs_0_.1), channel_id=1, source_target_pairs={{0,1},{1,0},{2,3},{3,2},{4,5},{5,4},{6,7},{7,6},{8,9},{9,8},{10,11... | collective-permute-start | bytes 2457608 | tf_op jit(solution)/shard_map/ppermute | solution.py:202
  6.5 27.5 %collective-permute-start.4 = (bf16[640,640]{1,0:T(8,128)(2,1)}, bf16[640,640]{1,0:T(8,128)(2,1)}, u32[]{:S(2)}, u32[]{:S(2)}) collective-permute-start(bf16[640,640]{1,0:T(8,128)(2,1)} %refs_0_.1), channel_id=1, source_target_pairs={{0,6},{1,7},{2,0},{3,1},{4,2},{5,3},{6,4},{7,5},{8,14},{9,15},{10,... | collective-permute-start | bytes 2457608 | tf_op jit(solution)/shard_map/ppermute | solution.py:199
  8.6 25.0 %all-to-all-start = ((bf16[8,64,640]{2,1,0:T(8,128)(2,1)}), bf16[8,64,640]{2,1,0:T(8,128)(2,1)S(1)}, u32[]{:S(2)}, u32[]{:S(2)}) async-start(bf16[8,64,640]{2,1,0:T(8,128)(2,1)} %bitcast.150), calls=%async_computation | async-start | bytes 1310720 | tf_op jit(solution)/shard_map/all_to_all | solution.py:320
  34.0 94.8 %copy-start.2 = (bf16[512,640]{1,0:T(8,128)(2,1)}, bf16[512,640]{1,0:T(8,128)(2,1)S(1)}, u32[]{:S(2)}) copy-start(bf16[512,640]{1,0:T(8,128)(2,1)S(1)} %collective-permute-done.refs_1_) | copy-start | bytes 1966084
  34.0 23.3 %collective-permute-start.6 = (bf16[640,640]{1,0:T(8,128)(2,1)}, bf16[640,640]{1,0:T(8,128)(2,1)S(1)}, u32[]{:S(2)}, u32[]{:S(2)}) collective-permute-start(bf16[640,640]{1,0:T(8,128)(2,1)} %collective-permute-done.2.refs_3_), channel_id=1, source_target_pairs={{0,6},{1,7},{2,0},{3,1},{4,2},{5,3},{6,4},{7,5},{8,14},{9,15},{10,... | collective-permute-start | bytes 2457608 | tf_op jit(solution)/shard_map/ppermute | solution.py:199
  36.9 20.4 %collective-permute-start.5 = (bf16[640,640]{1,0:T(8,128)(2,1)}, bf16[640,640]{1,0:T(8,128)(2,1)S(1)}, u32[]{:S(2)}, u32[]{:S(2)}) collective-permute-start(bf16[640,640]{1,0:T(8,128)(2,1)} %collective-permute-done.2.refs_3_), channel_id=1, source_target_pairs={{0,2},{1,3},{2,4},{3,5},{4,6},{5,7},{6,0},{7,1},{8,10},{9,11},{10,... | collective-permute-start | bytes 2457608 | tf_op jit(solution)/shard_map/ppermute | solution.py:196
  37.2 15.4 %collective-permute-start.9 = (bf16[64,5120]{1,0:T(8,128)(2,1)S(1)}, bf16[64,5120]{1,0:T(8,128)(2,1)S(1)}, u32[]{:S(2)}, u32[]{:S(2)}) collective-permute-start(bf16[64,5120]{1,0:T(8,128)(2,1)S(1)} %multiply_convert_fusion), channel_id=1, source_target_pairs={{0,64},{8,72},{16,80},{24,88},{32,96},{40,104},{48,112},{56,120},{... | collective-permute-start | bytes 1966088 | tf_op jit(solution)/shard_map/ppermute | solution.py:202
  40.0 15.6 %collective-permute-start.8 = (bf16[64,5120]{1,0:T(8,128)(2,1)S(1)}, bf16[64,5120]{1,0:T(8,128)(2,1)S(1)}, u32[]{:S(2)}, u32[]{:S(2)}) collective-permute-start(bf16[64,5120]{1,0:T(8,128)(2,1)S(1)} %multiply_convert_fusion), channel_id=1, source_target_pairs={{0,48},{8,56},{16,0},{24,8},{32,16},{40,24},{48,32},{56,40},{64,11... | collective-permute-start | bytes 1966088 | tf_op jit(solution)/shard_map/ppermute | solution.py:199
  42.9 14.4 %collective-permute-start.7 = (bf16[64,5120]{1,0:T(8,128)(2,1)S(1)}, bf16[64,5120]{1,0:T(8,128)(2,1)S(1)}, u32[]{:S(2)}, u32[]{:S(2)}) collective-permute-start(bf16[64,5120]{1,0:T(8,128)(2,1)S(1)} %multiply_convert_fusion), channel_id=1, source_target_pairs={{0,16},{8,24},{16,32},{24,40},{32,48},{40,56},{48,0},{56,8},{64,80... | collective-permute-start | bytes 1966088 | tf_op jit(solution)/shard_map/ppermute | solution.py:196
  42.9 9.6 %copy-start.5 = (bf16[512,640]{1,0:T(8,128)(2,1)S(1)}, bf16[512,640]{1,0:T(8,128)(2,1)}, u32[]{:S(2)}) copy-start(bf16[512,640]{1,0:T(8,128)(2,1)} %refs_0_.3) | copy-start | bytes 1966084
  52.6 16.9 %collective-permute-start.14 = (bf16[512,640]{1,0:T(8,128)(2,1)S(1)}, bf16[512,640]{1,0:T(8,128)(2,1)S(1)}, u32[]{:S(2)}, u32[]{:S(2)}) collective-permute-start(bf16[512,640]{1,0:T(8,128)(2,1)S(1)} %copy-done.5), channel_id=1, source_target_pairs={{0,64},{8,72},{16,80},{24,88},{32,96},{40,104},{48,112},{56,120},{... | collective-permute-start | bytes 1966088 | tf_op jit(solution)/shard_map/ppermute | solution.py:202
  57.5 8.2 %copy-start.13 = (bf16[640,640]{1,0:T(8,128)(2,1)S(1)}, bf16[640,640]{1,0:T(8,128)(2,1)}, u32[]{:S(2)}) copy-start(bf16[640,640]{1,0:T(8,128)(2,1)} %refs_0_.1) | copy-start | bytes 2457604
  57.7 15.9 %collective-permute-start.11 = (bf16[640,640]{1,0:T(8,128)(2,1)S(1)}, bf16[640,640]{1,0:T(8,128)(2,1)S(1)}, u32[]{:S(2)}, u32[]{:S(2)}) collective-permute-start(bf16[640,640]{1,0:T(8,128)(2,1)S(1)} %pad_maximum_fusion.11), channel_id=1, source_target_pairs={{0,6},{1,7},{2,0},{3,1},{4,2},{5,3},{6,4},{7,5},{8,14},{9,15},{10,... | collective-permute-start | bytes 2457608 | tf_op jit(solution)/shard_map/ppermute | solution.py:199
  60.6 16.3 %collective-permute-start.10 = (bf16[640,640]{1,0:T(8,128)(2,1)S(1)}, bf16[640,640]{1,0:T(8,128)(2,1)S(1)}, u32[]{:S(2)}, u32[]{:S(2)}) collective-permute-start(bf16[640,640]{1,0:T(8,128)(2,1)S(1)} %pad_maximum_fusion.10), channel_id=1, source_target_pairs={{0,2},{1,3},{2,4},{3,5},{4,6},{5,7},{6,0},{7,1},{8,10},{9,11},{10,... | collective-permute-start | bytes 2457608 | tf_op jit(solution)/shard_map/ppermute | solution.py:196
  60.9 19.8 %collective-permute-start.13 = (bf16[96,5120]{1,0:T(8,128)(2,1)S(1)}, bf16[96,5120]{1,0:T(8,128)(2,1)S(1)}, u32[]{:S(2)}, u32[]{:S(2)}) collective-permute-start(bf16[96,5120]{1,0:T(8,128)(2,1)S(1)} %get-tuple-element.124), channel_id=1, source_target_pairs={{0,48},{8,56},{16,0},{24,8},{32,16},{40,24},{48,32},{56,40},{64,11... | collective-permute-start | bytes 2949128 | tf_op jit(solution)/shard_map/ppermute | solution.py:199
  61.9 21.4 %collective-permute-start.12 = (bf16[96,5120]{1,0:T(8,128)(2,1)S(1)}, bf16[96,5120]{1,0:T(8,128)(2,1)S(1)}, u32[]{:S(2)}, u32[]{:S(2)}) collective-permute-start(bf16[96,5120]{1,0:T(8,128)(2,1)S(1)} %get-tuple-element.125), channel_id=1, source_target_pairs={{0,16},{8,24},{16,32},{24,40},{32,48},{40,56},{48,0},{56,8},{64,80... | collective-permute-start | bytes 2949128 | tf_op jit(solution)/shard_map/ppermute | solution.py:196
  65.7 19.9 %slice-start = ((s8[10485760]{0:T(1024)(128)(4,1)}), s8[4194304]{0:T(1024)(128)(4,1)S(1)}, s32[]{:S(2)}) async-start(s8[10485760]{0:T(1024)(128)(4,1)} %bitcast.124), calls=%async_computation.2 | async-start | bytes 8388608
  65.7 19.9 %slice-start.1 = ((s8[10485760]{0:T(1024)(128)(4,1)}), s8[4194304]{0:T(1024)(128)(4,1)S(1)}, s32[]{:S(2)}) async-start(s8[10485760]{0:T(1024)(128)(4,1)} %bitcast.124), calls=%async_computation.3 | async-start | bytes 8388608
  69.1 16.5 %slice-start.2 = ((s8[10485760]{0:T(1024)(128)(4,1)}), s8[2097152]{0:T(1024)(128)(4,1)S(1)}, s32[]{:S(2)}) async-start(s8[10485760]{0:T(1024)(128)(4,1)} %bitcast.124), calls=%async_computation.4 | async-start | bytes 4194304
  83.5 7.1 %collective-permute-start.16 = (bf16[32,5120]{1,0:T(8,128)(2,1)S(1)}, bf16[32,5120]{1,0:T(8,128)(2,1)S(1)}, u32[]{:S(2)}, u32[]{:S(2)}) collective-permute-start(bf16[32,5120]{1,0:T(8,128)(2,1)S(1)} %slice.105), channel_id=1, source_target_pairs={{0,48},{8,56},{16,0},{24,8},{32,16},{40,24},{48,32},{56,40},{64,11... | collective-permute-start | bytes 983048 | tf_op jit(solution)/shard_map/ppermute | solution.py:199
  83.9 8.3 %collective-permute-start.15 = (bf16[32,5120]{1,0:T(8,128)(2,1)S(1)}, bf16[32,5120]{1,0:T(8,128)(2,1)S(1)}, u32[]{:S(2)}, u32[]{:S(2)}) collective-permute-start(bf16[32,5120]{1,0:T(8,128)(2,1)S(1)} %slice.104), channel_id=1, source_target_pairs={{0,16},{8,24},{16,32},{24,40},{32,48},{40,56},{48,0},{56,8},{64,80... | collective-permute-start | bytes 983048 | tf_op jit(solution)/shard_map/ppermute | solution.py:196
  86.0 6.6 %collective-permute-start.17 = (bf16[2,96,5120]{2,1,0:T(8,128)(2,1)S(1)}, bf16[2,96,5120]{2,1,0:T(8,128)(2,1)S(1)}, u32[]{:S(2)}, u32[]{:S(2)}) collective-permute-start(bf16[2,96,5120]{2,1,0:T(8,128)(2,1)S(1)} %pad_maximum_fusion.2), channel_id=1, source_target_pairs={{0,8},{8,0},{16,24},{24,16},{32,40},{40,32},{48,56},{56,48},{64,72... | collective-permute-start | bytes 5898248 | tf_op jit(solution)/shard_map/ppermute | solution.py:205
  86.1 8.7 %collective-permute-start.19 = (bf16[4,64,5120]{2,1,0:T(8,128)(2,1)S(1)}, bf16[4,64,5120]{2,1,0:T(8,128)(2,1)S(1)}, u32[]{:S(2)}, u32[]{:S(2)}) collective-permute-start(bf16[4,64,5120]{2,1,0:T(8,128)(2,1)S(1)} %pad_maximum_fusion.1), channel_id=1, source_target_pairs={{0,8},{8,0},{16,24},{24,16},{32,40},{40,32},{48,56},{56,48},{64,72... | collective-permute-start | bytes 7864328 | tf_op jit(solution)/shard_map/ppermute | solution.py:205
  92.2 2.5 %collective-permute-start.18 = (bf16[2,32,5120]{2,1,0:T(8,128)(2,1)S(1)}, bf16[2,32,5120]{2,1,0:T(8,128)(2,1)S(1)}, u32[]{:S(2)}, u32[]{:S(2)}) collective-permute-start(bf16[2,32,5120]{2,1,0:T(8,128)(2,1)S(1)} %pad_maximum_fusion.12), channel_id=1, source_target_pairs={{0,8},{8,0},{16,24},{24,16},{32,40},{40,32},{48,56},{56,48},{64,72... | collective-permute-start | bytes 1966088 | tf_op jit(solution)/shard_map/ppermute | solution.py:205
  103.5 27.6 %copy-start.7 = (bf16[4,256,1024]{2,1,0:T(8,128)(2,1)S(1)}, bf16[4,256,1024]{2,1,0:T(8,128)(2,1)}, u32[]{:S(2)}) copy-start(bf16[4,256,1024]{2,1,0:T(8,128)(2,1)} %keys.1) | copy-start | bytes 6291460
  103.5 27.6 %copy-start.8 = (bf16[4,256,1024]{2,1,0:T(8,128)(2,1)S(1)}, bf16[4,256,1024]{2,1,0:T(8,128)(2,1)}, u32[]{:S(2)}) copy-start(bf16[4,256,1024]{2,1,0:T(8,128)(2,1)} %values.1) | copy-start | bytes 6291460
  103.5 27.6 %copy-start.14 = (s32[4]{0:T(128)S(1)}, s32[4]{0:T(128)}, u32[]{:S(2)}) copy-start(s32[4]{0:T(128)} %fills.1) | copy-start | bytes 52
  103.6 27.6 %copy-start.15 = (s32[4]{0:T(128)S(1)}, s32[4]{0:T(128)}, u32[]{:S(2)}) copy-start(s32[4]{0:T(128)} %spans.1) | copy-start | bytes 52
  103.6 27.6 %copy-start.16 = (f32[128]{0:T(128)S(1)}, f32[128]{0:T(128)}, u32[]{:S(2)}) copy-start(f32[128]{0:T(128)} %param.13) | copy-start | bytes 1540
  103.6 27.6 %copy-start.17 = (f32[128]{0:T(128)S(1)}, f32[128]{0:T(128)}, u32[]{:S(2)}) copy-start(f32[128]{0:T(128)} %param.14) | copy-start | bytes 1540
  128.9 26.7 %copy-start.3 = (bf16[512,640]{1,0:T(8,128)(2,1)S(1)}, bf16[512,640]{1,0:T(8,128)(2,1)}, u32[]{:S(2)}) copy-start(bf16[512,640]{1,0:T(8,128)(2,1)} %copy-done.2) | copy-start | bytes 1966084
  129.1 23.3 %collective-permute-start.25 = (bf16[768,640]{1,0:T(8,128)(2,1)S(1)}, bf16[768,640]{1,0:T(8,128)(2,1)S(1)}, u32[]{:S(2)}, u32[]{:S(2)}) collective-permute-start(bf16[768,640]{1,0:T(8,128)(2,1)S(1)} %get-tuple-element.122), channel_id=1, source_target_pairs={{0,48},{8,56},{16,0},{24,8},{32,16},{40,24},{48,32},{56,40},{64,11... | collective-permute-start | bytes 2949128 | tf_op jit(solution)/shard_map/ppermute | solution.py:199
  130.1 25.3 %collective-permute-start.23 = (bf16[768,640]{1,0:T(8,128)(2,1)S(1)}, bf16[768,640]{1,0:T(8,128)(2,1)S(1)}, u32[]{:S(2)}, u32[]{:S(2)}) collective-permute-start(bf16[768,640]{1,0:T(8,128)(2,1)S(1)} %get-tuple-element.123), channel_id=1, source_target_pairs={{0,16},{8,24},{16,32},{24,40},{32,48},{40,56},{48,0},{56,8},{64,80... | collective-permute-start | bytes 2949128 | tf_op jit(solution)/shard_map/ppermute | solution.py:196
  139.1 16.3 %copy-start = (bf16[64,8192]{1,0:T(8,128)(2,1)}, bf16[64,8192]{1,0:T(8,128)(2,1)S(1)}, u32[]{:S(2)}) copy-start(bf16[64,8192]{1,0:T(8,128)(2,1)S(1)} %attend.1) | copy-start | bytes 3145732
  139.1 27.5 %collective-permute-start.22 = (bf16[64,8192]{1,0:T(8,128)(2,1)S(1)}, bf16[64,8192]{1,0:T(8,128)(2,1)}, u32[]{:S(2)}, u32[]{:S(2)}) collective-permute-start(bf16[64,8192]{1,0:T(8,128)(2,1)S(1)} %attend.1), channel_id=1, source_target_pairs={{0,1},{1,0},{2,3},{3,2},{4,5},{5,4},{6,7},{7,6},{8,9},{9,8},{10,11... | collective-permute-start | bytes 3145736 | tf_op jit(solution)/shard_map/ppermute | solution.py:202
  139.2 27.4 %collective-permute-start.21 = (bf16[64,8192]{1,0:T(8,128)(2,1)S(1)}, bf16[64,8192]{1,0:T(8,128)(2,1)}, u32[]{:S(2)}, u32[]{:S(2)}) collective-permute-start(bf16[64,8192]{1,0:T(8,128)(2,1)S(1)} %attend.1), channel_id=1, source_target_pairs={{0,6},{1,7},{2,0},{3,1},{4,2},{5,3},{6,4},{7,5},{8,14},{9,15},{10,... | collective-permute-start | bytes 3145736 | tf_op jit(solution)/shard_map/ppermute | solution.py:199
  141.7 24.9 %collective-permute-start.20 = (bf16[64,8192]{1,0:T(8,128)(2,1)S(1)}, bf16[64,8192]{1,0:T(8,128)(2,1)}, u32[]{:S(2)}, u32[]{:S(2)}) collective-permute-start(bf16[64,8192]{1,0:T(8,128)(2,1)S(1)} %attend.1), channel_id=1, source_target_pairs={{0,2},{1,3},{2,4},{3,5},{4,6},{5,7},{6,0},{7,1},{8,10},{9,11},{10,... | collective-permute-start | bytes 3145736 | tf_op jit(solution)/shard_map/ppermute | solution.py:196
  152.4 9.8 %collective-permute-start.26 = (bf16[256,640]{1,0:T(8,128)(2,1)S(1)}, bf16[256,640]{1,0:T(8,128)(2,1)S(1)}, u32[]{:S(2)}, u32[]{:S(2)}) collective-permute-start(bf16[256,640]{1,0:T(8,128)(2,1)S(1)} %slice.127), channel_id=1, source_target_pairs={{0,48},{8,56},{16,0},{24,8},{32,16},{40,24},{48,32},{56,40},{64,11... | collective-permute-start | bytes 983048 | tf_op jit(solution)/shard_map/ppermute | solution.py:199
  155.4 10.2 %collective-permute-start.24 = (bf16[256,640]{1,0:T(8,128)(2,1)S(1)}, bf16[256,640]{1,0:T(8,128)(2,1)S(1)}, u32[]{:S(2)}, u32[]{:S(2)}) collective-permute-start(bf16[256,640]{1,0:T(8,128)(2,1)S(1)} %slice.126), channel_id=1, source_target_pairs={{0,16},{8,24},{16,32},{24,40},{32,48},{40,56},{48,0},{56,8},{64,80... | collective-permute-start | bytes 983048 | tf_op jit(solution)/shard_map/ppermute | solution.py:196
  162.1 4.5 %copy-start.9 = (bf16[256,640]{1,0:T(8,128)(2,1)}, bf16[256,640]{1,0:T(8,128)(2,1)S(1)}, u32[]{:S(2)}) copy-start(bf16[256,640]{1,0:T(8,128)(2,1)S(1)} %collective-permute-done.26.refs_7_) | copy-start | bytes 983044
  165.6 1.0 copy-start.11
  166.6 13.9 %collective-permute-start.30 = (bf16[3584,640]{1,0:T(8,128)(2,1)}, bf16[3584,640]{1,0:T(8,128)(2,1)}, u32[]{:S(2)}, u32[]{:S(2)}) collective-permute-start(bf16[3584,640]{1,0:T(8,128)(2,1)} %pack.1), channel_id=1, source_target_pairs={{0,8},{8,0},{16,24},{24,16},{32,40},{40,32},{48,56},{56,48},{64,72... | collective-permute-start | bytes 13762568 | tf_op jit(solution)/shard_map/ppermute | solution.py:205
  167.3 8.8 %copy-start.1 = (bf16[64,8192]{1,0:T(8,128)(2,1)S(1)}, bf16[64,8192]{1,0:T(8,128)(2,1)}, u32[]{:S(2)}) copy-start(bf16[64,8192]{1,0:T(8,128)(2,1)} %copy-done) | copy-start | bytes 3145732
  169.6 10.9 %collective-permute-start.31 = (bf16[2,256,640]{2,1,0:T(8,128)(2,1)}, bf16[2,256,640]{2,1,0:T(8,128)(2,1)S(1)}, u32[]{:S(2)}, u32[]{:S(2)}) collective-permute-start(bf16[2,256,640]{2,1,0:T(8,128)(2,1)} %pad_maximum_fusion.13), channel_id=1, source_target_pairs={{0,8},{8,0},{16,24},{24,16},{32,40},{40,32},{48,56},{56,48},{64,72... | collective-permute-start | bytes 1966088 | tf_op jit(solution)/shard_map/ppermute | solution.py:205
  171.4 6.7 %copy-start.4 = (bf16[512,640]{1,0:T(8,128)(2,1)S(1)}, bf16[512,640]{1,0:T(8,128)(2,1)}, u32[]{:S(2)}) copy-start(bf16[512,640]{1,0:T(8,128)(2,1)} %copy-done.2) | copy-start | bytes 1966084
  171.4 6.7 %copy-start.6 = (bf16[512,640]{1,0:T(8,128)(2,1)S(1)}, bf16[512,640]{1,0:T(8,128)(2,1)}, u32[]{:S(2)}) copy-start(bf16[512,640]{1,0:T(8,128)(2,1)} %refs_0_.3) | copy-start | bytes 1966084
  171.4 6.7 %copy-start.10 = (bf16[256,640]{1,0:T(8,128)(2,1)S(1)}, bf16[256,640]{1,0:T(8,128)(2,1)}, u32[]{:S(2)}) copy-start(bf16[256,640]{1,0:T(8,128)(2,1)} %copy-done.9) | copy-start | bytes 983044
  171.4 6.7 %copy-start.12 = (bf16[256,640]{1,0:T(8,128)(2,1)S(1)}, bf16[256,640]{1,0:T(8,128)(2,1)}, u32[]{:S(2)}) copy-start(bf16[256,640]{1,0:T(8,128)(2,1)} %copy-done.11) | copy-start | bytes 983044
  171.8 25.2 %collective-permute-start.29 = (bf16[64,8192]{1,0:T(8,128)(2,1)S(1)}, bf16[64,8192]{1,0:T(8,128)(2,1)S(1)}, u32[]{:S(2)}, u32[]{:S(2)}) collective-permute-start(bf16[64,8192]{1,0:T(8,128)(2,1)S(1)} %get-tuple-element.126), channel_id=1, source_target_pairs={{0,1},{1,0},{2,3},{3,2},{4,5},{5,4},{6,7},{7,6},{8,9},{9,8},{10,11... | collective-permute-start | bytes 3145736 | tf_op jit(solution)/shard_map/ppermute | solution.py:202
  172.8 26.0 %collective-permute-start.27 = (bf16[64,8192]{1,0:T(8,128)(2,1)S(1)}, bf16[64,8192]{1,0:T(8,128)(2,1)S(1)}, u32[]{:S(2)}, u32[]{:S(2)}) collective-permute-start(bf16[64,8192]{1,0:T(8,128)(2,1)S(1)} %get-tuple-element.127), channel_id=1, source_target_pairs={{0,2},{1,3},{2,4},{3,5},{4,6},{5,7},{6,0},{7,1},{8,10},{9,11},{10,... | collective-permute-start | bytes 3145736 | tf_op jit(solution)/shard_map/ppermute | solution.py:196
  172.8 26.0 %collective-permute-start.28 = (bf16[64,8192]{1,0:T(8,128)(2,1)S(1)}, bf16[64,8192]{1,0:T(8,128)(2,1)S(1)}, u32[]{:S(2)}, u32[]{:S(2)}) collective-permute-start(bf16[64,8192]{1,0:T(8,128)(2,1)S(1)} %get-tuple-element.128), channel_id=1, source_target_pairs={{0,6},{1,7},{2,0},{3,1},{4,2},{5,3},{6,4},{7,5},{8,14},{9,15},{10,... | collective-permute-start | bytes 3145736 | tf_op jit(solution)/shard_map/ppermute | solution.py:199
  199.0 9.4 %collective-permute-start.35 = (bf16[16,8192]{1,0:T(8,128)(2,1)S(1)}, bf16[16,8192]{1,0:T(8,128)(2,1)S(1)}, u32[]{:S(2)}, u32[]{:S(2)}) collective-permute-start(bf16[16,8192]{1,0:T(8,128)(2,1)S(1)} %get-tuple-element.117), channel_id=1, source_target_pairs={{0,1},{1,0},{2,3},{3,2},{4,5},{5,4},{6,7},{7,6},{8,9},{9,8},{10,11... | collective-permute-start | bytes 786440 | tf_op jit(solution)/shard_map/ppermute | solution.py:202
  200.1 11.7 %collective-permute-start.34 = (bf16[16,8192]{1,0:T(8,128)(2,1)S(1)}, bf16[16,8192]{1,0:T(8,128)(2,1)S(1)}, u32[]{:S(2)}, u32[]{:S(2)}) collective-permute-start(bf16[16,8192]{1,0:T(8,128)(2,1)S(1)} %get-tuple-element.118), channel_id=1, source_target_pairs={{0,1},{1,0},{2,3},{3,2},{4,5},{5,4},{6,7},{7,6},{8,9},{9,8},{10,11... | collective-permute-start | bytes 786440 | tf_op jit(solution)/shard_map/ppermute | solution.py:202
  201.1 10.7 %collective-permute-start.32 = (bf16[16,8192]{1,0:T(8,128)(2,1)S(1)}, bf16[16,8192]{1,0:T(8,128)(2,1)S(1)}, u32[]{:S(2)}, u32[]{:S(2)}) collective-permute-start(bf16[16,8192]{1,0:T(8,128)(2,1)S(1)} %get-tuple-element.119), channel_id=1, source_target_pairs={{0,2},{1,3},{2,4},{3,5},{4,6},{5,7},{6,0},{7,1},{8,10},{9,11},{10,... | collective-permute-start | bytes 786440 | tf_op jit(solution)/shard_map/ppermute | solution.py:196
  201.1 10.7 %collective-permute-start.33 = (bf16[16,8192]{1,0:T(8,128)(2,1)S(1)}, bf16[16,8192]{1,0:T(8,128)(2,1)S(1)}, u32[]{:S(2)}, u32[]{:S(2)}) collective-permute-start(bf16[16,8192]{1,0:T(8,128)(2,1)S(1)} %slice.119), channel_id=1, source_target_pairs={{0,6},{1,7},{2,0},{3,1},{4,2},{5,3},{6,4},{7,5},{8,14},{9,15},{10,... | collective-permute-start | bytes 786440 | tf_op jit(solution)/shard_map/ppermute | solution.py:199
